TPU v7x, 32 devices: a whole 2x2x4 slice. The times are simulated.
32 devices in a mesh: rows: 8 (over z, x), cols: 4 (over y, core).
Axes of the slice: x: 2, y: 2, z: 4, core: 2. Of those that a mesh axis runs over, the one named last changes fastest.
Arguments:
- tiles: bfloat16 [4096, 4096], P(('rows', 'cols')), may hold values from -0.125 to 0.125
- integral_cd_tile: int32 [4096], P(('rows', 'cols')), may hold values from 0 to 31
- part_dest: int32 [1024, 1], P(('rows', 'cols')), may hold values from 0 to 7; in each aligned block of 32 rows (0 to 31, 32 to 63, ...) at most 8 rows name the same one
- partial_row_place: int32 [1024], P(('rows', 'cols')), may hold values from 0 to 15
- amplitudes: bfloat16 [4, 32, 4096], P('cols', 'rows'), may hold values from -6 to 6
- residual_in: float32 [8, 16, 4096], P('rows', 'cols'), may hold values from -6 to 6
Outputs:
- residual: float32 [8, 16, 4096], P('rows', 'cols')
Inputs may be any that keep to these rules, and one draw needn't show every extreme that they name: `part_dest`: among the 32 partial tiles of one device no index of rows is named more than 8 times, and at least one is named exactly 8 times.
All inputs are finite; a program needn't handle non-finite values.
Results may differ from a plain program's by a relative error of at most 0.0022.
Values may be sent and summed in bfloat16 or wider, within the bound.
No kernel may reach another device: no remote copies, remote signals or barrier semaphores. Data moves between devices by JAX's collectives and lax.ppermute only.
A program may use at most 64 MiB of HBM per device.

v0:
```python
import jax
import jax.numpy as jnp
from jax import lax
from jax.sharding import PartitionSpec as P

TILE_SPAN = 64
NIJ = 64
TILES_PER_PART = 4
PAB = 32
OWNR = 16


def per_device(tiles, integral_cd_tile, part_dest, partial_row_place, amplitudes, residual_in):
    gathered = lax.all_gather(amplitudes, "rows", axis=1, tiled=True)[0]
    picked = jnp.take(gathered, integral_cd_tile, axis=0).reshape(
        PAB, TILES_PER_PART, NIJ, TILE_SPAN
    )
    block_list = tiles.reshape(PAB, TILES_PER_PART, TILE_SPAN, TILE_SPAN)
    per_tile = jnp.einsum("ptic,ptac->ptia", picked, block_list, preferred_element_type=jnp.float32)
    partial_value = jnp.sum(per_tile, axis=1)
    partial_value = partial_value.reshape(PAB, NIJ * TILE_SPAN).astype(jnp.bfloat16)
    row_count = lax.axis_size("rows")
    capacity = max(2, 2 * PAB // row_count)
    destination = part_dest[:, 0]
    onehot = (destination[:, None] == jnp.arange(row_count, dtype=jnp.int32)[None, :]).astype(
        jnp.int32
    )
    earlier = jnp.sum((jnp.cumsum(onehot, axis=0) - onehot) * onehot, axis=1)
    position = destination * capacity + earlier
    outgoing = (
        jnp.zeros((row_count * capacity, NIJ * TILE_SPAN), jnp.bfloat16)
        .at[position]
        .set(partial_value)
    )
    slot_ids = (
        jnp.full((row_count * capacity,), float(OWNR), jnp.float32)
        .at[position]
        .set(partial_row_place.astype(jnp.float32))
        .astype(jnp.bfloat16)
    )
    incoming, incoming_ids = (
        lax.all_to_all(
            outgoing.reshape(row_count, capacity, NIJ * TILE_SPAN),
            "rows",
            split_axis=0,
            concat_axis=0,
            tiled=True,
        ),
        lax.all_to_all(
            slot_ids.reshape(row_count, capacity), "rows", split_axis=0, concat_axis=0, tiled=True
        ),
    )
    incoming = incoming.reshape(row_count * capacity, NIJ * TILE_SPAN)
    incoming_ids = incoming_ids.reshape(row_count * capacity).astype(jnp.float32)
    select = (incoming_ids[None, :] == jnp.arange(OWNR, dtype=jnp.float32)[:, None]).astype(
        jnp.bfloat16
    )
    owned = jnp.dot(select, incoming, preferred_element_type=jnp.float32)
    shared = lax.psum_scatter(owned, "cols", scatter_dimension=0, tiled=True)
    return residual_in + shared[None, :, :]


def solution(mesh):
    return jax.shard_map(
        per_device,
        mesh=mesh,
        in_specs=(
            P(("rows", "cols"), None),
            P(("rows", "cols")),
            P(("rows", "cols"), None),
            P(("rows", "cols")),
            P("cols", "rows", None),
            P("rows", "cols", None),
        ),
        out_specs=P("rows", "cols", None),
        check_vma=False,
    )
```

profile of v0, /device:TPU:0, one launch (start us, length us, event | category | flops | bytes accessed | tf_op | source)
XLA Modules:
  0.0 121.2 jit_solution(10204505423707535486)
XLA Ops:
  6.5 0.7 fusion.15
  7.3 0.1 reduce_window_sum.11
  7.3 0.8 select_reduce_fusion
  8.2 0.7 fusion.17
  8.8 0.7 convert_element_type.27
  9.5 0.7 scatter_custom_fusion
  10.2 0.7 all_to_all.12
  10.9 7.3 %all-to-all-start = ((bf16[8,1,8]{2,1,0:T(2,128)(2,1)}), bf16[8,1,8]{2,1,0:T(2,128)(2,1)S(1)}, u32[]{:S(2)}, u32[]{:S(2)}) async-start(bf16[8,1,8]{2,1,0:T(2,128)(2,1)} %all_to_all.12), calls=%async_computation | async-start | bytes 8192 | tf_op jit(solution)/shard_map/all_to_all | solution.py:49
  18.1 0.7 compare_select_fusion
  18.8 0.7 compare_and_fusion
  19.4 0.8 copy.10
  20.2 31.9 %all_gather.3 = bf16[1,32,4096]{2,0,1:T(2,128)(2,1)S(1)} all-gather(bf16[1,4,4096]{2,0,1:T(2,128)(2,1)S(1)} %copy.10), channel_id=1, replica_groups=mesh['rows'=8,'cols'=4] {'rows'}, dimensions={1}, use_global_device_ids=true | all-gather | bytes 294912 | tf_op jit(solution)/shard_map/all_gather | solution.py:14
  52.2 0.3 copy.14
  52.5 1.2 gather_fusion
  53.7 2.3 %gather.7 = bf16[32,4,64,64]{3,2,1,0:T(8,128)(2,1)S(1)} reshape(bf16[128,4096]{1,0:T(8,128)(2,1)S(1)} %gather_fusion) | data formatting | bytes 2097152 | tf_op jit(solution)/shard_map/jit(_take)/gather | solution.py:15
  56.0 4.3 %reshape.37 = bf16[32,4,64,64]{3,2,1,0:T(8,128)(2,1)} reshape(bf16[128,4096]{1,0:T(8,128)(2,1)} %param.6) | data formatting | bytes 2097152 | tf_op jit(solution)/shard_map/reshape | solution.py:18
  60.2 0.1 broadcast_in_dim.30
  60.3 2.4 %fusion.6 = bf16[32,64,64]{2,1,0:T(8,128)(2,1)S(1)} fusion(bf16[32,4,64,64]{3,2,1,0:T(8,128)(2,1)} %reshape.37, bf16[32,4,64,64]{3,2,1,0:T(8,128)(2,1)S(1)} %gather.7, pred[32,4]{1,0:T(8,128)(4,1)S(1)} %broadcast_in_dim.30), kind=kOutput, calls=%fused_computation.7 | convolution fusion | flops 67764224 | bytes 2359424 | tf_op jit(solution)/shard_map/ptic,ptac->ptia/dot_general | solution.py:19
  62.7 0.0 copy-start.1
  62.7 0.0 copy-start
  62.7 0.5 reshape.61
  63.2 1.8 %scatter_custom_fusion.1 = bf16[64,4096]{1,0:T(8,128)(2,1)} fusion(s32[32]{0:T(128)S(1)} %fusion.17, bf16[32,4096]{1,0:T(8,128)(2,1)S(1)} %reshape.61, bf16[]{:T(256)} %constant.19.clone.1), kind=kCustom, calls=%fused_computation.12 | custom fusion | bytes 524290 | tf_op jit(solution)/shard_map/scatter | solution.py:33
  65.0 0.0 all-to-all-done
  65.0 5.4 %all-to-all-start.1 = ((bf16[8,8,4096]{2,1,0:T(8,128)(2,1)}), bf16[8,8,4096]{2,1,0:T(8,128)(2,1)S(1)}, u32[]{:S(2)}, u32[]{:S(2)}) async-start(bf16[8,8,4096]{2,1,0:T(8,128)(2,1)} %bitcast.5), calls=%async_computation.1 | async-start | bytes 1048576 | tf_op jit(solution)/shard_map/all_to_all | solution.py:42
  70.3 0.0 all-reduce.3.cloned.1.call-start
  70.4 0.1 reshape.40
  70.5 10.1 %all-to-all-done.1 = bf16[8,8,4096]{2,1,0:T(8,128)(2,1)S(1)} async-done(((bf16[8,8,4096]{2,1,0:T(8,128)(2,1)}), bf16[8,8,4096]{2,1,0:T(8,128)(2,1)S(1)}, u32[]{:S(2)}, u32[]{:S(2)}) %all-to-all-start.1) | async-done | bytes 524320 | tf_op jit(solution)/shard_map/all_to_all | solution.py:42
  80.6 0.9 fusion.10
  81.5 0.0 all-reduce.3.cloned.1.call-update
  81.5 0.0 copy-done.1
  81.6 0.6 dynamic-slice
  82.8 30.0 %all-reduce.3.cloned.1.call-done = f32[16,4096]{1,0:T(8,128)} async-done(((f32[16,4096]{1,0:T(8,128)}), f32[16,4096]{1,0:T(8,128)}) %all-reduce.3.cloned.1.call-update) | async-done | bytes 262160
  112.8 0.0 copy-done
  112.8 1.6 %fusion.14 = f32[1,4,4096]{2,1,0:T(4,128)} fusion(f32[1,4,4096]{2,1,0:T(4,128)S(1)} %copy-done, f32[16,4096]{1,0:T(8,128)} %all-reduce.3.cloned.1.call-done, u32[]{:T(128)S(6)} %multiply.1), kind=kLoop, calls=%fused_computation.15 | loop fusion | flops 16384 | bytes 196612 | tf_op jit(solution)/shard_map/add | solution.py:60
  (3 shorter events, 0.0 us)
Async XLA Ops:
  10.9 54.1 %all-to-all-start = ((bf16[8,1,8]{2,1,0:T(2,128)(2,1)}), bf16[8,1,8]{2,1,0:T(2,128)(2,1)S(1)}, u32[]{:S(2)}, u32[]{:S(2)}) async-start(bf16[8,1,8]{2,1,0:T(2,128)(2,1)} %all_to_all.12), calls=%async_computation | async-start | bytes 8192 | tf_op jit(solution)/shard_map/all_to_all | solution.py:49
  62.7 18.8 %copy-start.1 = (u32[32]{0:T(128)S(1)}, u32[32]{0:T(128)}, u32[]{:S(2)}) copy-start(u32[32]{0:T(128)} %constant.35) | copy-start | bytes 388
  62.7 50.1 %copy-start = (f32[1,4,4096]{2,1,0:T(4,128)S(1)}, f32[1,4,4096]{2,1,0:T(4,128)}, u32[]{:S(2)}) copy-start(f32[1,4,4096]{2,1,0:T(4,128)} %param.11) | copy-start | bytes 196612
  65.0 15.7 %all-to-all-start.1 = ((bf16[8,8,4096]{2,1,0:T(8,128)(2,1)}), bf16[8,8,4096]{2,1,0:T(8,128)(2,1)S(1)}, u32[]{:S(2)}, u32[]{:S(2)}) async-start(bf16[8,8,4096]{2,1,0:T(8,128)(2,1)} %bitcast.5), calls=%async_computation.1 | async-start | bytes 1048576 | tf_op jit(solution)/shard_map/all_to_all | solution.py:42
  70.3 42.5 %all-reduce.3.cloned.1.call-start = ((), (), s32[]{:S(2)}) async-start(), calls=%async_computation.2 | async-start | bytes 524288
Sparse Core Ops, SparseCore 0:
  81.7 31.0 all-reduce.2
where the time goes:
time: 122 us; the launch traced here: 121 us
  waiting for transfers between devices  40.2 us (33%)
  blocking collectives  31.9 us (26%)
  between operations  14.1 us (12%)
  local copies, waits for them, and re-layouts  13.2 us (11%)
  starting transfers between devices  12.7 us (10%)
  other arithmetic  5.84 us (5%)
  matrix products  3.25 us (3%)
    all_gather x1, blocking collectives, per_device(): gathered = lax.all_gather(amplitudes, 'rows', axis=1, tiled=True)[0]  31.9 us
    unnamed x2, waiting for transfers between devices  30 us
    all_to_all x1, waiting for transfers between devices, per_device(): lax.all_to_all(outgoing.reshape(row_count, capacity, NIJ * TILE_SPAN), 'r...  10.1 us
    all_to_all x1, starting transfers between devices, per_device(): lax.all_to_all(slot_ids.reshape(row_count, capacity), 'rows', split_axis=...  7.25 us
    all_to_all x1, starting transfers between devices, per_device(): lax.all_to_all(outgoing.reshape(row_count, capacity, NIJ * TILE_SPAN), 'r...  5.37 us
    reshape x1, local copies, waits for them, and re-layouts, per_device(): block_list = tiles.reshape(PAB, TILES_PER_PART, TILE_SPAN, TILE_SPAN)  4.26 us
    gather x2, local copies, waits for them, and re-layouts, per_device(): jnp.take(gathered, integral_cd_tile, axis=0)  3.48 us
  transfers between devices with their start and end apart: 3, of which 2 were waited for; matrix products, arithmetic and copies ran while one was open for 13% of the time, Pallas kernels for 0%

commit v1 on v0

v1 whole, which is shorter than its diff:
```python
import functools

import jax
import jax.numpy as jnp
from jax import lax
from jax.experimental import pallas as pl
from jax.experimental.pallas import tpu as pltpu
from jax.sharding import Mesh
from jax.sharding import PartitionSpec as P

SPAN = 64
LANES = 128
PER_PART = 4
OWNR = 16
ROWS_OF_TILE = SPAN * SPAN // LANES
VMEM = pl.BlockSpec(memory_space=pltpu.VMEM)
SMEM = pl.BlockSpec(memory_space=pltpu.SMEM)


def halves_swapped(x):
    return jnp.concatenate([x[:, SPAN:], x[:, :SPAN]], axis=1)


def partial_kernel(cd_ref, amp_ref, tile_ref, out_ref):
    low = lax.broadcasted_iota(jnp.int32, (ROWS_OF_TILE, LANES), 1) < SPAN

    def pair(first, second):
        even = jnp.where(low, first, halves_swapped(second))
        odd = jnp.where(low, halves_swapped(first), second)
        return even, odd

    for q in range(out_ref.shape[0] // ROWS_OF_TILE):
        amps, tiles = [], []
        for t in range(0, PER_PART, 2):
            k = q * PER_PART + t
            amps.append(
                pair(*[
                    amp_ref[
                        pl.ds(pl.multiple_of(cd_ref[k + i] * ROWS_OF_TILE, ROWS_OF_TILE), ROWS_OF_TILE), :
                    ]
                    for i in (0, 1)
                ])
            )
            tiles.append(
                pair(*[tile_ref[pl.ds((k + i) * ROWS_OF_TILE, ROWS_OF_TILE), :] for i in (0, 1)])
            )
        left = jnp.concatenate([jnp.concatenate([a[h] for a in amps], axis=1) for h in (0, 1)], axis=0)
        right = jnp.concatenate([jnp.concatenate([v[h] for v in tiles], axis=1) for h in (0, 1)], axis=0)
        value = lax.dot_general(
            left, right, (((1,), (1,)), ((), ())), preferred_element_type=jnp.float32
        )
        packed = jnp.concatenate([value[:ROWS_OF_TILE], value[ROWS_OF_TILE:]], axis=1)
        out_ref[pl.ds(q * ROWS_OF_TILE, ROWS_OF_TILE), :] = packed.astype(jnp.bfloat16)


def dense_kernel(per_col, pair, own_code_ref, other_code_ref, own_ref, other_ref, out_ref, sum_ref):
    me = lax.axis_index("core")
    groups = OWNR // per_col // pair
    slots = out_ref.shape[0] // ROWS_OF_TILE
    sum_ref[...] = jnp.zeros_like(sum_ref)
    for code_ref, ref in ((own_code_ref, own_ref), (other_code_ref, other_ref)):
        for q in range(ref.shape[0] // ROWS_OF_TILE):
            code = code_ref[q]
            dest, place = code // OWNR, code % OWNR
            col, inner = place // per_col, place % per_col
            slot = (dest * groups + col // pair) * per_col + inner
            slot = jnp.where(col % pair == me, slot, slots)
            at = pl.ds(pl.multiple_of(slot * ROWS_OF_TILE, ROWS_OF_TILE), ROWS_OF_TILE)
            sum_ref[at, :] += ref[pl.ds(q * ROWS_OF_TILE, ROWS_OF_TILE), :].astype(jnp.float32)
    out_ref[...] = sum_ref[pl.ds(0, out_ref.shape[0]), :].astype(jnp.bfloat16)


def final_kernel(in_ref, residual_ref, out_ref, sum_ref):
    total = in_ref[0].astype(jnp.float32)
    for source in range(1, in_ref.shape[0]):
        total += in_ref[source].astype(jnp.float32)
    half = SPAN // 2
    lane = lax.broadcasted_iota(jnp.int32, (LANES, LANES), 0)
    place = lax.broadcasted_iota(jnp.int32, (LANES, LANES), 1)
    target = lane // SPAN * SPAN + lane % half * 2 + lane % SPAN // half
    order = (target == place).astype(jnp.float32)
    sum_ref[...] = jnp.dot(
        total, order, precision=lax.Precision.HIGHEST, preferred_element_type=jnp.float32
    )
    tiles = sum_ref.shape[0] // ROWS_OF_TILE
    for i in range(ROWS_OF_TILE):
        at = pl.ds(i * LANES, LANES)
        out_ref[0, :, at] = residual_ref[0, :, at] + sum_ref[pl.ds(i, tiles, stride=ROWS_OF_TILE), :]


def per_device(rows, groups, pair, tiles, cd_tile, part_dest, place, amplitudes, residual_in):
    held, parts = tiles.shape[0], place.shape[0]
    own_cd = amplitudes.shape[1]
    per_col = residual_in.shape[1]
    bf16, f32 = jnp.bfloat16, jnp.float32
    params = pltpu.CompilerParams(vmem_limit_bytes=48 * 2**20)

    code = part_dest[:, 0] * OWNR + place
    swap = [(i, (i + 1) % pair) for i in range(pair)]
    other_code = lax.ppermute(code, "core", swap)

    shard = amplitudes.reshape(1, own_cd * ROWS_OF_TILE, LANES)
    repeated = jnp.broadcast_to(shard, (rows,) + shard.shape[1:])
    gathered = lax.all_to_all(repeated, "rows", split_axis=0, concat_axis=0, tiled=True)
    gathered = gathered.reshape(rows * own_cd * ROWS_OF_TILE, LANES)

    partial = pl.pallas_call(
        partial_kernel,
        out_shape=jax.ShapeDtypeStruct((parts * ROWS_OF_TILE, LANES), bf16),
        in_specs=[SMEM, VMEM, VMEM],
        out_specs=VMEM,
        compiler_params=params,
    )(cd_tile, gathered, tiles.reshape(held * ROWS_OF_TILE, LANES))

    other = lax.ppermute(partial, "core", swap)
    owners = rows * groups
    dense = pl.pallas_call(
        functools.partial(dense_kernel, per_col, pair),
        out_shape=jax.ShapeDtypeStruct((owners * per_col * ROWS_OF_TILE, LANES), bf16),
        in_specs=[SMEM, SMEM, VMEM, VMEM],
        out_specs=VMEM,
        scratch_shapes=[pltpu.VMEM(((owners * per_col + 1) * ROWS_OF_TILE, LANES), f32)],
        compiler_params=params,
    )(code, other_code, partial, other)

    incoming = lax.all_to_all(
        dense.reshape(owners, per_col * ROWS_OF_TILE, LANES),
        ("rows", "groups"),
        split_axis=0,
        concat_axis=0,
        tiled=True,
    )
    return pl.pallas_call(
        final_kernel,
        out_shape=jax.ShapeDtypeStruct(residual_in.shape, f32),
        in_specs=[VMEM, VMEM],
        out_specs=VMEM,
        scratch_shapes=[pltpu.VMEM((per_col * ROWS_OF_TILE, LANES), f32)],
        compiler_params=params,
    )(incoming, residual_in)


def solution(mesh):
    rows, cols = mesh.shape["rows"], mesh.shape["cols"]
    pair = 2 if cols % 2 == 0 else 1
    split = Mesh(mesh.devices.reshape(rows, cols // pair, pair), ("rows", "groups", "core"))
    every = ("rows", "groups", "core")
    return jax.shard_map(
        functools.partial(per_device, rows, cols // pair, pair),
        mesh=split,
        in_specs=(
            P(every, None),
            P(every),
            P(every, None),
            P(every),
            P(("groups", "core"), "rows", None),
            P("rows", ("groups", "core"), None),
        ),
        out_specs=P("rows", ("groups", "core"), None),
        check_vma=False,
    )
```

time: 122 us -> 44.1 us (0.36)
  waiting for transfers between devices: 40.2 us -> 8.3 us
  between operations: 14.1 us -> 0.07 us
  blocking collectives: 31.9 us -> 20 us
  local copies, waits for them, and re-layouts: 13.2 us -> 3.11 us
  other arithmetic: 5.84 us -> 0.01 us
  starting transfers between devices: 12.7 us -> 7.86 us
  Pallas kernels: 0 us -> 4.36 us
  matrix products: 3.25 us -> 0 us
    all_gather x1 -> x0, blocking collectives: 31.9 us -> none  [per_device(): gathered = lax.all_gather(amplitudes, 'rows', axis=1, tiled=True)[0]]
    unnamed x2 -> x0, waiting for transfers between devices: 30 us -> none
    all_to_all x0 -> x1, blocking collectives: none -> 20 us  [per_device(): lax.all_to_all(dense.reshape(owners, per_col * ROWS_OF_TILE, LANES), ('ro...]
    all_to_all x2 -> x1, starting transfers between devices: 12.6 us -> 7.25 us  [per_device(): lax.all_to_all(repeated, 'rows', split_axis=0, concat_axis=0, tiled=True)]
    pallas_call x0 -> x3, Pallas kernels: none -> 4.36 us  [the longest x1 1.73 us: per_device(): pl.pallas_call(functools.partial(dense_kernel, per_col, pair), out_shape=...]
    gather x2 -> x0, local copies, waits for them, and re-layouts: 3.48 us -> none  [per_device(): jnp.take(gathered, integral_cd_tile, axis=0)]
    dot_general x2 -> x0, matrix products: 3.25 us -> none  [the longest x1 2.35 us: per_device(): jnp.einsum('ptic,ptac->ptia', picked, block_list, preferred_element_type=...]
    all_to_all x2 -> x1, waiting for transfers between devices: 10.1 us -> 7.35 us  [per_device(): lax.all_to_all(repeated, 'rows', split_axis=0, concat_axis=0, tiled=True)]
  transfers between devices with their start and end apart: 3 -> 3, of which waited for: 2 -> 2; matrix products, arithmetic and copies ran while one was open for 13% -> 4% of each run, Pallas kernels for 0% -> 0%
where the time goes in v1:
time: 44.1 us; the launch traced here: 43.7 us
  blocking collectives  20 us (45%)
  waiting for transfers between devices  8.3 us (19%)
  starting transfers between devices  7.86 us (18%)
  Pallas kernels  4.36 us (10%)
  local copies, waits for them, and re-layouts  3.11 us (7%)
    all_to_all x1, blocking collectives, per_device(): lax.all_to_all(dense.reshape(owners, per_col * ROWS_OF_TILE, LANES), ('ro...  20 us
    all_to_all x1, waiting for transfers between devices, per_device(): lax.all_to_all(repeated, 'rows', split_axis=0, concat_axis=0, tiled=True)  7.35 us
    all_to_all x1, starting transfers between devices, per_device(): lax.all_to_all(repeated, 'rows', split_axis=0, concat_axis=0, tiled=True)  7.25 us
    pallas_call x1, Pallas kernels, per_device(): pl.pallas_call(functools.partial(dense_kernel, per_col, pair), out_shape=...  1.73 us
    pallas_call x1, Pallas kernels, per_device(): pl.pallas_call(partial_kernel, out_shape=jax.ShapeDtypeStruct((parts * RO...  1.66 us
    reshape x1, local copies, waits for them, and re-layouts, per_device(): tiles.reshape(held * ROWS_OF_TILE, LANES)  1.55 us
    broadcast_in_dim x2, local copies, waits for them, and re-layouts, per_device(): repeated = jnp.broadcast_to(shard, (rows,) + shard.shape[1:])  1.53 us
    pallas_call x1, Pallas kernels, per_device(): pl.pallas_call(final_kernel, out_shape=jax.ShapeDtypeStruct(residual_in.s...  0.96 us
  transfers between devices with their start and end apart: 3, of which 2 were waited for; matrix products, arithmetic and copies ran while one was open for 4% of the time, Pallas kernels for 0%

profile of v1, /device:TPU:0, one launch (start us, length us, event | category | flops | bytes accessed | tf_op | source)
XLA Modules:
  0.0 43.7 jit_solution(1779158412141795257)
XLA Ops:
  0.0 0.8 %broadcast_in_dim.7 = bf16[128,128]{1,0:T(8,128)(2,1)S(1)} reshape(bf16[1,4,4096]{2,1,0:T(4,128)(2,1)} %param.10) | data formatting | bytes 65536 | tf_op jit(solution)/shard_map/broadcast_in_dim | solution.py:103
  0.8 0.7 %broadcast_in_dim.8 = bf16[8,128,128]{2,1,0:T(8,128)(2,1)} broadcast(bf16[128,128]{1,0:T(8,128)(2,1)S(1)} %broadcast_in_dim.7), dimensions={1,2} | broadcast | bytes 294912 | tf_op jit(solution)/shard_map/broadcast_in_dim | solution.py:103
  1.5 7.3 %all-to-all-start = ((bf16[8,128,128]{2,1,0:T(8,128)(2,1)}), bf16[8,128,128]{2,1,0:T(8,128)(2,1)S(1)}, u32[]{:S(2)}, u32[]{:S(2)}) async-start(bf16[8,128,128]{2,1,0:T(8,128)(2,1)} %broadcast_in_dim.8), calls=%async_computation | async-start | bytes 524288 | tf_op jit(solution)/shard_map/all_to_all | solution.py:104
  8.8 1.6 %reshape.14.tile_ref = bf16[4096,128]{1,0:T(8,128)(2,1)S(1)} reshape(bf16[128,4096]{1,0:T(8,128)(2,1)} %param.6) | data formatting | bytes 2097152 | tf_op jit(solution)/shard_map/reshape | solution.py:113
  10.3 0.0 copy-start.1
  10.4 7.3 %all-to-all-done = bf16[8,128,128]{2,1,0:T(8,128)(2,1)S(1)} async-done(((bf16[8,128,128]{2,1,0:T(8,128)(2,1)}), bf16[8,128,128]{2,1,0:T(8,128)(2,1)S(1)}, u32[]{:S(2)}, u32[]{:S(2)}) %all-to-all-start) | async-done | bytes 262176 | tf_op jit(solution)/shard_map/all_to_all | solution.py:104
  17.7 0.0 copy-done.1
  17.7 0.0 copy-start.2
  17.7 0.0 copy-start.3
  17.7 1.7 %shard_map.64.own_ref = bf16[1024,128]{1,0:T(8,128)(2,1)S(1)} custom-call(s32[128]{0:T(128)S(1)} %copy-done.1, bf16[1024,128]{1,0:T(8,128)(2,1)S(1)} %bitcast.5, bf16[4096,128]{1,0:T(8,128)(2,1)S(1)} %reshape.14.tile_ref), custom_call_target="tpu_custom_call" | custom-call | tf_op jit(solution)/shard_map/pallas_call | solution.py:107
  19.4 0.1 collective-permute-start.1
  19.5 0.0 copy-done.2
  19.5 0.0 copy-done.3
  19.5 0.5 %collective-permute-start = (s32[32]{0:T(128)S(1)}, s32[32]{0:T(128)S(1)}, u32[]{:S(2)}, u32[]{:S(2)}) collective-permute-start(s32[32]{0:T(128)S(1)} %bitcast_add_fusion.own_code_ref), channel_id=1, source_target_pairs={{0,1},{1,0},{2,3},{3,2},{4,5},{5,4},{6,7},{7,6},{8,9},{9,8},{10,11... | collective-permute-start | bytes 392 | tf_op jit(solution)/shard_map/ppermute | solution.py:100
  20.0 0.9 %collective-permute-done.other_code_ref = s32[32]{0:T(128)S(1)} collective-permute-done((s32[32]{0:T(128)S(1)}, s32[32]{0:T(128)S(1)}, u32[]{:S(2)}, u32[]{:S(2)}) %collective-permute-start) | collective-permute-done | bytes 160 | tf_op jit(solution)/shard_map/ppermute | solution.py:100
  21.0 0.0 collective-permute-done.1.other_ref
  21.0 1.7 %shard_map.65 = bf16[2048,128]{1,0:T(8,128)(2,1)S(1)} custom-call(s32[32]{0:T(128)S(1)} %bitcast_add_fusion.own_code_ref, s32[32]{0:T(128)S(1)} %collective-permute-done.other_code_ref, bf16[1024,128]{1,0:T(8,128)(2,1)S(1)} %shard_map.64.own_ref, bf16[1024,128]{1,0:T(8,128)(2,1)S(1)} %collective-permute-done.1.other_ref), custom_call_target="tpu_custom_call" | custom-call | tf_op jit(solution)/shard_map/pallas_call | solution.py:117
  22.7 0.0 copy-start
  22.7 20.0 %all_to_all.10.in_ref = bf16[16,128,128]{2,1,0:T(8,128)(2,1)S(1)} all-to-all(bf16[16,128,128]{2,1,0:T(8,128)(2,1)S(1)} %bitcast.4), channel_id=1, replica_groups=mesh['rows'=8,'groups'=2,'core'=2] {'rows','groups'}, dimensions={0} | all-to-all | bytes 1048576 | tf_op jit(solution)/shard_map/all_to_all | solution.py:126
  42.8 0.0 copy-done
  42.8 1.0 %shard_map.66 = f32[1,4,4096]{2,1,0:T(4,128)} custom-call(bf16[16,128,128]{2,1,0:T(8,128)(2,1)S(1)} %all_to_all.10.in_ref, f32[1,4,4096]{2,1,0:T(4,128)S(1)} %copy-done), custom_call_target="tpu_custom_call" | custom-call | tf_op jit(solution)/shard_map/pallas_call | solution.py:133
  (1 shorter events, 0.0 us)
Async XLA Ops:
  1.5 16.2 %all-to-all-start = ((bf16[8,128,128]{2,1,0:T(8,128)(2,1)}), bf16[8,128,128]{2,1,0:T(8,128)(2,1)S(1)}, u32[]{:S(2)}, u32[]{:S(2)}) async-start(bf16[8,128,128]{2,1,0:T(8,128)(2,1)} %broadcast_in_dim.8), calls=%async_computation | async-start | bytes 524288 | tf_op jit(solution)/shard_map/all_to_all | solution.py:104
  10.3 7.4 %copy-start.1 = (s32[128]{0:T(128)S(1)}, s32[128]{0:T(128)}, u32[]{:S(2)}) copy-start(s32[128]{0:T(128)} %cd_ref.1) | copy-start | bytes 1540
  17.7 1.8 %copy-start.2 = (s32[32]{0:T(128)S(1)}, s32[32]{0:T(128)}, u32[]{:S(2)}) copy-start(s32[32]{0:T(128)} %param.9) | copy-start | bytes 388
  17.7 1.8 %copy-start.3 = (s32[32,1]{0,1:T(1,128)S(1)}, s32[32,1]{0,1:T(1,128)}, u32[]{:S(2)}) copy-start(s32[32,1]{0,1:T(1,128)} %param.8) | copy-start | bytes 388
  19.4 1.6 %collective-permute-start.1 = (bf16[1024,128]{1,0:T(8,128)(2,1)S(1)}, bf16[1024,128]{1,0:T(8,128)(2,1)S(1)}, u32[]{:S(2)}, u32[]{:S(2)}) collective-permute-start(bf16[1024,128]{1,0:T(8,128)(2,1)S(1)} %shard_map.64.own_ref), channel_id=1, source_target_pairs={{0,1},{1,0},{2,3},{3,2},{4,5},{5,4},{6,7},{7,6},{8,9},{9,8},{10,11... | collective-permute-start | bytes 786440 | tf_op jit(solution)/shard_map/ppermute | solution.py:115
  19.5 1.5 %collective-permute-start = (s32[32]{0:T(128)S(1)}, s32[32]{0:T(128)S(1)}, u32[]{:S(2)}, u32[]{:S(2)}) collective-permute-start(s32[32]{0:T(128)S(1)} %bitcast_add_fusion.own_code_ref), channel_id=1, source_target_pairs={{0,1},{1,0},{2,3},{3,2},{4,5},{5,4},{6,7},{7,6},{8,9},{9,8},{10,11... | collective-permute-start | bytes 392 | tf_op jit(solution)/shard_map/ppermute | solution.py:100
  22.7 20.0 %copy-start = (f32[1,4,4096]{2,1,0:T(4,128)S(1)}, f32[1,4,4096]{2,1,0:T(4,128)}, u32[]{:S(2)}) copy-start(f32[1,4,4096]{2,1,0:T(4,128)} %residual_ref.1) | copy-start | bytes 196612

commit v2 on v1

v2 whole, which is shorter than its diff:
```python
import functools

import jax
import jax.numpy as jnp
from jax import lax
from jax.experimental import pallas as pl
from jax.experimental.pallas import tpu as pltpu
from jax.sharding import Mesh
from jax.sharding import PartitionSpec as P

SPAN = 64
LANES = 128
PER_PART = 4
OWNR = 16
ROWS_OF_TILE = SPAN * SPAN // LANES
VMEM = pl.BlockSpec(memory_space=pltpu.VMEM)
SMEM = pl.BlockSpec(memory_space=pltpu.SMEM)


def call(kernel, out_shape, in_specs, *args, scratch=(), aliases=None):
    single = isinstance(out_shape, jax.ShapeDtypeStruct)
    return pl.pallas_call(
        kernel,
        out_shape=out_shape,
        in_specs=in_specs,
        out_specs=VMEM if single else [VMEM] * len(out_shape),
        scratch_shapes=scratch,
        input_output_aliases=aliases or {},
        compiler_params=pltpu.CompilerParams(vmem_limit_bytes=48 * 2**20),
    )(*args)


def tile_rows(first, count=ROWS_OF_TILE):
    return pl.ds(pl.multiple_of(first, ROWS_OF_TILE), count)


def repeat_kernel(in_ref, out_ref, row_ref):
    held = in_ref.shape[1]
    for j in range(ROWS_OF_TILE):
        row_ref[pl.ds(j, held, stride=ROWS_OF_TILE), :] = in_ref[
            0, :, pl.ds(j * LANES, LANES)
        ].astype(jnp.float32)
    rows = row_ref[...].astype(jnp.bfloat16)
    for receiver in range(out_ref.shape[0]):
        out_ref[receiver] = rows


def halves_swapped(x):
    return jnp.concatenate([x[:, SPAN:], x[:, :SPAN]], axis=1)


def pair(low, first, second):
    even = jnp.where(low, first, halves_swapped(second))
    odd = jnp.where(low, halves_swapped(first), second)
    return even, odd


def low_lanes():
    return lax.broadcasted_iota(jnp.int32, (ROWS_OF_TILE, LANES), 1) < SPAN


def pair_kernel(tile_ref, out_ref):
    low = low_lanes()
    for q in range(out_ref.shape[0] // SPAN):
        for t in range(0, PER_PART, 2):
            k = q * PER_PART + t
            halves = pair(
                low, *[tile_ref[pl.ds((k + i) * ROWS_OF_TILE, ROWS_OF_TILE), :] for i in (0, 1)]
            )
            for h in (0, 1):
                at = pl.ds(q * SPAN + h * ROWS_OF_TILE, ROWS_OF_TILE)
                out_ref[at, pl.ds(t * SPAN, LANES)] = halves[h]


def partial_kernel(cd_ref, amp_ref, tile_ref, out_ref):
    low = low_lanes()
    for q in range(out_ref.shape[0] // ROWS_OF_TILE):
        amps = []
        for t in range(0, PER_PART, 2):
            k = q * PER_PART + t
            amps.append(
                pair(low, *[amp_ref[tile_rows(cd_ref[k + i] * ROWS_OF_TILE), :] for i in (0, 1)])
            )
        left = jnp.concatenate([jnp.concatenate([a[h] for a in amps], axis=1) for h in (0, 1)], axis=0)
        value = lax.dot_general(
            left,
            tile_ref[pl.ds(q * SPAN, SPAN), :],
            (((1,), (1,)), ((), ())),
            preferred_element_type=jnp.float32,
        )
        packed = jnp.concatenate([value[:ROWS_OF_TILE], value[ROWS_OF_TILE:]], axis=1)
        out_ref[pl.ds(q * ROWS_OF_TILE, ROWS_OF_TILE), :] = packed.astype(jnp.bfloat16)


def add_tiles(slot_ref, ref, sum_ref):
    for q in range(ref.shape[0] // ROWS_OF_TILE):
        at = tile_rows(slot_ref[q] * ROWS_OF_TILE)
        sum_ref[at, :] += ref[pl.ds(q * ROWS_OF_TILE, ROWS_OF_TILE), :].astype(jnp.float32)


def own_kernel(slot_ref, ref, sum_ref):
    sum_ref[...] = jnp.zeros_like(sum_ref)
    add_tiles(slot_ref, ref, sum_ref)


def other_kernel(slot_ref, ref, in_ref, out_ref, sum_ref):
    add_tiles(slot_ref, ref, sum_ref)
    out_ref[...] = sum_ref[pl.ds(0, out_ref.shape[0]), :].astype(jnp.bfloat16)


def final_kernel(in_ref, residual_ref, out_ref, sum_ref):
    total = in_ref[0].astype(jnp.float32)
    for source in range(1, in_ref.shape[0]):
        total += in_ref[source].astype(jnp.float32)
    half = SPAN // 2
    lane = lax.broadcasted_iota(jnp.int32, (LANES, LANES), 0)
    place = lax.broadcasted_iota(jnp.int32, (LANES, LANES), 1)
    target = lane // SPAN * SPAN + lane % half * 2 + lane % SPAN // half
    order = (target == place).astype(jnp.float32)
    sum_ref[...] = jnp.dot(
        total, order, precision=lax.Precision.HIGHEST, preferred_element_type=jnp.float32
    )
    tiles = sum_ref.shape[0] // ROWS_OF_TILE
    for i in range(ROWS_OF_TILE):
        at = pl.ds(i * LANES, LANES)
        out_ref[0, :, at] = residual_ref[0, :, at] + sum_ref[pl.ds(i, tiles, stride=ROWS_OF_TILE), :]


def per_device(rows, groups, cores, tiles, cd_tile, part_dest, place, amplitudes, residual_in):
    held, parts = tiles.shape[0], place.shape[0]
    own_cd = amplitudes.shape[1]
    per_col = residual_in.shape[1]
    bf16, f32 = jnp.bfloat16, jnp.float32
    shape = jax.ShapeDtypeStruct
    owners = rows * groups
    slots = owners * per_col
    swap = [(i, (i + 1) % cores) for i in range(cores)]

    repeated = call(
        repeat_kernel,
        shape((rows, own_cd * ROWS_OF_TILE, LANES), bf16),
        [VMEM],
        amplitudes,
        scratch=[pltpu.VMEM((own_cd * ROWS_OF_TILE, LANES), f32)],
    )
    gathered = lax.all_to_all(repeated, "rows", split_axis=0, concat_axis=0, tiled=True)

    paired = call(
        pair_kernel,
        shape((parts * SPAN, PER_PART * SPAN), bf16),
        [VMEM],
        tiles.reshape(held * ROWS_OF_TILE, LANES),
    )
    col = place // per_col
    slot = (part_dest[:, 0] * groups + col // cores) * per_col + place % per_col
    stays = col % cores == lax.axis_index("core")
    own_slot = jnp.where(stays, slot, slots)
    if cores > 1:
        other_slot = lax.ppermute(jnp.where(stays, slots, slot), "core", swap)
    else:
        other_slot = jnp.full_like(slot, slots)
    gathered, paired, own_slot, other_slot = lax.optimization_barrier(
        (gathered, paired, own_slot, other_slot)
    )

    partial = call(
        partial_kernel,
        shape((parts * ROWS_OF_TILE, LANES), bf16),
        [SMEM, VMEM, VMEM],
        cd_tile,
        gathered.reshape(rows * own_cd * ROWS_OF_TILE, LANES),
        paired,
    )
    other = lax.ppermute(partial, "core", swap)
    summed = shape(((slots + 1) * ROWS_OF_TILE, LANES), f32)
    own_sum = call(own_kernel, summed, [SMEM, VMEM], own_slot, partial)
    dense, _ = call(
        other_kernel,
        [shape((slots * ROWS_OF_TILE, LANES), bf16), summed],
        [SMEM, VMEM, VMEM],
        other_slot,
        other,
        own_sum,
        aliases={2: 1},
    )
    incoming = lax.all_to_all(
        dense.reshape(owners, per_col * ROWS_OF_TILE, LANES),
        ("rows", "groups"),
        split_axis=0,
        concat_axis=0,
        tiled=True,
    )
    return call(
        final_kernel,
        shape(residual_in.shape, f32),
        [VMEM, VMEM],
        incoming,
        residual_in,
        scratch=[pltpu.VMEM((per_col * ROWS_OF_TILE, LANES), f32)],
    )


def solution(mesh):
    rows, cols = mesh.shape["rows"], mesh.shape["cols"]
    cores = 2 if cols % 2 == 0 else 1
    split = Mesh(mesh.devices.reshape(rows, cols // cores, cores), ("rows", "groups", "core"))
    every = ("rows", "groups", "core")
    return jax.shard_map(
        functools.partial(per_device, rows, cols // cores, cores),
        mesh=split,
        in_specs=(
            P(every, None),
            P(every),
            P(every, None),
            P(every),
            P(("groups", "core"), "rows", None),
            P("rows", ("groups", "core"), None),
        ),
        out_specs=P("rows", ("groups", "core"), None),
        check_vma=False,
    )
```

time: 44.1 us -> 42.3 us (0.959)
  waiting for transfers between devices: 8.3 us -> 6.97 us
  local copies, waits for them, and re-layouts: 3.11 us -> 2.33 us
  other arithmetic: 0.01 us -> 0.7 us
  starting transfers between devices: 7.86 us -> 7.39 us
    broadcast_in_dim x2 -> x0, local copies, waits for them, and re-layouts: 1.53 us -> none  [per_device(): repeated = jnp.broadcast_to(shard, (rows,) + shard.shape[1:])]
    all_to_all x1, waiting for transfers between devices: 7.35 us -> 6.2 us  [per_device(): lax.all_to_all(repeated, 'rows', split_axis=0, concat_axis=0, tiled=True)]
    ppermute x1, waiting for transfers between devices: 0.95 us -> 0.01 us  [per_device(): other_slot = lax.ppermute(jnp.where(stays, slots, slot), 'core', swap)]
    ppermute x1, waiting for transfers between devices: 0.01 us -> 0.77 us  [per_device(): other = lax.ppermute(partial, 'core', swap)]
    unnamed x8 -> x6, local copies, waits for them, and re-layouts: 0.02 us -> 0.77 us
    select_n x0 -> x2, other arithmetic: none -> 0.7 us  [the longest x1 0.69 us: per_device(): other_slot = lax.ppermute(jnp.where(stays, slots, slot), 'core', swap)]
    ppermute x1, starting transfers between devices: 0.54 us -> 0.07 us  [per_device(): other_slot = lax.ppermute(jnp.where(stays, slots, slot), 'core', swap)]
    pallas_call x3 -> x6, Pallas kernels: 4.36 us -> 4.68 us  [call(): pl.pallas_call(kernel, out_shape=out_shape, in_specs=in_specs, out_specs=...]
  transfers between devices with their start and end apart: 3 -> 3, of which waited for: 2 -> 2; matrix products, arithmetic and copies ran while one was open for 4% -> 5% of each run, Pallas kernels for 0% -> 3%
where the time goes in v2:
time: 42.3 us; the launch traced here: 42 us
  blocking collectives  19.9 us (47%)
  starting transfers between devices  7.39 us (17%)
  waiting for transfers between devices  6.97 us (16%)
  Pallas kernels  4.68 us (11%)
  local copies, waits for them, and re-layouts  2.33 us (6%)
  other arithmetic  0.7 us (2%)
    all_to_all x1, blocking collectives, per_device(): lax.all_to_all(dense.reshape(owners, per_col * ROWS_OF_TILE, LANES), ('ro...  19.9 us
    all_to_all x1, starting transfers between devices, per_device(): lax.all_to_all(repeated, 'rows', split_axis=0, concat_axis=0, tiled=True)  7.25 us
    all_to_all x1, waiting for transfers between devices, per_device(): lax.all_to_all(repeated, 'rows', split_axis=0, concat_axis=0, tiled=True)  6.2 us
    pallas_call x6, Pallas kernels, call(): pl.pallas_call(kernel, out_shape=out_shape, in_specs=in_specs, out_specs=...  4.68 us
    reshape x1, local copies, waits for them, and re-layouts, per_device(): tiles.reshape(held * ROWS_OF_TILE, LANES)  1.56 us
  transfers between devices with their start and end apart: 3, of which 2 were waited for; matrix products, arithmetic and copies ran while one was open for 5% of the time, Pallas kernels for 3%

profile of v2, /device:TPU:0, one launch (start us, length us, event | category | flops | bytes accessed | tf_op | source)
XLA Modules:
  0.0 42.0 jit_solution(2566131776391241851)
XLA Ops:
  0.0 0.0 copy-start.1
  0.0 0.8 %copy-done.1 = bf16[1,4,4096]{2,1,0:T(4,128)(2,1)S(1)} copy-done((bf16[1,4,4096]{2,1,0:T(4,128)(2,1)S(1)}, bf16[1,4,4096]{2,1,0:T(4,128)(2,1)}, u32[]{:S(2)}) %copy-start.1) | copy-done | bytes 32792
  0.8 0.8 %shard_map.64 = bf16[8,128,128]{2,1,0:T(8,128)(2,1)} custom-call(bf16[1,4,4096]{2,1,0:T(4,128)(2,1)S(1)} %copy-done.1), custom_call_target="tpu_custom_call" | custom-call | tf_op jit(solution)/shard_map/pallas_call | solution.py:22
  1.5 7.3 %all-to-all-start = ((bf16[8,128,128]{2,1,0:T(8,128)(2,1)}), bf16[8,128,128]{2,1,0:T(8,128)(2,1)S(1)}, u32[]{:S(2)}, u32[]{:S(2)}) async-start(bf16[8,128,128]{2,1,0:T(8,128)(2,1)} %shard_map.64), calls=%async_computation | async-start | bytes 524288 | tf_op jit(solution)/shard_map/all_to_all | solution.py:146
  8.8 0.7 %compare_select_fusion.6 = (s32[32]{0:T(128)S(1)}, s32[32]{0:T(128)S(1)}, s32[32]{0:T(128)S(1)}) fusion(s32[]{:T(128)S(6)} %axis_index.12, s32[32]{0:T(128)} %param.9, s32[32,1]{0,1:T(1,128)} %param.8), kind=kLoop, calls=%fused_computation.10 | loop fusion | flops 1408 | bytes 644 | tf_op jit(solution)/shard_map/jit(_where)/select_n | solution.py:159
  9.5 0.1 collective-permute-start
  9.6 1.6 %reshape.11.tile_ref = bf16[4096,128]{1,0:T(8,128)(2,1)S(1)} reshape(bf16[128,4096]{1,0:T(8,128)(2,1)} %param.6) | data formatting | bytes 2097152 | tf_op jit(solution)/shard_map/reshape | solution.py:152
  11.1 0.0 copy-start.2
  11.1 0.3 shard_map.65.tile_ref
  11.5 0.0 collective-permute-done.slot_ref
  11.5 6.2 %all-to-all-done = bf16[8,128,128]{2,1,0:T(8,128)(2,1)S(1)} async-done(((bf16[8,128,128]{2,1,0:T(8,128)(2,1)}), bf16[8,128,128]{2,1,0:T(8,128)(2,1)S(1)}, u32[]{:S(2)}, u32[]{:S(2)}) %all-to-all-start) | async-done | bytes 262176 | tf_op jit(solution)/shard_map/all_to_all | solution.py:146
  17.7 0.0 copy-done.2
  17.7 1.1 %shard_map.66.ref = bf16[1024,128]{1,0:T(8,128)(2,1)S(1)} custom-call(s32[128]{0:T(128)S(1)} %copy-done.2, bf16[1024,128]{1,0:T(8,128)(2,1)S(1)} %bitcast.9, bf16[2048,256]{1,0:T(8,128)(2,1)S(1)} %shard_map.65.tile_ref), custom_call_target="tpu_custom_call" | custom-call | tf_op jit(solution)/shard_map/pallas_call | solution.py:22
  18.8 0.1 collective-permute-start.1
  18.9 0.7 %shard_map.67.in_ref = f32[2080,128]{1,0:T(8,128)S(1)} custom-call(s32[32]{0:T(128)S(1)} %compare_select_fusion.7.slot_ref, bf16[1024,128]{1,0:T(8,128)(2,1)S(1)} %shard_map.66.ref), custom_call_target="tpu_custom_call" | custom-call | tf_op jit(solution)/shard_map/pallas_call | solution.py:22
  19.6 0.0 copy-start
  19.6 0.8 %collective-permute-done.1.ref = bf16[1024,128]{1,0:T(8,128)(2,1)S(1)} collective-permute-done((bf16[1024,128]{1,0:T(8,128)(2,1)S(1)}, bf16[1024,128]{1,0:T(8,128)(2,1)S(1)}, u32[]{:S(2)}, u32[]{:S(2)}) %collective-permute-start.1) | collective-permute-done | bytes 262176 | tf_op jit(solution)/shard_map/ppermute | solution.py:174
  20.4 0.8 %shard_map.68 = (bf16[2048,128]{1,0:T(8,128)(2,1)S(1)}, f32[2080,128]{1,0:T(8,128)S(1)}) custom-call(s32[32]{0:T(128)S(1)} %collective-permute-done.slot_ref, bf16[1024,128]{1,0:T(8,128)(2,1)S(1)} %collective-permute-done.1.ref, f32[2080,128]{1,0:T(8,128)S(1)} %shard_map.67.in_ref), custom_call_target="tpu_custom_call", output_to_operand_aliasing={{1}: (2, {})} | custom-call | tf_op jit(solution)/shard_map/pallas_call | solution.py:22
  21.2 19.9 %all_to_all.10.in_ref = bf16[16,128,128]{2,1,0:T(8,128)(2,1)S(1)} all-to-all(bf16[16,128,128]{2,1,0:T(8,128)(2,1)S(1)} %bitcast.10), channel_id=1, replica_groups=mesh['rows'=8,'groups'=2,'core'=2] {'rows','groups'}, dimensions={0} | all-to-all | bytes 1048576 | tf_op jit(solution)/shard_map/all_to_all | solution.py:186
  41.0 0.0 copy-done
  41.0 1.0 %shard_map.69 = f32[1,4,4096]{2,1,0:T(4,128)} custom-call(bf16[16,128,128]{2,1,0:T(8,128)(2,1)S(1)} %all_to_all.10.in_ref, f32[1,4,4096]{2,1,0:T(4,128)S(1)} %copy-done), custom_call_target="tpu_custom_call" | custom-call | tf_op jit(solution)/shard_map/pallas_call | solution.py:22
  (1 shorter events, 0.0 us)
Async XLA Ops:
  0.0 0.8 %copy-start.1 = (bf16[1,4,4096]{2,1,0:T(4,128)(2,1)S(1)}, bf16[1,4,4096]{2,1,0:T(4,128)(2,1)}, u32[]{:S(2)}) copy-start(bf16[1,4,4096]{2,1,0:T(4,128)(2,1)} %in_ref.1) | copy-start | bytes 98308
  1.5 16.2 %all-to-all-start = ((bf16[8,128,128]{2,1,0:T(8,128)(2,1)}), bf16[8,128,128]{2,1,0:T(8,128)(2,1)S(1)}, u32[]{:S(2)}, u32[]{:S(2)}) async-start(bf16[8,128,128]{2,1,0:T(8,128)(2,1)} %shard_map.64), calls=%async_computation | async-start | bytes 524288 | tf_op jit(solution)/shard_map/all_to_all | solution.py:146
  9.5 2.0 %collective-permute-start = (s32[32]{0:T(128)S(1)}, s32[32]{0:T(128)S(1)}, u32[]{:S(2)}, u32[]{:S(2)}) collective-permute-start(s32[32]{0:T(128)S(1)} %get-tuple-element.15), channel_id=1, source_target_pairs={{0,1},{1,0},{2,3},{3,2},{4,5},{5,4},{6,7},{7,6},{8,9},{9,8},{10,11... | collective-permute-start | bytes 392 | tf_op jit(solution)/shard_map/ppermute | solution.py:159
  11.1 6.6 %copy-start.2 = (s32[128]{0:T(128)S(1)}, s32[128]{0:T(128)}, u32[]{:S(2)}) copy-start(s32[128]{0:T(128)} %cd_ref.1) | copy-start | bytes 1540
  18.8 1.6 %collective-permute-start.1 = (bf16[1024,128]{1,0:T(8,128)(2,1)S(1)}, bf16[1024,128]{1,0:T(8,128)(2,1)S(1)}, u32[]{:S(2)}, u32[]{:S(2)}) collective-permute-start(bf16[1024,128]{1,0:T(8,128)(2,1)S(1)} %shard_map.66.ref), channel_id=1, source_target_pairs={{0,1},{1,0},{2,3},{3,2},{4,5},{5,4},{6,7},{7,6},{8,9},{9,8},{10,11... | collective-permute-start | bytes 786440 | tf_op jit(solution)/shard_map/ppermute | solution.py:174
  19.6 21.4 %copy-start = (f32[1,4,4096]{2,1,0:T(4,128)S(1)}, f32[1,4,4096]{2,1,0:T(4,128)}, u32[]{:S(2)}) copy-start(f32[1,4,4096]{2,1,0:T(4,128)} %residual_ref.1) | copy-start | bytes 196612

commit v3 on v2

--- a/solution.py
+++ b/solution.py
@@ -1,4 +1,5 @@
 import functools
+import itertools
 
 import jax
 import jax.numpy as jnp
@@ -13,6 +14,7 @@
 PER_PART = 4
 OWNR = 16
 ROWS_OF_TILE = SPAN * SPAN // LANES
+MOST_PERMUTED = 4
 VMEM = pl.BlockSpec(memory_space=pltpu.VMEM)
 SMEM = pl.BlockSpec(memory_space=pltpu.SMEM)
 
@@ -103,15 +105,35 @@
     add_tiles(slot_ref, ref, sum_ref)
 
 
-def other_kernel(slot_ref, ref, in_ref, out_ref, sum_ref):
+def other_kernel(slot_ref, ref, in_ref, *refs):
+    out_refs, sum_ref = refs[:-1], refs[-1]
     add_tiles(slot_ref, ref, sum_ref)
-    out_ref[...] = sum_ref[pl.ds(0, out_ref.shape[0]), :].astype(jnp.bfloat16)
-
-
-def final_kernel(in_ref, residual_ref, out_ref, sum_ref):
-    total = in_ref[0].astype(jnp.float32)
-    for source in range(1, in_ref.shape[0]):
-        total += in_ref[source].astype(jnp.float32)
+    for block, out_ref in enumerate(out_refs):
+        size = out_ref.shape[0]
+        out_ref[...] = sum_ref[pl.ds((block + 1) * size, size), :].astype(jnp.bfloat16)
+
+
+def plane_kernel(others, own_ref, *refs):
+    in_refs, out_refs = refs[:others], refs[others:]
+    start = 0
+    for out_ref in out_refs:
+        at = pl.ds(start, out_ref.shape[0])
+        total = own_ref[at, :]
+        for ref in in_refs:
+            total += ref[at, :].astype(jnp.float32)
+        out_ref[...] = total.astype(out_ref.dtype)
+        start += out_ref.shape[0]
+
+
+def final_kernel(*refs):
+    in_refs, (residual_ref, out_ref, sum_ref) = refs[:-3], refs[-3:]
+    size = sum_ref.shape[0]
+    blocks = [
+        ref[pl.ds(first, size), :] for ref in in_refs for first in range(0, ref.shape[0], size)
+    ]
+    total = blocks[0].astype(jnp.float32)
+    for block in blocks[1:]:
+        total += block.astype(jnp.float32)
     half = SPAN // 2
     lane = lax.broadcasted_iota(jnp.int32, (LANES, LANES), 0)
     place = lax.broadcasted_iota(jnp.int32, (LANES, LANES), 1)
@@ -120,20 +142,34 @@
     sum_ref[...] = jnp.dot(
         total, order, precision=lax.Precision.HIGHEST, preferred_element_type=jnp.float32
     )
-    tiles = sum_ref.shape[0] // ROWS_OF_TILE
+    tiles = size // ROWS_OF_TILE
     for i in range(ROWS_OF_TILE):
         at = pl.ds(i * LANES, LANES)
         out_ref[0, :, at] = residual_ref[0, :, at] + sum_ref[pl.ds(i, tiles, stride=ROWS_OF_TILE), :]
 
 
-def per_device(rows, groups, cores, tiles, cd_tile, part_dest, place, amplitudes, residual_in):
+def shifts(sizes):
+    places = list(itertools.product(*map(range, sizes)))
+    number = {place: i for i, place in enumerate(places)}
+    return [
+        [
+            (number[p], number[tuple((a + b) % n for a, b, n in zip(p, offset, sizes))])
+            for p in places
+        ]
+        for offset in places[1:]
+    ]
+
+
+def per_device(outer, inner, groups, cores, tiles, cd_tile, part_dest, place, amplitudes, residual_in):
     held, parts = tiles.shape[0], place.shape[0]
     own_cd = amplitudes.shape[1]
     per_col = residual_in.shape[1]
     bf16, f32 = jnp.bfloat16, jnp.float32
     shape = jax.ShapeDtypeStruct
-    owners = rows * groups
-    slots = owners * per_col
+    rows = outer * inner
+    plane = inner * groups
+    slots = rows * groups * per_col
+    by_permutes = outer <= MOST_PERMUTED
     swap = [(i, (i + 1) % cores) for i in range(cores)]
 
     repeated = call(
@@ -143,7 +179,7 @@
         amplitudes,
         scratch=[pltpu.VMEM((own_cd * ROWS_OF_TILE, LANES), f32)],
     )
-    gathered = lax.all_to_all(repeated, "rows", split_axis=0, concat_axis=0, tiled=True)
+    gathered = lax.all_to_all(repeated, ("outer", "inner"), split_axis=0, concat_axis=0, tiled=True)
 
     paired = call(
         pair_kernel,
@@ -151,8 +187,13 @@
         [VMEM],
         tiles.reshape(held * ROWS_OF_TILE, LANES),
     )
-    col = place // per_col
-    slot = (part_dest[:, 0] * groups + col // cores) * per_col + place % per_col
+    dest, col = part_dest[:, 0], place // per_col
+    to_inner = (dest % inner - lax.axis_index("inner")) % inner
+    to_group = (col // cores - lax.axis_index("groups")) % groups
+    to_outer = dest // inner
+    if by_permutes:
+        to_outer = (to_outer - lax.axis_index("outer")) % outer
+    slot = ((to_inner * groups + to_group) * outer + to_outer) * per_col + place % per_col
     stays = col % cores == lax.axis_index("core")
     own_slot = jnp.where(stays, slot, slots)
     if cores > 1:
@@ -174,48 +215,70 @@
     other = lax.ppermute(partial, "core", swap)
     summed = shape(((slots + 1) * ROWS_OF_TILE, LANES), f32)
     own_sum = call(own_kernel, summed, [SMEM, VMEM], own_slot, partial)
-    dense, _ = call(
+    block = slots // plane * ROWS_OF_TILE
+    *leaving, own_sum = call(
         other_kernel,
-        [shape((slots * ROWS_OF_TILE, LANES), bf16), summed],
+        [shape((block, LANES), bf16)] * (plane - 1) + [summed],
         [SMEM, VMEM, VMEM],
         other_slot,
         other,
         own_sum,
-        aliases={2: 1},
-    )
-    incoming = lax.all_to_all(
-        dense.reshape(owners, per_col * ROWS_OF_TILE, LANES),
-        ("rows", "groups"),
-        split_axis=0,
-        concat_axis=0,
-        tiled=True,
-    )
+        aliases={2: plane - 1},
+    )
+    arrived = [
+        lax.ppermute(x, ("inner", "groups"), pairs)
+        for x, pairs in zip(leaving, shifts((inner, groups)))
+    ]
+    mine = per_col * ROWS_OF_TILE
+    if by_permutes:
+        split = [shape((mine, LANES), f32)] + [shape((mine, LANES), bf16)] * (outer - 1)
+    else:
+        split = [shape((outer * mine, LANES), bf16)]
+    sums = call(
+        functools.partial(plane_kernel, len(arrived)),
+        split,
+        [VMEM] * (1 + len(arrived)),
+        own_sum,
+        *arrived,
+    )
+    if by_permutes:
+        incoming = [sums[0]] + [
+            lax.ppermute(x, "outer", pairs) for x, pairs in zip(sums[1:], shifts((outer,)))
+        ]
+    else:
+        incoming = [
+            lax.all_to_all(
+                sums[0].reshape(outer, mine, LANES), "outer", split_axis=0, concat_axis=0, tiled=True
+            ).reshape(outer * mine, LANES)
+        ]
     return call(
         final_kernel,
         shape(residual_in.shape, f32),
-        [VMEM, VMEM],
-        incoming,
+        [VMEM] * (len(incoming) + 1),
+        *incoming,
         residual_in,
-        scratch=[pltpu.VMEM((per_col * ROWS_OF_TILE, LANES), f32)],
+        scratch=[pltpu.VMEM((mine, LANES), f32)],
     )
 
 
 def solution(mesh):
     rows, cols = mesh.shape["rows"], mesh.shape["cols"]
+    inner = 2 if rows % 2 == 0 else 1
     cores = 2 if cols % 2 == 0 else 1
-    split = Mesh(mesh.devices.reshape(rows, cols // cores, cores), ("rows", "groups", "core"))
-    every = ("rows", "groups", "core")
+    axes = ("outer", "inner", "groups", "core")
+    sizes = (rows // inner, inner, cols // cores, cores)
+    split = Mesh(mesh.devices.reshape(sizes), axes)
     return jax.shard_map(
-        functools.partial(per_device, rows, cols // cores, cores),
+        functools.partial(per_device, *sizes),
         mesh=split,
         in_specs=(
-            P(every, None),
-            P(every),
-            P(every, None),
-            P(every),
-            P(("groups", "core"), "rows", None),
-            P("rows", ("groups", "core"), None),
+            P(axes, None),
+            P(axes),
+            P(axes, None),
+            P(axes),
+            P(axes[2:], axes[:2], None),
+            P(axes[:2], axes[2:], None),
         ),
-        out_specs=P("rows", ("groups", "core"), None),
+        out_specs=P(axes[:2], axes[2:], None),
         check_vma=False,
     )

time: 42.3 us -> 38.8 us (0.917)
  blocking collectives: 19.9 us -> 0 us
  waiting for transfers between devices: 6.97 us -> 15.7 us
  starting transfers between devices: 7.39 us -> 15 us
    all_to_all x1 -> x0, blocking collectives: 19.9 us -> none  [per_device(): lax.all_to_all(dense.reshape(owners, per_col * ROWS_OF_TILE, LANES), ('ro...]
    ppermute x0 -> x6, waiting for transfers between devices: none -> 8.73 us  [the longest x3 6.03 us: per_device(): lax.ppermute(x, ('inner', 'groups'), pairs)]
    ppermute x0 -> x6, starting transfers between devices: none -> 7.58 us  [the longest x3 4.03 us: per_device(): lax.ppermute(x, 'outer', pairs)]
    pallas_call x6 -> x7, Pallas kernels: 4.68 us -> 4.66 us  [call(): pl.pallas_call(kernel, out_shape=out_shape, in_specs=in_specs, out_specs=...]
  transfers between devices with their start and end apart: 3 -> 9, of which waited for: 2 -> 7; matrix products, arithmetic and copies ran while one was open for 5% -> 6% of each run, Pallas kernels for 3% -> 3%
where the time goes in v3:
time: 38.8 us; the launch traced here: 38.4 us
  waiting for transfers between devices  15.7 us (40%)
  starting transfers between devices  15 us (39%)
  Pallas kernels  4.66 us (12%)
  local copies, waits for them, and re-layouts  2.33 us (6%)
  other arithmetic  0.71 us (2%)
    all_to_all x1, starting transfers between devices, per_device(): lax.all_to_all(repeated, ('outer', 'inner'), split_axis=0, concat_axis=0,...  7.25 us
    all_to_all x1, waiting for transfers between devices, per_device(): lax.all_to_all(repeated, ('outer', 'inner'), split_axis=0, concat_axis=0,...  6.19 us
    ppermute x3, waiting for transfers between devices, per_device(): lax.ppermute(x, ('inner', 'groups'), pairs)  6.03 us
    pallas_call x7, Pallas kernels, call(): pl.pallas_call(kernel, out_shape=out_shape, in_specs=in_specs, out_specs=...  4.66 us
    ppermute x3, starting transfers between devices, per_device(): lax.ppermute(x, 'outer', pairs)  4.03 us
    ppermute x3, starting transfers between devices, per_device(): lax.ppermute(x, ('inner', 'groups'), pairs)  3.55 us
    ppermute x3, waiting for transfers between devices, per_device(): lax.ppermute(x, 'outer', pairs)  2.7 us
    reshape x1, local copies, waits for them, and re-layouts, per_device(): tiles.reshape(held * ROWS_OF_TILE, LANES)  1.56 us
  transfers between devices with their start and end apart: 9, of which 7 were waited for; matrix products, arithmetic and copies ran while one was open for 6% of the time, Pallas kernels for 3%

profile of v3, /device:TPU:0, one launch (start us, length us, event | category | flops | bytes accessed | tf_op | source)
XLA Modules:
  0.0 38.4 jit_solution(17815662689825202624)
XLA Ops:
  0.0 0.0 copy-start.1
  0.0 0.8 %copy-done.1 = bf16[1,4,4096]{2,1,0:T(4,128)(2,1)S(1)} copy-done((bf16[1,4,4096]{2,1,0:T(4,128)(2,1)S(1)}, bf16[1,4,4096]{2,1,0:T(4,128)(2,1)}, u32[]{:S(2)}) %copy-start.1) | copy-done | bytes 32792
  0.8 0.8 %shard_map.64 = bf16[8,128,128]{2,1,0:T(8,128)(2,1)} custom-call(bf16[1,4,4096]{2,1,0:T(4,128)(2,1)S(1)} %copy-done.1), custom_call_target="tpu_custom_call" | custom-call | tf_op jit(solution)/shard_map/pallas_call | solution.py:24
  1.5 7.3 %all-to-all-start = ((bf16[8,128,128]{2,1,0:T(8,128)(2,1)}), bf16[8,128,128]{2,1,0:T(8,128)(2,1)S(1)}, u32[]{:S(2)}, u32[]{:S(2)}) async-start(bf16[8,128,128]{2,1,0:T(8,128)(2,1)} %shard_map.64), calls=%async_computation | async-start | bytes 524288 | tf_op jit(solution)/shard_map/all_to_all | solution.py:182
  8.8 0.7 %compare_select_fusion.15 = (s32[32]{0:T(128)S(1)}, s32[32]{0:T(128)S(1)}, s32[32]{0:T(128)S(1)}) fusion(s32[]{:T(128)S(6)} %axis_index.42, s32[32]{0:T(128)} %param.9, s32[]{:T(128)S(6)} %axis_index.51, s32[]{:T(128)S(6)} %axis_index.48, s32[]{:T(128)S(6)} %axis_index.45, s32[32,1]{0,1:T(1,128)} %param.8), kind=kLoop, calls=%fused_computation.24 | loop fusion | flops 3232 | bytes 656 | tf_op jit(solution)/shard_map/jit(_where)/select_n | solution.py:200
  9.5 0.1 collective-permute-start
  9.6 1.6 %reshape.6.tile_ref = bf16[4096,128]{1,0:T(8,128)(2,1)S(1)} reshape(bf16[128,4096]{1,0:T(8,128)(2,1)} %param.6) | data formatting | bytes 2097152 | tf_op jit(solution)/shard_map/reshape | solution.py:188
  11.1 0.0 copy-start.2
  11.1 0.3 shard_map.65.tile_ref
  11.5 0.0 collective-permute-done.slot_ref
  11.5 6.2 %all-to-all-done = bf16[8,128,128]{2,1,0:T(8,128)(2,1)S(1)} async-done(((bf16[8,128,128]{2,1,0:T(8,128)(2,1)}), bf16[8,128,128]{2,1,0:T(8,128)(2,1)S(1)}, u32[]{:S(2)}, u32[]{:S(2)}) %all-to-all-start) | async-done | bytes 262176 | tf_op jit(solution)/shard_map/all_to_all | solution.py:182
  17.7 0.0 copy-done.2
  17.7 1.1 %shard_map.66.ref = bf16[1024,128]{1,0:T(8,128)(2,1)S(1)} custom-call(s32[128]{0:T(128)S(1)} %copy-done.2, bf16[1024,128]{1,0:T(8,128)(2,1)S(1)} %bitcast.15, bf16[2048,256]{1,0:T(8,128)(2,1)S(1)} %shard_map.65.tile_ref), custom_call_target="tpu_custom_call" | custom-call | tf_op jit(solution)/shard_map/pallas_call | solution.py:24
  18.8 0.1 collective-permute-start.1
  18.9 0.7 %shard_map.67.in_ref = f32[2080,128]{1,0:T(8,128)S(1)} custom-call(s32[32]{0:T(128)S(1)} %compare_select_fusion.16.slot_ref, bf16[1024,128]{1,0:T(8,128)(2,1)S(1)} %shard_map.66.ref), custom_call_target="tpu_custom_call" | custom-call | tf_op jit(solution)/shard_map/pallas_call | solution.py:24
  19.6 0.8 %collective-permute-done.1.ref = bf16[1024,128]{1,0:T(8,128)(2,1)S(1)} collective-permute-done((bf16[1024,128]{1,0:T(8,128)(2,1)S(1)}, bf16[1024,128]{1,0:T(8,128)(2,1)S(1)}, u32[]{:S(2)}, u32[]{:S(2)}) %collective-permute-start.1) | collective-permute-done | bytes 262176 | tf_op jit(solution)/shard_map/ppermute | solution.py:215
  20.4 0.7 %shard_map.68 = (bf16[512,128]{1,0:T(8,128)(2,1)S(1)}, bf16[512,128]{1,0:T(8,128)(2,1)S(1)}, bf16[512,128]{1,0:T(8,128)(2,1)S(1)}, f32[2080,128]{1,0:T(8,128)S(1)}) custom-call(s32[32]{0:T(128)S(1)} %collective-permute-done.slot_ref, bf16[1024,128]{1,0:T(8,128)(2,1)S(1)} %collective-permute-done.1.ref, ...), custom_call_target="tpu_custom_call", output_to_operand_aliasing={{3}: (2, {})} | custom-call | tf_op jit(solution)/shard_map/pallas_call | solution.py:24
  21.1 0.0 copy-start
  21.2 1.6 %collective-permute-start.2 = (bf16[512,128]{1,0:T(8,128)(2,1)S(1)}, bf16[512,128]{1,0:T(8,128)(2,1)S(1)}, u32[]{:S(2)}, u32[]{:S(2)}) collective-permute-start(bf16[512,128]{1,0:T(8,128)(2,1)S(1)} %get-tuple-element.22), channel_id=1, source_target_pairs={{0,2},{2,0},{4,6},{6,4},{1,3},{3,1},{5,7},{7,5},{8,10},{10,8},{12,... | collective-permute-start | bytes 393224 | tf_op jit(solution)/shard_map/ppermute | solution.py:229
  22.8 1.4 %collective-permute-start.3 = (bf16[512,128]{1,0:T(8,128)(2,1)S(1)}, bf16[512,128]{1,0:T(8,128)(2,1)S(1)}, u32[]{:S(2)}, u32[]{:S(2)}) collective-permute-start(bf16[512,128]{1,0:T(8,128)(2,1)S(1)} %get-tuple-element.23), channel_id=1, source_target_pairs={{0,4},{2,6},{4,0},{6,2},{1,5},{3,7},{5,1},{7,3},{8,12},{10,14},{12... | collective-permute-start | bytes 393224 | tf_op jit(solution)/shard_map/ppermute | solution.py:229
  24.2 0.5 %collective-permute-start.4 = (bf16[512,128]{1,0:T(8,128)(2,1)S(1)}, bf16[512,128]{1,0:T(8,128)(2,1)S(1)}, u32[]{:S(2)}, u32[]{:S(2)}) collective-permute-start(bf16[512,128]{1,0:T(8,128)(2,1)S(1)} %get-tuple-element.24), channel_id=1, source_target_pairs={{0,6},{2,4},{4,2},{6,0},{1,7},{3,5},{5,3},{7,1},{8,14},{10,12},{12... | collective-permute-start | bytes 393224 | tf_op jit(solution)/shard_map/ppermute | solution.py:229
  24.7 2.0 %collective-permute-done.2.refs_0_ = bf16[512,128]{1,0:T(8,128)(2,1)S(1)} collective-permute-done((bf16[512,128]{1,0:T(8,128)(2,1)S(1)}, bf16[512,128]{1,0:T(8,128)(2,1)S(1)}, u32[]{:S(2)}, u32[]{:S(2)}) %collective-permute-start.2) | collective-permute-done | bytes 131104 | tf_op jit(solution)/shard_map/ppermute | solution.py:229
  26.8 2.4 %collective-permute-done.3.refs_1_ = bf16[512,128]{1,0:T(8,128)(2,1)S(1)} collective-permute-done((bf16[512,128]{1,0:T(8,128)(2,1)S(1)}, bf16[512,128]{1,0:T(8,128)(2,1)S(1)}, u32[]{:S(2)}, u32[]{:S(2)}) %collective-permute-start.3) | collective-permute-done | bytes 131104 | tf_op jit(solution)/shard_map/ppermute | solution.py:229
  29.1 1.6 %collective-permute-done.4.refs_2_ = bf16[512,128]{1,0:T(8,128)(2,1)S(1)} collective-permute-done((bf16[512,128]{1,0:T(8,128)(2,1)S(1)}, bf16[512,128]{1,0:T(8,128)(2,1)S(1)}, u32[]{:S(2)}, u32[]{:S(2)}) %collective-permute-start.4) | collective-permute-done | bytes 131104 | tf_op jit(solution)/shard_map/ppermute | solution.py:229
  30.7 0.1 shard_map.69
  30.8 1.1 %collective-permute-start.5 = (bf16[128,128]{1,0:T(8,128)(2,1)S(1)}, bf16[128,128]{1,0:T(8,128)(2,1)S(1)}, u32[]{:S(2)}, u32[]{:S(2)}) collective-permute-start(bf16[128,128]{1,0:T(8,128)(2,1)S(1)} %get-tuple-element.26), channel_id=1, source_target_pairs={{0,8},{8,16},{16,24},{24,0},{1,9},{9,17},{17,25},{25,1},{2,10},{10... | collective-permute-start | bytes 98312 | tf_op jit(solution)/shard_map/ppermute | solution.py:246
  32.0 0.6 %collective-permute-start.6 = (bf16[128,128]{1,0:T(8,128)(2,1)S(1)}, bf16[128,128]{1,0:T(8,128)(2,1)S(1)}, u32[]{:S(2)}, u32[]{:S(2)}) collective-permute-start(bf16[128,128]{1,0:T(8,128)(2,1)S(1)} %get-tuple-element.27), channel_id=1, source_target_pairs={{0,16},{8,24},{16,0},{24,8},{1,17},{9,25},{17,1},{25,9},{2,18},{10... | collective-permute-start | bytes 98312 | tf_op jit(solution)/shard_map/ppermute | solution.py:246
  32.6 2.2 %collective-permute-start.7 = (bf16[128,128]{1,0:T(8,128)(2,1)S(1)}, bf16[128,128]{1,0:T(8,128)(2,1)S(1)}, u32[]{:S(2)}, u32[]{:S(2)}) collective-permute-start(bf16[128,128]{1,0:T(8,128)(2,1)S(1)} %get-tuple-element.28), channel_id=1, source_target_pairs={{0,24},{8,0},{16,8},{24,16},{1,25},{9,1},{17,9},{25,17},{2,26},{10... | collective-permute-start | bytes 98312 | tf_op jit(solution)/shard_map/ppermute | solution.py:246
  34.9 1.8 %collective-permute-done.5.refs_1_ = bf16[128,128]{1,0:T(8,128)(2,1)S(1)} collective-permute-done((bf16[128,128]{1,0:T(8,128)(2,1)S(1)}, bf16[128,128]{1,0:T(8,128)(2,1)S(1)}, u32[]{:S(2)}, u32[]{:S(2)}) %collective-permute-start.5) | collective-permute-done | bytes 32800 | tf_op jit(solution)/shard_map/ppermute | solution.py:246
  36.7 0.9 %collective-permute-done.6.refs_2_ = bf16[128,128]{1,0:T(8,128)(2,1)S(1)} collective-permute-done((bf16[128,128]{1,0:T(8,128)(2,1)S(1)}, bf16[128,128]{1,0:T(8,128)(2,1)S(1)}, u32[]{:S(2)}, u32[]{:S(2)}) %collective-permute-start.6) | collective-permute-done | bytes 32800 | tf_op jit(solution)/shard_map/ppermute | solution.py:246
  37.5 0.0 collective-permute-done.7.refs_3_
  37.5 0.0 copy-done
  37.6 0.9 %shard_map.70 = f32[1,4,4096]{2,1,0:T(4,128)} custom-call(f32[128,128]{1,0:T(8,128)S(1)} %get-tuple-element.25.refs_0_, bf16[128,128]{1,0:T(8,128)(2,1)S(1)} %collective-permute-done.5.refs_1_, bf16[128,128]{1,0:T(8,128)(2,1)S(1)} %collective-permute-done.6.refs_2_, bf16[128,128]{1,0:T(8,128)(2,1)S(1)} %collective-permute-done.7.refs_3_, ...), custom_call_target="tpu_custom_call" | custom-call | tf_op jit(solution)/shard_map/pallas_call | solution.py:24
  (1 shorter events, 0.0 us)
Async XLA Ops:
  0.0 0.8 %copy-start.1 = (bf16[1,4,4096]{2,1,0:T(4,128)(2,1)S(1)}, bf16[1,4,4096]{2,1,0:T(4,128)(2,1)}, u32[]{:S(2)}) copy-start(bf16[1,4,4096]{2,1,0:T(4,128)(2,1)} %in_ref.1) | copy-start | bytes 98308
  1.5 16.2 %all-to-all-start = ((bf16[8,128,128]{2,1,0:T(8,128)(2,1)}), bf16[8,128,128]{2,1,0:T(8,128)(2,1)S(1)}, u32[]{:S(2)}, u32[]{:S(2)}) async-start(bf16[8,128,128]{2,1,0:T(8,128)(2,1)} %shard_map.64), calls=%async_computation | async-start | bytes 524288 | tf_op jit(solution)/shard_map/all_to_all | solution.py:182
  9.5 2.0 %collective-permute-start = (s32[32]{0:T(128)S(1)}, s32[32]{0:T(128)S(1)}, u32[]{:S(2)}, u32[]{:S(2)}) collective-permute-start(s32[32]{0:T(128)S(1)} %get-tuple-element.29), channel_id=1, source_target_pairs={{0,1},{1,0},{2,3},{3,2},{4,5},{5,4},{6,7},{7,6},{8,9},{9,8},{10,11... | collective-permute-start | bytes 392 | tf_op jit(solution)/shard_map/ppermute | solution.py:200
  11.1 6.6 %copy-start.2 = (s32[128]{0:T(128)S(1)}, s32[128]{0:T(128)}, u32[]{:S(2)}) copy-start(s32[128]{0:T(128)} %cd_ref.1) | copy-start | bytes 1540
  18.8 1.6 %collective-permute-start.1 = (bf16[1024,128]{1,0:T(8,128)(2,1)S(1)}, bf16[1024,128]{1,0:T(8,128)(2,1)S(1)}, u32[]{:S(2)}, u32[]{:S(2)}) collective-permute-start(bf16[1024,128]{1,0:T(8,128)(2,1)S(1)} %shard_map.66.ref), channel_id=1, source_target_pairs={{0,1},{1,0},{2,3},{3,2},{4,5},{5,4},{6,7},{7,6},{8,9},{9,8},{10,11... | collective-permute-start | bytes 786440 | tf_op jit(solution)/shard_map/ppermute | solution.py:215
  21.1 16.4 %copy-start = (f32[1,4,4096]{2,1,0:T(4,128)S(1)}, f32[1,4,4096]{2,1,0:T(4,128)}, u32[]{:S(2)}) copy-start(f32[1,4,4096]{2,1,0:T(4,128)} %refs_4_.1) | copy-start | bytes 196612
  21.2 5.6 %collective-permute-start.2 = (bf16[512,128]{1,0:T(8,128)(2,1)S(1)}, bf16[512,128]{1,0:T(8,128)(2,1)S(1)}, u32[]{:S(2)}, u32[]{:S(2)}) collective-permute-start(bf16[512,128]{1,0:T(8,128)(2,1)S(1)} %get-tuple-element.22), channel_id=1, source_target_pairs={{0,2},{2,0},{4,6},{6,4},{1,3},{3,1},{5,7},{7,5},{8,10},{10,8},{12,... | collective-permute-start | bytes 393224 | tf_op jit(solution)/shard_map/ppermute | solution.py:229
  22.8 6.4 %collective-permute-start.3 = (bf16[512,128]{1,0:T(8,128)(2,1)S(1)}, bf16[512,128]{1,0:T(8,128)(2,1)S(1)}, u32[]{:S(2)}, u32[]{:S(2)}) collective-permute-start(bf16[512,128]{1,0:T(8,128)(2,1)S(1)} %get-tuple-element.23), channel_id=1, source_target_pairs={{0,4},{2,6},{4,0},{6,2},{1,5},{3,7},{5,1},{7,3},{8,12},{10,14},{12... | collective-permute-start | bytes 393224 | tf_op jit(solution)/shard_map/ppermute | solution.py:229
  24.2 6.6 %collective-permute-start.4 = (bf16[512,128]{1,0:T(8,128)(2,1)S(1)}, bf16[512,128]{1,0:T(8,128)(2,1)S(1)}, u32[]{:S(2)}, u32[]{:S(2)}) collective-permute-start(bf16[512,128]{1,0:T(8,128)(2,1)S(1)} %get-tuple-element.24), channel_id=1, source_target_pairs={{0,6},{2,4},{4,2},{6,0},{1,7},{3,5},{5,3},{7,1},{8,14},{10,12},{12... | collective-permute-start | bytes 393224 | tf_op jit(solution)/shard_map/ppermute | solution.py:229
  30.8 5.9 %collective-permute-start.5 = (bf16[128,128]{1,0:T(8,128)(2,1)S(1)}, bf16[128,128]{1,0:T(8,128)(2,1)S(1)}, u32[]{:S(2)}, u32[]{:S(2)}) collective-permute-start(bf16[128,128]{1,0:T(8,128)(2,1)S(1)} %get-tuple-element.26), channel_id=1, source_target_pairs={{0,8},{8,16},{16,24},{24,0},{1,9},{9,17},{17,25},{25,1},{2,10},{10... | collective-permute-start | bytes 98312 | tf_op jit(solution)/shard_map/ppermute | solution.py:246
  32.0 5.6 %collective-permute-start.6 = (bf16[128,128]{1,0:T(8,128)(2,1)S(1)}, bf16[128,128]{1,0:T(8,128)(2,1)S(1)}, u32[]{:S(2)}, u32[]{:S(2)}) collective-permute-start(bf16[128,128]{1,0:T(8,128)(2,1)S(1)} %get-tuple-element.27), channel_id=1, source_target_pairs={{0,16},{8,24},{16,0},{24,8},{1,17},{9,25},{17,1},{25,9},{2,18},{10... | collective-permute-start | bytes 98312 | tf_op jit(solution)/shard_map/ppermute | solution.py:246
  32.6 4.9 %collective-permute-start.7 = (bf16[128,128]{1,0:T(8,128)(2,1)S(1)}, bf16[128,128]{1,0:T(8,128)(2,1)S(1)}, u32[]{:S(2)}, u32[]{:S(2)}) collective-permute-start(bf16[128,128]{1,0:T(8,128)(2,1)S(1)} %get-tuple-element.28), channel_id=1, source_target_pairs={{0,24},{8,0},{16,8},{24,16},{1,25},{9,1},{17,9},{25,17},{2,26},{10... | collective-permute-start | bytes 98312 | tf_op jit(solution)/shard_map/ppermute | solution.py:246

commit v4 on v3

--- a/solution.py
+++ b/solution.py
@@ -148,16 +148,24 @@
         out_ref[0, :, at] = residual_ref[0, :, at] + sum_ref[pl.ds(i, tiles, stride=ROWS_OF_TILE), :]
 
 
-def shifts(sizes):
+def offset(to, start, size):
+    return to ^ start if size & (size - 1) == 0 else (to - start) % size
+
+
+def permutes(sizes):
     places = list(itertools.product(*map(range, sizes)))
     number = {place: i for i, place in enumerate(places)}
-    return [
-        [
-            (number[p], number[tuple((a + b) % n for a, b, n in zip(p, offset, sizes))])
-            for p in places
-        ]
-        for offset in places[1:]
-    ]
+
+    def moved(place, by):
+        return tuple(
+            a ^ b if n & (n - 1) == 0 else (a + b) % n for a, b, n in zip(place, by, sizes)
+        )
+
+    return [[(number[p], number[moved(p, by)]) for p in places] for by in places[1:]]
+
+
+def exchange(blocks, axes, sizes):
+    return [lax.ppermute(x, axes, pairs) for x, pairs in zip(blocks, permutes(sizes))][::-1]
 
 
 def per_device(outer, inner, groups, cores, tiles, cd_tile, part_dest, place, amplitudes, residual_in):
@@ -188,11 +196,11 @@
         tiles.reshape(held * ROWS_OF_TILE, LANES),
     )
     dest, col = part_dest[:, 0], place // per_col
-    to_inner = (dest % inner - lax.axis_index("inner")) % inner
-    to_group = (col // cores - lax.axis_index("groups")) % groups
+    to_inner = offset(dest % inner, lax.axis_index("inner"), inner)
+    to_group = offset(col // cores, lax.axis_index("groups"), groups)
     to_outer = dest // inner
     if by_permutes:
-        to_outer = (to_outer - lax.axis_index("outer")) % outer
+        to_outer = offset(to_outer, lax.axis_index("outer"), outer)
     slot = ((to_inner * groups + to_group) * outer + to_outer) * per_col + place % per_col
     stays = col % cores == lax.axis_index("core")
     own_slot = jnp.where(stays, slot, slots)
@@ -225,10 +233,7 @@
         own_sum,
         aliases={2: plane - 1},
     )
-    arrived = [
-        lax.ppermute(x, ("inner", "groups"), pairs)
-        for x, pairs in zip(leaving, shifts((inner, groups)))
-    ]
+    arrived = exchange(leaving, ("inner", "groups"), (inner, groups))
     mine = per_col * ROWS_OF_TILE
     if by_permutes:
         split = [shape((mine, LANES), f32)] + [shape((mine, LANES), bf16)] * (outer - 1)
@@ -242,9 +247,7 @@
         *arrived,
     )
     if by_permutes:
-        incoming = [sums[0]] + [
-            lax.ppermute(x, "outer", pairs) for x, pairs in zip(sums[1:], shifts((outer,)))
-        ]
+        incoming = exchange(sums[1:], ("outer",), (outer,)) + [sums[0]]
     else:
         incoming = [
             lax.all_to_all(

time: 38.8 us -> 38.5 us (level)
  waiting for transfers between devices: 15.7 us -> 15 us
  starting transfers between devices: 15 us -> 15.4 us
    ppermute x6, waiting for transfers between devices: 8.73 us -> 8.03 us  [exchange(): lax.ppermute(x, axes, pairs)]
    ppermute x6, starting transfers between devices: 7.58 us -> 8.01 us  [exchange(): lax.ppermute(x, axes, pairs)]
where the time goes in v4:
time: 38.5 us; the launch traced here: 38.2 us
  starting transfers between devices  15.4 us (40%)
  waiting for transfers between devices  15 us (39%)
  Pallas kernels  4.63 us (12%)
  local copies, waits for them, and re-layouts  2.33 us (6%)
  other arithmetic  0.71 us (2%)
    ppermute x6, waiting for transfers between devices, exchange(): lax.ppermute(x, axes, pairs)  8.03 us
    ppermute x6, starting transfers between devices, exchange(): lax.ppermute(x, axes, pairs)  8.01 us
    all_to_all x1, starting transfers between devices, per_device(): lax.all_to_all(repeated, ('outer', 'inner'), split_axis=0, concat_axis=0,...  7.25 us
    all_to_all x1, waiting for transfers between devices, per_device(): lax.all_to_all(repeated, ('outer', 'inner'), split_axis=0, concat_axis=0,...  6.2 us
    pallas_call x7, Pallas kernels, call(): pl.pallas_call(kernel, out_shape=out_shape, in_specs=in_specs, out_specs=...  4.63 us
    reshape x1, local copies, waits for them, and re-layouts, per_device(): tiles.reshape(held * ROWS_OF_TILE, LANES)  1.56 us
    ppermute x1, waiting for transfers between devices, per_device(): other = lax.ppermute(partial, 'core', swap)  0.8 us
    unnamed x6, local copies, waits for them, and re-layouts  0.77 us
  transfers between devices with their start and end apart: 9, of which 7 were waited for; matrix products, arithmetic and copies ran while one was open for 6% of the time, Pallas kernels for 3%

profile of v4, /device:TPU:0, one launch (start us, length us, event | category | flops | bytes accessed | tf_op | source)
XLA Modules:
  0.0 38.2 jit_solution(7951993006865039979)
XLA Ops:
  0.0 0.0 copy-start.1
  0.0 0.8 %copy-done.1 = bf16[1,4,4096]{2,1,0:T(4,128)(2,1)S(1)} copy-done((bf16[1,4,4096]{2,1,0:T(4,128)(2,1)S(1)}, bf16[1,4,4096]{2,1,0:T(4,128)(2,1)}, u32[]{:S(2)}) %copy-start.1) | copy-done | bytes 32792
  0.8 0.8 %shard_map.64 = bf16[8,128,128]{2,1,0:T(8,128)(2,1)} custom-call(bf16[1,4,4096]{2,1,0:T(4,128)(2,1)S(1)} %copy-done.1), custom_call_target="tpu_custom_call" | custom-call | tf_op jit(solution)/shard_map/pallas_call | solution.py:24
  1.5 7.3 %all-to-all-start = ((bf16[8,128,128]{2,1,0:T(8,128)(2,1)}), bf16[8,128,128]{2,1,0:T(8,128)(2,1)S(1)}, u32[]{:S(2)}, u32[]{:S(2)}) async-start(bf16[8,128,128]{2,1,0:T(8,128)(2,1)} %shard_map.64), calls=%async_computation | async-start | bytes 524288 | tf_op jit(solution)/shard_map/all_to_all | solution.py:190
  8.8 0.7 %compare_select_fusion.9 = (s32[32]{0:T(128)S(1)}, s32[32]{0:T(128)S(1)}, s32[32]{0:T(128)S(1)}) fusion(s32[]{:T(128)S(6)} %axis_index.42, s32[32]{0:T(128)} %param.9, s32[]{:T(128)S(6)} %axis_index.51, s32[]{:T(128)S(6)} %axis_index.48, s32[]{:T(128)S(6)} %axis_index.45, s32[32,1]{0,1:T(1,128)} %param.8), kind=kLoop, calls=%fused_computation.15 | loop fusion | flops 2176 | bytes 656 | tf_op jit(solution)/shard_map/jit(_where)/select_n | solution.py:208
  9.5 0.1 collective-permute-start
  9.6 1.6 %reshape.6.tile_ref = bf16[4096,128]{1,0:T(8,128)(2,1)S(1)} reshape(bf16[128,4096]{1,0:T(8,128)(2,1)} %param.6) | data formatting | bytes 2097152 | tf_op jit(solution)/shard_map/reshape | solution.py:196
  11.1 0.0 copy-start.2
  11.1 0.3 shard_map.65.tile_ref
  11.5 0.0 collective-permute-done.slot_ref
  11.5 6.2 %all-to-all-done = bf16[8,128,128]{2,1,0:T(8,128)(2,1)S(1)} async-done(((bf16[8,128,128]{2,1,0:T(8,128)(2,1)}), bf16[8,128,128]{2,1,0:T(8,128)(2,1)S(1)}, u32[]{:S(2)}, u32[]{:S(2)}) %all-to-all-start) | async-done | bytes 262176 | tf_op jit(solution)/shard_map/all_to_all | solution.py:190
  17.7 0.0 copy-done.2
  17.7 1.1 %shard_map.66.ref = bf16[1024,128]{1,0:T(8,128)(2,1)S(1)} custom-call(s32[128]{0:T(128)S(1)} %copy-done.2, bf16[1024,128]{1,0:T(8,128)(2,1)S(1)} %bitcast.15, bf16[2048,256]{1,0:T(8,128)(2,1)S(1)} %shard_map.65.tile_ref), custom_call_target="tpu_custom_call" | custom-call | tf_op jit(solution)/shard_map/pallas_call | solution.py:24
  18.8 0.1 collective-permute-start.1
  18.9 0.7 %shard_map.67.in_ref = f32[2080,128]{1,0:T(8,128)S(1)} custom-call(s32[32]{0:T(128)S(1)} %compare_select_fusion.10.slot_ref, bf16[1024,128]{1,0:T(8,128)(2,1)S(1)} %shard_map.66.ref), custom_call_target="tpu_custom_call" | custom-call | tf_op jit(solution)/shard_map/pallas_call | solution.py:24
  19.6 0.8 %collective-permute-done.1.ref = bf16[1024,128]{1,0:T(8,128)(2,1)S(1)} collective-permute-done((bf16[1024,128]{1,0:T(8,128)(2,1)S(1)}, bf16[1024,128]{1,0:T(8,128)(2,1)S(1)}, u32[]{:S(2)}, u32[]{:S(2)}) %collective-permute-start.1) | collective-permute-done | bytes 262176 | tf_op jit(solution)/shard_map/ppermute | solution.py:223
  20.4 0.7 %shard_map.68 = (bf16[512,128]{1,0:T(8,128)(2,1)S(1)}, bf16[512,128]{1,0:T(8,128)(2,1)S(1)}, bf16[512,128]{1,0:T(8,128)(2,1)S(1)}, f32[2080,128]{1,0:T(8,128)S(1)}) custom-call(s32[32]{0:T(128)S(1)} %collective-permute-done.slot_ref, bf16[1024,128]{1,0:T(8,128)(2,1)S(1)} %collective-permute-done.1.ref, ...), custom_call_target="tpu_custom_call", output_to_operand_aliasing={{3}: (2, {})} | custom-call | tf_op jit(solution)/shard_map/pallas_call | solution.py:24
  21.1 0.0 copy-start
  21.2 2.4 %collective-permute-start.2 = (bf16[512,128]{1,0:T(8,128)(2,1)S(1)}, bf16[512,128]{1,0:T(8,128)(2,1)S(1)}, u32[]{:S(2)}, u32[]{:S(2)}) collective-permute-start(bf16[512,128]{1,0:T(8,128)(2,1)S(1)} %get-tuple-element.22), channel_id=1, source_target_pairs={{0,6},{2,4},{4,2},{6,0},{1,7},{3,5},{5,3},{7,1},{8,14},{10,12},{12... | collective-permute-start | bytes 393224 | tf_op jit(solution)/shard_map/ppermute | solution.py:168
  23.6 0.6 %collective-permute-start.3 = (bf16[512,128]{1,0:T(8,128)(2,1)S(1)}, bf16[512,128]{1,0:T(8,128)(2,1)S(1)}, u32[]{:S(2)}, u32[]{:S(2)}) collective-permute-start(bf16[512,128]{1,0:T(8,128)(2,1)S(1)} %get-tuple-element.23), channel_id=1, source_target_pairs={{0,4},{2,6},{4,0},{6,2},{1,5},{3,7},{5,1},{7,3},{8,12},{10,14},{12... | collective-permute-start | bytes 393224 | tf_op jit(solution)/shard_map/ppermute | solution.py:168
  24.2 0.5 %collective-permute-start.4 = (bf16[512,128]{1,0:T(8,128)(2,1)S(1)}, bf16[512,128]{1,0:T(8,128)(2,1)S(1)}, u32[]{:S(2)}, u32[]{:S(2)}) collective-permute-start(bf16[512,128]{1,0:T(8,128)(2,1)S(1)} %get-tuple-element.24), channel_id=1, source_target_pairs={{0,2},{2,0},{4,6},{6,4},{1,3},{3,1},{5,7},{7,5},{8,10},{10,8},{12,... | collective-permute-start | bytes 393224 | tf_op jit(solution)/shard_map/ppermute | solution.py:168
  24.7 3.8 %collective-permute-done.2.refs_0_ = bf16[512,128]{1,0:T(8,128)(2,1)S(1)} collective-permute-done((bf16[512,128]{1,0:T(8,128)(2,1)S(1)}, bf16[512,128]{1,0:T(8,128)(2,1)S(1)}, u32[]{:S(2)}, u32[]{:S(2)}) %collective-permute-start.2) | collective-permute-done | bytes 131104 | tf_op jit(solution)/shard_map/ppermute | solution.py:168
  28.5 2.0 %collective-permute-done.3.refs_1_ = bf16[512,128]{1,0:T(8,128)(2,1)S(1)} collective-permute-done((bf16[512,128]{1,0:T(8,128)(2,1)S(1)}, bf16[512,128]{1,0:T(8,128)(2,1)S(1)}, u32[]{:S(2)}, u32[]{:S(2)}) %collective-permute-start.3) | collective-permute-done | bytes 131104 | tf_op jit(solution)/shard_map/ppermute | solution.py:168
  30.5 0.0 collective-permute-done.4.refs_2_
  30.5 0.1 shard_map.69
  30.6 1.2 %collective-permute-start.5 = (bf16[128,128]{1,0:T(8,128)(2,1)S(1)}, bf16[128,128]{1,0:T(8,128)(2,1)S(1)}, u32[]{:S(2)}, u32[]{:S(2)}) collective-permute-start(bf16[128,128]{1,0:T(8,128)(2,1)S(1)} %get-tuple-element.25), channel_id=1, source_target_pairs={{0,24},{8,16},{16,8},{24,0},{1,25},{9,17},{17,9},{25,1},{2,26},{10... | collective-permute-start | bytes 98312 | tf_op jit(solution)/shard_map/ppermute | solution.py:168
  31.8 1.4 %collective-permute-start.6 = (bf16[128,128]{1,0:T(8,128)(2,1)S(1)}, bf16[128,128]{1,0:T(8,128)(2,1)S(1)}, u32[]{:S(2)}, u32[]{:S(2)}) collective-permute-start(bf16[128,128]{1,0:T(8,128)(2,1)S(1)} %get-tuple-element.26), channel_id=1, source_target_pairs={{0,16},{8,24},{16,0},{24,8},{1,17},{9,25},{17,1},{25,9},{2,18},{10... | collective-permute-start | bytes 98312 | tf_op jit(solution)/shard_map/ppermute | solution.py:168
  33.2 1.9 %collective-permute-start.7 = (bf16[128,128]{1,0:T(8,128)(2,1)S(1)}, bf16[128,128]{1,0:T(8,128)(2,1)S(1)}, u32[]{:S(2)}, u32[]{:S(2)}) collective-permute-start(bf16[128,128]{1,0:T(8,128)(2,1)S(1)} %get-tuple-element.27), channel_id=1, source_target_pairs={{0,8},{8,0},{16,24},{24,16},{1,9},{9,1},{17,25},{25,17},{2,10},{10... | collective-permute-start | bytes 98312 | tf_op jit(solution)/shard_map/ppermute | solution.py:168
  35.0 1.6 %collective-permute-done.5.refs_0_ = bf16[128,128]{1,0:T(8,128)(2,1)S(1)} collective-permute-done((bf16[128,128]{1,0:T(8,128)(2,1)S(1)}, bf16[128,128]{1,0:T(8,128)(2,1)S(1)}, u32[]{:S(2)}, u32[]{:S(2)}) %collective-permute-start.5) | collective-permute-done | bytes 32800 | tf_op jit(solution)/shard_map/ppermute | solution.py:168
  36.7 0.6 %collective-permute-done.6.refs_1_ = bf16[128,128]{1,0:T(8,128)(2,1)S(1)} collective-permute-done((bf16[128,128]{1,0:T(8,128)(2,1)S(1)}, bf16[128,128]{1,0:T(8,128)(2,1)S(1)}, u32[]{:S(2)}, u32[]{:S(2)}) %collective-permute-start.6) | collective-permute-done | bytes 32800 | tf_op jit(solution)/shard_map/ppermute | solution.py:168
  37.2 0.1 collective-permute-done.7.refs_2_
  37.3 0.0 copy-done
  37.3 0.9 %shard_map.70 = f32[1,4,4096]{2,1,0:T(4,128)} custom-call(bf16[128,128]{1,0:T(8,128)(2,1)S(1)} %collective-permute-done.5.refs_0_, bf16[128,128]{1,0:T(8,128)(2,1)S(1)} %collective-permute-done.6.refs_1_, bf16[128,128]{1,0:T(8,128)(2,1)S(1)} %collective-permute-done.7.refs_2_, f32[128,128]{1,0:T(8,128)S(1)} %get-tuple-element.28.refs_3_, ...), custom_call_target="tpu_custom_call" | custom-call | tf_op jit(solution)/shard_map/pallas_call | solution.py:24
  (1 shorter events, 0.0 us)
Async XLA Ops:
  0.0 0.8 %copy-start.1 = (bf16[1,4,4096]{2,1,0:T(4,128)(2,1)S(1)}, bf16[1,4,4096]{2,1,0:T(4,128)(2,1)}, u32[]{:S(2)}) copy-start(bf16[1,4,4096]{2,1,0:T(4,128)(2,1)} %in_ref.1) | copy-start | bytes 98308
  1.5 16.2 %all-to-all-start = ((bf16[8,128,128]{2,1,0:T(8,128)(2,1)}), bf16[8,128,128]{2,1,0:T(8,128)(2,1)S(1)}, u32[]{:S(2)}, u32[]{:S(2)}) async-start(bf16[8,128,128]{2,1,0:T(8,128)(2,1)} %shard_map.64), calls=%async_computation | async-start | bytes 524288 | tf_op jit(solution)/shard_map/all_to_all | solution.py:190
  9.5 2.0 %collective-permute-start = (s32[32]{0:T(128)S(1)}, s32[32]{0:T(128)S(1)}, u32[]{:S(2)}, u32[]{:S(2)}) collective-permute-start(s32[32]{0:T(128)S(1)} %get-tuple-element.29), channel_id=1, source_target_pairs={{0,1},{1,0},{2,3},{3,2},{4,5},{5,4},{6,7},{7,6},{8,9},{9,8},{10,11... | collective-permute-start | bytes 392 | tf_op jit(solution)/shard_map/ppermute | solution.py:208
  11.1 6.6 %copy-start.2 = (s32[128]{0:T(128)S(1)}, s32[128]{0:T(128)}, u32[]{:S(2)}) copy-start(s32[128]{0:T(128)} %cd_ref.1) | copy-start | bytes 1540
  18.8 1.6 %collective-permute-start.1 = (bf16[1024,128]{1,0:T(8,128)(2,1)S(1)}, bf16[1024,128]{1,0:T(8,128)(2,1)S(1)}, u32[]{:S(2)}, u32[]{:S(2)}) collective-permute-start(bf16[1024,128]{1,0:T(8,128)(2,1)S(1)} %shard_map.66.ref), channel_id=1, source_target_pairs={{0,1},{1,0},{2,3},{3,2},{4,5},{5,4},{6,7},{7,6},{8,9},{9,8},{10,11... | collective-permute-start | bytes 786440 | tf_op jit(solution)/shard_map/ppermute | solution.py:223
  21.1 16.1 %copy-start = (f32[1,4,4096]{2,1,0:T(4,128)S(1)}, f32[1,4,4096]{2,1,0:T(4,128)}, u32[]{:S(2)}) copy-start(f32[1,4,4096]{2,1,0:T(4,128)} %refs_4_.1) | copy-start | bytes 196612
  21.2 7.3 %collective-permute-start.2 = (bf16[512,128]{1,0:T(8,128)(2,1)S(1)}, bf16[512,128]{1,0:T(8,128)(2,1)S(1)}, u32[]{:S(2)}, u32[]{:S(2)}) collective-permute-start(bf16[512,128]{1,0:T(8,128)(2,1)S(1)} %get-tuple-element.22), channel_id=1, source_target_pairs={{0,6},{2,4},{4,2},{6,0},{1,7},{3,5},{5,3},{7,1},{8,14},{10,12},{12... | collective-permute-start | bytes 393224 | tf_op jit(solution)/shard_map/ppermute | solution.py:168
  23.6 6.9 %collective-permute-start.3 = (bf16[512,128]{1,0:T(8,128)(2,1)S(1)}, bf16[512,128]{1,0:T(8,128)(2,1)S(1)}, u32[]{:S(2)}, u32[]{:S(2)}) collective-permute-start(bf16[512,128]{1,0:T(8,128)(2,1)S(1)} %get-tuple-element.23), channel_id=1, source_target_pairs={{0,4},{2,6},{4,0},{6,2},{1,5},{3,7},{5,1},{7,3},{8,12},{10,14},{12... | collective-permute-start | bytes 393224 | tf_op jit(solution)/shard_map/ppermute | solution.py:168
  24.2 6.3 %collective-permute-start.4 = (bf16[512,128]{1,0:T(8,128)(2,1)S(1)}, bf16[512,128]{1,0:T(8,128)(2,1)S(1)}, u32[]{:S(2)}, u32[]{:S(2)}) collective-permute-start(bf16[512,128]{1,0:T(8,128)(2,1)S(1)} %get-tuple-element.24), channel_id=1, source_target_pairs={{0,2},{2,0},{4,6},{6,4},{1,3},{3,1},{5,7},{7,5},{8,10},{10,8},{12,... | collective-permute-start | bytes 393224 | tf_op jit(solution)/shard_map/ppermute | solution.py:168
  30.6 6.1 %collective-permute-start.5 = (bf16[128,128]{1,0:T(8,128)(2,1)S(1)}, bf16[128,128]{1,0:T(8,128)(2,1)S(1)}, u32[]{:S(2)}, u32[]{:S(2)}) collective-permute-start(bf16[128,128]{1,0:T(8,128)(2,1)S(1)} %get-tuple-element.25), channel_id=1, source_target_pairs={{0,24},{8,16},{16,8},{24,0},{1,25},{9,17},{17,9},{25,1},{2,26},{10... | collective-permute-start | bytes 98312 | tf_op jit(solution)/shard_map/ppermute | solution.py:168
  31.8 5.4 %collective-permute-start.6 = (bf16[128,128]{1,0:T(8,128)(2,1)S(1)}, bf16[128,128]{1,0:T(8,128)(2,1)S(1)}, u32[]{:S(2)}, u32[]{:S(2)}) collective-permute-start(bf16[128,128]{1,0:T(8,128)(2,1)S(1)} %get-tuple-element.26), channel_id=1, source_target_pairs={{0,16},{8,24},{16,0},{24,8},{1,17},{9,25},{17,1},{25,9},{2,18},{10... | collective-permute-start | bytes 98312 | tf_op jit(solution)/shard_map/ppermute | solution.py:168
  33.2 4.1 %collective-permute-start.7 = (bf16[128,128]{1,0:T(8,128)(2,1)S(1)}, bf16[128,128]{1,0:T(8,128)(2,1)S(1)}, u32[]{:S(2)}, u32[]{:S(2)}) collective-permute-start(bf16[128,128]{1,0:T(8,128)(2,1)S(1)} %get-tuple-element.27), channel_id=1, source_target_pairs={{0,8},{8,0},{16,24},{24,16},{1,9},{9,1},{17,25},{25,17},{2,10},{10... | collective-permute-start | bytes 98312 | tf_op jit(solution)/shard_map/ppermute | solution.py:168

commit v5 on v4

--- a/solution.py
+++ b/solution.py
@@ -36,15 +36,35 @@
     return pl.ds(pl.multiple_of(first, ROWS_OF_TILE), count)
 
 
-def repeat_kernel(in_ref, out_ref, row_ref):
+def offset(to, start, size):
+    return to ^ start if size & (size - 1) == 0 else (to - start) % size
+
+
+def source(by, start, size):
+    return start ^ by if size & (size - 1) == 0 else (start - by) % size
+
+
+def as_rows(in_ref, row_ref):
     held = in_ref.shape[1]
     for j in range(ROWS_OF_TILE):
         row_ref[pl.ds(j, held, stride=ROWS_OF_TILE), :] = in_ref[
             0, :, pl.ds(j * LANES, LANES)
         ].astype(jnp.float32)
-    rows = row_ref[...].astype(jnp.bfloat16)
-    for receiver in range(out_ref.shape[0]):
-        out_ref[receiver] = rows
+    return row_ref[...].astype(jnp.bfloat16)
+
+
+def layout_kernel(in_ref, out_ref, row_ref):
+    out_ref[...] = as_rows(in_ref, row_ref)
+
+
+def near_kernel(own_ref, *refs):
+    in_refs, (out_ref, row_ref) = refs[:-2], refs[-2:]
+    size = own_ref.shape[0]
+    me = lax.axis_index("inner")
+    out_ref[tile_rows(me * size, size), :] = own_ref[...]
+    for by, in_ref in enumerate(in_refs):
+        at = tile_rows(source(by + 1, me, len(in_refs) + 1) * size, size)
+        out_ref[at, :] = as_rows(in_ref, row_ref)
 
 
 def halves_swapped(x):
@@ -74,8 +94,13 @@
                 out_ref[at, pl.ds(t * SPAN, LANES)] = halves[h]
 
 
-def partial_kernel(cd_ref, amp_ref, tile_ref, out_ref):
+def partial_kernel(cd_ref, tile_ref, *refs):
+    in_refs, (out_ref, amp_ref) = refs[:-2], refs[-2:]
     low = low_lanes()
+    me = lax.axis_index("outer")
+    size = in_refs[0].shape[0]
+    for by, in_ref in enumerate(reversed(in_refs)):
+        amp_ref[tile_rows(source(by, me, len(in_refs)) * size, size), :] = in_ref[...]
     for q in range(out_ref.shape[0] // ROWS_OF_TILE):
         amps = []
         for t in range(0, PER_PART, 2):
@@ -148,10 +173,6 @@
         out_ref[0, :, at] = residual_ref[0, :, at] + sum_ref[pl.ds(i, tiles, stride=ROWS_OF_TILE), :]
 
 
-def offset(to, start, size):
-    return to ^ start if size & (size - 1) == 0 else (to - start) % size
-
-
 def permutes(sizes):
     places = list(itertools.product(*map(range, sizes)))
     number = {place: i for i, place in enumerate(places)}
@@ -180,14 +201,24 @@
     by_permutes = outer <= MOST_PERMUTED
     swap = [(i, (i + 1) % cores) for i in range(cores)]
 
-    repeated = call(
-        repeat_kernel,
-        shape((rows, own_cd * ROWS_OF_TILE, LANES), bf16),
-        [VMEM],
-        amplitudes,
-        scratch=[pltpu.VMEM((own_cd * ROWS_OF_TILE, LANES), f32)],
-    )
-    gathered = lax.all_to_all(repeated, ("outer", "inner"), split_axis=0, concat_axis=0, tiled=True)
+    others = exchange([amplitudes] * (inner - 1), ("inner",), (inner,))[::-1]
+    shard_rows = own_cd * ROWS_OF_TILE
+    row_scratch = [pltpu.VMEM((shard_rows, LANES), f32)]
+    own = call(layout_kernel, shape((shard_rows, LANES), bf16), [VMEM], amplitudes, scratch=row_scratch)
+    near = call(
+        near_kernel,
+        shape((inner * shard_rows, LANES), bf16),
+        [VMEM] * inner,
+        own,
+        *others,
+        scratch=row_scratch,
+    )
+    if by_permutes:
+        gathered = exchange([near] * (outer - 1), ("outer",), (outer,))[::-1]
+    else:
+        repeated = jnp.broadcast_to(near, (outer,) + near.shape)
+        gathered = lax.all_to_all(repeated, "outer", split_axis=0, concat_axis=0, tiled=True)
+        gathered = [gathered.reshape(rows * shard_rows, LANES)]
 
     paired = call(
         pair_kernel,
@@ -212,13 +243,15 @@
         (gathered, paired, own_slot, other_slot)
     )
 
+    sources = gathered[::-1] + [near] if by_permutes else gathered
     partial = call(
         partial_kernel,
         shape((parts * ROWS_OF_TILE, LANES), bf16),
-        [SMEM, VMEM, VMEM],
+        [SMEM] + [VMEM] * (1 + len(sources)),
         cd_tile,
-        gathered.reshape(rows * own_cd * ROWS_OF_TILE, LANES),
         paired,
+        *sources,
+        scratch=[pltpu.VMEM((rows * shard_rows, LANES), bf16)],
     )
     other = lax.ppermute(partial, "core", swap)
     summed = shape(((slots + 1) * ROWS_OF_TILE, LANES), f32)

time: 38.5 us -> 36.2 us (0.940)
  waiting for transfers between devices: 15 us -> 12.9 us
  Pallas kernels: 4.63 us -> 4.06 us
  starting transfers between devices: 15.4 us -> 15.9 us
    ppermute x6 -> x10, starting transfers between devices: 8.01 us -> 15.8 us  [exchange(): lax.ppermute(x, axes, pairs)]
    all_to_all x1 -> x0, starting transfers between devices: 7.25 us -> none  [per_device(): lax.all_to_all(repeated, ('outer', 'inner'), split_axis=0, concat_axis=0,...]
    all_to_all x1 -> x0, waiting for transfers between devices: 6.2 us -> none  [per_device(): lax.all_to_all(repeated, ('outer', 'inner'), split_axis=0, concat_axis=0,...]
    ppermute x6 -> x10, waiting for transfers between devices: 8.03 us -> 12.1 us  [exchange(): lax.ppermute(x, axes, pairs)]
    pallas_call x7 -> x8, Pallas kernels: 4.63 us -> 4.06 us  [call(): pl.pallas_call(kernel, out_shape=out_shape, in_specs=in_specs, out_specs=...]
  transfers between devices with their start and end apart: 9 -> 12, of which waited for: 7 -> 9; matrix products, arithmetic and copies ran while one was open for 6% -> 6% of each run, Pallas kernels for 3% -> 3%
where the time goes in v5:
time: 36.2 us; the launch traced here: 36 us
  starting transfers between devices  15.9 us (44%)
  waiting for transfers between devices  12.9 us (36%)
  Pallas kernels  4.06 us (11%)
  local copies, waits for them, and re-layouts  2.32 us (6%)
  other arithmetic  0.71 us (2%)
    ppermute x10, starting transfers between devices, exchange(): lax.ppermute(x, axes, pairs)  15.8 us
    ppermute x10, waiting for transfers between devices, exchange(): lax.ppermute(x, axes, pairs)  12.1 us
    pallas_call x8, Pallas kernels, call(): pl.pallas_call(kernel, out_shape=out_shape, in_specs=in_specs, out_specs=...  4.06 us
    reshape x1, local copies, waits for them, and re-layouts, per_device(): tiles.reshape(held * ROWS_OF_TILE, LANES)  1.55 us
    ppermute x1, waiting for transfers between devices, per_device(): other = lax.ppermute(partial, 'core', swap)  0.77 us
    unnamed x6, local copies, waits for them, and re-layouts  0.77 us
  transfers between devices with their start and end apart: 12, of which 9 were waited for; matrix products, arithmetic and copies ran while one was open for 6% of the time, Pallas kernels for 3%

profile of v5, /device:TPU:0, one launch (start us, length us, event | category | flops | bytes accessed | tf_op | source)
XLA Modules:
  0.0 36.0 jit_solution(17094293736143934114)
XLA Ops:
  0.0 2.9 %collective-permute-start = (bf16[1,4,4096]{2,1,0:T(4,128)(2,1)}, bf16[1,4,4096]{2,1,0:T(4,128)(2,1)S(1)}, u32[]{:S(2)}, u32[]{:S(2)}) collective-permute-start(bf16[1,4,4096]{2,1,0:T(4,128)(2,1)} %in_ref.1), channel_id=1, source_target_pairs={{0,4},{4,0},{1,5},{5,1},{2,6},{6,2},{3,7},{7,3},{8,12},{12,8},{9,1... | collective-permute-start | bytes 98312 | tf_op jit(solution)/shard_map/ppermute | solution.py:189
  2.9 0.7 %compare_select_fusion.9 = (s32[32]{0:T(128)S(1)}, s32[32]{0:T(128)S(1)}, s32[32]{0:T(128)S(1)}) fusion(s32[]{:T(128)S(6)} %axis_index.42, s32[32]{0:T(128)} %param.9, s32[]{:T(128)S(6)} %axis_index.51, s32[]{:T(128)S(6)} %axis_index.48, s32[]{:T(128)S(6)} %axis_index.45, s32[32,1]{0,1:T(1,128)} %param.8), kind=kLoop, calls=%fused_computation.15 | loop fusion | flops 2176 | bytes 656 | tf_op jit(solution)/shard_map/jit(_where)/select_n | solution.py:239
  3.6 0.1 collective-permute-start.4
  3.7 0.0 copy-start.1
  3.7 0.7 %copy-done.1 = bf16[1,4,4096]{2,1,0:T(4,128)(2,1)S(1)} copy-done((bf16[1,4,4096]{2,1,0:T(4,128)(2,1)S(1)}, bf16[1,4,4096]{2,1,0:T(4,128)(2,1)}, u32[]{:S(2)}) %copy-start.1) | copy-done | bytes 32792
  4.5 0.5 %collective-permute-done.refs_0_ = bf16[1,4,4096]{2,1,0:T(4,128)(2,1)S(1)} collective-permute-done((bf16[1,4,4096]{2,1,0:T(4,128)(2,1)}, bf16[1,4,4096]{2,1,0:T(4,128)(2,1)S(1)}, u32[]{:S(2)}, u32[]{:S(2)}) %collective-permute-start) | collective-permute-done | bytes 32800 | tf_op jit(solution)/shard_map/ppermute | solution.py:189
  5.1 4.2 %collective-permute-start.3 = (bf16[256,128]{1,0:T(8,128)(2,1)S(1)}, bf16[256,128]{1,0:T(8,128)(2,1)S(1)}, u32[]{:S(2)}, u32[]{:S(2)}) collective-permute-start(bf16[256,128]{1,0:T(8,128)(2,1)S(1)} %shard_map.65.refs_3_), channel_id=1, source_target_pairs={{0,24},{8,16},{16,8},{24,0},{1,25},{9,17},{17,9},{25,1},{2,26},{10... | collective-permute-start | bytes 196616 | tf_op jit(solution)/shard_map/ppermute | solution.py:189
  9.3 0.0 collective-permute-start.2
  9.3 0.6 %collective-permute-start.1 = (bf16[256,128]{1,0:T(8,128)(2,1)S(1)}, bf16[256,128]{1,0:T(8,128)(2,1)S(1)}, u32[]{:S(2)}, u32[]{:S(2)}) collective-permute-start(bf16[256,128]{1,0:T(8,128)(2,1)S(1)} %shard_map.65.refs_3_), channel_id=1, source_target_pairs={{0,8},{8,0},{16,24},{24,16},{1,9},{9,1},{17,25},{25,17},{2,10},{10... | collective-permute-start | bytes 196616 | tf_op jit(solution)/shard_map/ppermute | solution.py:189
  9.9 1.6 %reshape.3.tile_ref = bf16[4096,128]{1,0:T(8,128)(2,1)S(1)} reshape(bf16[128,4096]{1,0:T(8,128)(2,1)} %param.6) | data formatting | bytes 2097152 | tf_op jit(solution)/shard_map/reshape | solution.py:227
  11.5 0.0 copy-start.2
  11.5 0.3 shard_map.66.tile_ref
  11.9 0.0 collective-permute-done.4.slot_ref
  11.9 0.4 collective-permute-done.3.refs_0_
  12.2 2.4 %collective-permute-done.2.refs_1_ = bf16[256,128]{1,0:T(8,128)(2,1)S(1)} collective-permute-done((bf16[256,128]{1,0:T(8,128)(2,1)S(1)}, bf16[256,128]{1,0:T(8,128)(2,1)S(1)}, u32[]{:S(2)}, u32[]{:S(2)}) %collective-permute-start.2) | collective-permute-done | bytes 65568 | tf_op jit(solution)/shard_map/ppermute | solution.py:189
  14.6 0.1 collective-permute-done.1.refs_2_
  14.6 0.0 copy-done.2
  14.6 1.1 %shard_map.67.ref = bf16[1024,128]{1,0:T(8,128)(2,1)S(1)} custom-call(s32[128]{0:T(128)S(1)} %copy-done.2, bf16[2048,256]{1,0:T(8,128)(2,1)S(1)} %shard_map.66.tile_ref, bf16[256,128]{1,0:T(8,128)(2,1)S(1)} %collective-permute-done.3.refs_0_, bf16[256,128]{1,0:T(8,128)(2,1)S(1)} %collective-permute-done.2.refs_1_, ...), custom_call_target="tpu_custom_call" | custom-call | tf_op jit(solution)/shard_map/pallas_call | solution.py:24
  15.8 0.1 collective-permute-start.5
  15.9 0.8 %shard_map.68.in_ref = f32[2080,128]{1,0:T(8,128)S(1)} custom-call(s32[32]{0:T(128)S(1)} %compare_select_fusion.10.slot_ref, bf16[1024,128]{1,0:T(8,128)(2,1)S(1)} %shard_map.67.ref), custom_call_target="tpu_custom_call" | custom-call | tf_op jit(solution)/shard_map/pallas_call | solution.py:24
  16.6 0.8 %collective-permute-done.5.ref = bf16[1024,128]{1,0:T(8,128)(2,1)S(1)} collective-permute-done((bf16[1024,128]{1,0:T(8,128)(2,1)S(1)}, bf16[1024,128]{1,0:T(8,128)(2,1)S(1)}, u32[]{:S(2)}, u32[]{:S(2)}) %collective-permute-start.5) | collective-permute-done | bytes 262176 | tf_op jit(solution)/shard_map/ppermute | solution.py:256
  17.4 0.8 %shard_map.69 = (bf16[512,128]{1,0:T(8,128)(2,1)S(1)}, bf16[512,128]{1,0:T(8,128)(2,1)S(1)}, bf16[512,128]{1,0:T(8,128)(2,1)S(1)}, f32[2080,128]{1,0:T(8,128)S(1)}) custom-call(s32[32]{0:T(128)S(1)} %collective-permute-done.4.slot_ref, bf16[1024,128]{1,0:T(8,128)(2,1)S(1)} %collective-permute-done.5.ref, ...), custom_call_target="tpu_custom_call", output_to_operand_aliasing={{3}: (2, {})} | custom-call | tf_op jit(solution)/shard_map/pallas_call | solution.py:24
  18.1 0.0 copy-start
  18.2 2.3 %collective-permute-start.6 = (bf16[512,128]{1,0:T(8,128)(2,1)S(1)}, bf16[512,128]{1,0:T(8,128)(2,1)S(1)}, u32[]{:S(2)}, u32[]{:S(2)}) collective-permute-start(bf16[512,128]{1,0:T(8,128)(2,1)S(1)} %get-tuple-element.26), channel_id=1, source_target_pairs={{0,6},{2,4},{4,2},{6,0},{1,7},{3,5},{5,3},{7,1},{8,14},{10,12},{12... | collective-permute-start | bytes 393224 | tf_op jit(solution)/shard_map/ppermute | solution.py:189
  20.5 0.7 %collective-permute-start.7 = (bf16[512,128]{1,0:T(8,128)(2,1)S(1)}, bf16[512,128]{1,0:T(8,128)(2,1)S(1)}, u32[]{:S(2)}, u32[]{:S(2)}) collective-permute-start(bf16[512,128]{1,0:T(8,128)(2,1)S(1)} %get-tuple-element.27), channel_id=1, source_target_pairs={{0,4},{2,6},{4,0},{6,2},{1,5},{3,7},{5,1},{7,3},{8,12},{10,14},{12... | collective-permute-start | bytes 393224 | tf_op jit(solution)/shard_map/ppermute | solution.py:189
  21.2 0.5 %collective-permute-start.8 = (bf16[512,128]{1,0:T(8,128)(2,1)S(1)}, bf16[512,128]{1,0:T(8,128)(2,1)S(1)}, u32[]{:S(2)}, u32[]{:S(2)}) collective-permute-start(bf16[512,128]{1,0:T(8,128)(2,1)S(1)} %get-tuple-element.28), channel_id=1, source_target_pairs={{0,2},{2,0},{4,6},{6,4},{1,3},{3,1},{5,7},{7,5},{8,10},{10,8},{12,... | collective-permute-start | bytes 393224 | tf_op jit(solution)/shard_map/ppermute | solution.py:189
  21.7 3.8 %collective-permute-done.6.refs_0_ = bf16[512,128]{1,0:T(8,128)(2,1)S(1)} collective-permute-done((bf16[512,128]{1,0:T(8,128)(2,1)S(1)}, bf16[512,128]{1,0:T(8,128)(2,1)S(1)}, u32[]{:S(2)}, u32[]{:S(2)}) %collective-permute-start.6) | collective-permute-done | bytes 131104 | tf_op jit(solution)/shard_map/ppermute | solution.py:189
  25.5 2.0 %collective-permute-done.7.refs_1_ = bf16[512,128]{1,0:T(8,128)(2,1)S(1)} collective-permute-done((bf16[512,128]{1,0:T(8,128)(2,1)S(1)}, bf16[512,128]{1,0:T(8,128)(2,1)S(1)}, u32[]{:S(2)}, u32[]{:S(2)}) %collective-permute-start.7) | collective-permute-done | bytes 131104 | tf_op jit(solution)/shard_map/ppermute | solution.py:189
  27.5 0.0 collective-permute-done.8.refs_2_
  27.5 0.1 shard_map.70
  27.6 2.7 %collective-permute-start.9 = (bf16[128,128]{1,0:T(8,128)(2,1)S(1)}, bf16[128,128]{1,0:T(8,128)(2,1)S(1)}, u32[]{:S(2)}, u32[]{:S(2)}) collective-permute-start(bf16[128,128]{1,0:T(8,128)(2,1)S(1)} %get-tuple-element.29), channel_id=1, source_target_pairs={{0,24},{8,16},{16,8},{24,0},{1,25},{9,17},{17,9},{25,1},{2,26},{10... | collective-permute-start | bytes 98312 | tf_op jit(solution)/shard_map/ppermute | solution.py:189
  30.3 0.0 collective-permute-start.10
  30.3 1.7 %collective-permute-start.11 = (bf16[128,128]{1,0:T(8,128)(2,1)S(1)}, bf16[128,128]{1,0:T(8,128)(2,1)S(1)}, u32[]{:S(2)}, u32[]{:S(2)}) collective-permute-start(bf16[128,128]{1,0:T(8,128)(2,1)S(1)} %get-tuple-element.31), channel_id=1, source_target_pairs={{0,8},{8,0},{16,24},{24,16},{1,9},{9,1},{17,25},{25,17},{2,10},{10... | collective-permute-start | bytes 98312 | tf_op jit(solution)/shard_map/ppermute | solution.py:189
  32.0 1.3 %collective-permute-done.9.refs_0_ = bf16[128,128]{1,0:T(8,128)(2,1)S(1)} collective-permute-done((bf16[128,128]{1,0:T(8,128)(2,1)S(1)}, bf16[128,128]{1,0:T(8,128)(2,1)S(1)}, u32[]{:S(2)}, u32[]{:S(2)}) %collective-permute-start.9) | collective-permute-done | bytes 32800 | tf_op jit(solution)/shard_map/ppermute | solution.py:189
  33.3 1.7 %collective-permute-done.10.refs_1_ = bf16[128,128]{1,0:T(8,128)(2,1)S(1)} collective-permute-done((bf16[128,128]{1,0:T(8,128)(2,1)S(1)}, bf16[128,128]{1,0:T(8,128)(2,1)S(1)}, u32[]{:S(2)}, u32[]{:S(2)}) %collective-permute-start.10) | collective-permute-done | bytes 32800 | tf_op jit(solution)/shard_map/ppermute | solution.py:189
  35.1 0.0 collective-permute-done.11.refs_2_
  35.1 0.0 copy-done
  35.1 0.9 %shard_map.71 = f32[1,4,4096]{2,1,0:T(4,128)} custom-call(bf16[128,128]{1,0:T(8,128)(2,1)S(1)} %collective-permute-done.9.refs_0_, bf16[128,128]{1,0:T(8,128)(2,1)S(1)} %collective-permute-done.10.refs_1_, bf16[128,128]{1,0:T(8,128)(2,1)S(1)} %collective-permute-done.11.refs_2_, f32[128,128]{1,0:T(8,128)S(1)} %get-tuple-element.32.refs_3_, ...), custom_call_target="tpu_custom_call" | custom-call | tf_op jit(solution)/shard_map/pallas_call | solution.py:24
  (3 shorter events, 0.1 us)
Async XLA Ops:
  0.0 5.0 %collective-permute-start = (bf16[1,4,4096]{2,1,0:T(4,128)(2,1)}, bf16[1,4,4096]{2,1,0:T(4,128)(2,1)S(1)}, u32[]{:S(2)}, u32[]{:S(2)}) collective-permute-start(bf16[1,4,4096]{2,1,0:T(4,128)(2,1)} %in_ref.1), channel_id=1, source_target_pairs={{0,4},{4,0},{1,5},{5,1},{2,6},{6,2},{3,7},{7,3},{8,12},{12,8},{9,1... | collective-permute-start | bytes 98312 | tf_op jit(solution)/shard_map/ppermute | solution.py:189
  3.6 8.2 %collective-permute-start.4 = (s32[32]{0:T(128)S(1)}, s32[32]{0:T(128)S(1)}, u32[]{:S(2)}, u32[]{:S(2)}) collective-permute-start(s32[32]{0:T(128)S(1)} %get-tuple-element.33), channel_id=1, source_target_pairs={{0,1},{1,0},{2,3},{3,2},{4,5},{5,4},{6,7},{7,6},{8,9},{9,8},{10,11... | collective-permute-start | bytes 392 | tf_op jit(solution)/shard_map/ppermute | solution.py:239
  3.7 0.8 %copy-start.1 = (bf16[1,4,4096]{2,1,0:T(4,128)(2,1)S(1)}, bf16[1,4,4096]{2,1,0:T(4,128)(2,1)}, u32[]{:S(2)}) copy-start(bf16[1,4,4096]{2,1,0:T(4,128)(2,1)} %in_ref.1) | copy-start | bytes 98308
  5.1 7.1 %collective-permute-start.3 = (bf16[256,128]{1,0:T(8,128)(2,1)S(1)}, bf16[256,128]{1,0:T(8,128)(2,1)S(1)}, u32[]{:S(2)}, u32[]{:S(2)}) collective-permute-start(bf16[256,128]{1,0:T(8,128)(2,1)S(1)} %shard_map.65.refs_3_), channel_id=1, source_target_pairs={{0,24},{8,16},{16,8},{24,0},{1,25},{9,17},{17,9},{25,1},{2,26},{10... | collective-permute-start | bytes 196616 | tf_op jit(solution)/shard_map/ppermute | solution.py:189
  9.3 5.3 %collective-permute-start.2 = (bf16[256,128]{1,0:T(8,128)(2,1)S(1)}, bf16[256,128]{1,0:T(8,128)(2,1)S(1)}, u32[]{:S(2)}, u32[]{:S(2)}) collective-permute-start(bf16[256,128]{1,0:T(8,128)(2,1)S(1)} %shard_map.65.refs_3_), channel_id=1, source_target_pairs={{0,16},{8,24},{16,0},{24,8},{1,17},{9,25},{17,1},{25,9},{2,18},{10... | collective-permute-start | bytes 196616 | tf_op jit(solution)/shard_map/ppermute | solution.py:189
  9.3 5.3 %collective-permute-start.1 = (bf16[256,128]{1,0:T(8,128)(2,1)S(1)}, bf16[256,128]{1,0:T(8,128)(2,1)S(1)}, u32[]{:S(2)}, u32[]{:S(2)}) collective-permute-start(bf16[256,128]{1,0:T(8,128)(2,1)S(1)} %shard_map.65.refs_3_), channel_id=1, source_target_pairs={{0,8},{8,0},{16,24},{24,16},{1,9},{9,1},{17,25},{25,17},{2,10},{10... | collective-permute-start | bytes 196616 | tf_op jit(solution)/shard_map/ppermute | solution.py:189
  11.5 3.1 %copy-start.2 = (s32[128]{0:T(128)S(1)}, s32[128]{0:T(128)}, u32[]{:S(2)}) copy-start(s32[128]{0:T(128)} %cd_ref.1) | copy-start | bytes 1540
  15.8 1.6 %collective-permute-start.5 = (bf16[1024,128]{1,0:T(8,128)(2,1)S(1)}, bf16[1024,128]{1,0:T(8,128)(2,1)S(1)}, u32[]{:S(2)}, u32[]{:S(2)}) collective-permute-start(bf16[1024,128]{1,0:T(8,128)(2,1)S(1)} %shard_map.67.ref), channel_id=1, source_target_pairs={{0,1},{1,0},{2,3},{3,2},{4,5},{5,4},{6,7},{7,6},{8,9},{9,8},{10,11... | collective-permute-start | bytes 786440 | tf_op jit(solution)/shard_map/ppermute | solution.py:256
  18.1 16.9 %copy-start = (f32[1,4,4096]{2,1,0:T(4,128)S(1)}, f32[1,4,4096]{2,1,0:T(4,128)}, u32[]{:S(2)}) copy-start(f32[1,4,4096]{2,1,0:T(4,128)} %refs_4_.1) | copy-start | bytes 196612
  18.2 7.3 %collective-permute-start.6 = (bf16[512,128]{1,0:T(8,128)(2,1)S(1)}, bf16[512,128]{1,0:T(8,128)(2,1)S(1)}, u32[]{:S(2)}, u32[]{:S(2)}) collective-permute-start(bf16[512,128]{1,0:T(8,128)(2,1)S(1)} %get-tuple-element.26), channel_id=1, source_target_pairs={{0,6},{2,4},{4,2},{6,0},{1,7},{3,5},{5,3},{7,1},{8,14},{10,12},{12... | collective-permute-start | bytes 393224 | tf_op jit(solution)/shard_map/ppermute | solution.py:189
  20.5 7.0 %collective-permute-start.7 = (bf16[512,128]{1,0:T(8,128)(2,1)S(1)}, bf16[512,128]{1,0:T(8,128)(2,1)S(1)}, u32[]{:S(2)}, u32[]{:S(2)}) collective-permute-start(bf16[512,128]{1,0:T(8,128)(2,1)S(1)} %get-tuple-element.27), channel_id=1, source_target_pairs={{0,4},{2,6},{4,0},{6,2},{1,5},{3,7},{5,1},{7,3},{8,12},{10,14},{12... | collective-permute-start | bytes 393224 | tf_op jit(solution)/shard_map/ppermute | solution.py:189
  21.2 6.3 %collective-permute-start.8 = (bf16[512,128]{1,0:T(8,128)(2,1)S(1)}, bf16[512,128]{1,0:T(8,128)(2,1)S(1)}, u32[]{:S(2)}, u32[]{:S(2)}) collective-permute-start(bf16[512,128]{1,0:T(8,128)(2,1)S(1)} %get-tuple-element.28), channel_id=1, source_target_pairs={{0,2},{2,0},{4,6},{6,4},{1,3},{3,1},{5,7},{7,5},{8,10},{10,8},{12,... | collective-permute-start | bytes 393224 | tf_op jit(solution)/shard_map/ppermute | solution.py:189
  27.6 5.8 %collective-permute-start.9 = (bf16[128,128]{1,0:T(8,128)(2,1)S(1)}, bf16[128,128]{1,0:T(8,128)(2,1)S(1)}, u32[]{:S(2)}, u32[]{:S(2)}) collective-permute-start(bf16[128,128]{1,0:T(8,128)(2,1)S(1)} %get-tuple-element.29), channel_id=1, source_target_pairs={{0,24},{8,16},{16,8},{24,0},{1,25},{9,17},{17,9},{25,1},{2,26},{10... | collective-permute-start | bytes 98312 | tf_op jit(solution)/shard_map/ppermute | solution.py:189
  30.3 4.8 %collective-permute-start.10 = (bf16[128,128]{1,0:T(8,128)(2,1)S(1)}, bf16[128,128]{1,0:T(8,128)(2,1)S(1)}, u32[]{:S(2)}, u32[]{:S(2)}) collective-permute-start(bf16[128,128]{1,0:T(8,128)(2,1)S(1)} %get-tuple-element.30), channel_id=1, source_target_pairs={{0,16},{8,24},{16,0},{24,8},{1,17},{9,25},{17,1},{25,9},{2,18},{10... | collective-permute-start | bytes 98312 | tf_op jit(solution)/shard_map/ppermute | solution.py:189
  30.3 4.8 %collective-permute-start.11 = (bf16[128,128]{1,0:T(8,128)(2,1)S(1)}, bf16[128,128]{1,0:T(8,128)(2,1)S(1)}, u32[]{:S(2)}, u32[]{:S(2)}) collective-permute-start(bf16[128,128]{1,0:T(8,128)(2,1)S(1)} %get-tuple-element.31), channel_id=1, source_target_pairs={{0,8},{8,0},{16,24},{24,16},{1,9},{9,1},{17,25},{25,17},{2,10},{10... | collective-permute-start | bytes 98312 | tf_op jit(solution)/shard_map/ppermute | solution.py:189

commit v6 on v5

--- a/solution.py
+++ b/solution.py
@@ -1,5 +1,6 @@
 import functools
 import itertools
+import math
 
 import jax
 import jax.numpy as jnp
@@ -16,7 +17,6 @@
 ROWS_OF_TILE = SPAN * SPAN // LANES
 MOST_PERMUTED = 4
 VMEM = pl.BlockSpec(memory_space=pltpu.VMEM)
-SMEM = pl.BlockSpec(memory_space=pltpu.SMEM)
 
 
 def call(kernel, out_shape, in_specs, *args, scratch=(), aliases=None):
@@ -53,8 +53,42 @@
     return row_ref[...].astype(jnp.bfloat16)
 
 
-def layout_kernel(in_ref, out_ref, row_ref):
+def down(row):
+    size = row.shape[1]
+    here = lax.broadcasted_iota(jnp.int32, (size, size), 0) == lax.broadcasted_iota(
+        jnp.int32, (size, size), 1
+    )
+    column = jnp.sum(jnp.where(here, row.astype(jnp.float32), 0.0), axis=1, keepdims=True)
+    return jnp.broadcast_to(column.astype(jnp.int32), (size, LANES))
+
+
+def layout_kernel(sizes, per_col, by_permutes, *refs):
+    sources, refs = refs[:4], refs[4:]
+    out_ref, first_cd_ref, own_slot_ref, other_slot_ref, row_ref, *local_refs, arrivals = refs
+    copies = [
+        pltpu.make_async_copy(source_ref, local_ref, arrivals.at[i])
+        for i, (source_ref, local_ref) in enumerate(zip(sources, local_refs))
+    ]
+    for copy in copies:
+        copy.start()
+    for copy in copies:
+        copy.wait()
+    in_ref, cd_ref, dest_ref, place_ref = local_refs
+    outer, inner, groups, cores = sizes
     out_ref[...] = as_rows(in_ref, row_ref)
+    first_cd_ref[...] = down(cd_ref[...] * ROWS_OF_TILE)
+    dest, place = dest_ref[...], place_ref[...]
+    col = place // per_col
+    to_inner = offset(dest % inner, lax.axis_index("inner"), inner)
+    to_group = offset(col // cores, lax.axis_index("groups"), groups)
+    to_outer = dest // inner
+    if by_permutes:
+        to_outer = offset(to_outer, lax.axis_index("outer"), outer)
+    slot = ((to_inner * groups + to_group) * outer + to_outer) * per_col + place % per_col
+    stays = col % cores == lax.axis_index("core")
+    unused = math.prod(sizes[:3]) * per_col
+    own_slot_ref[...] = down(jnp.where(stays, slot, unused) * ROWS_OF_TILE)
+    other_slot_ref[...] = down(jnp.where(stays, unused, slot) * ROWS_OF_TILE)
 
 
 def near_kernel(own_ref, *refs):
@@ -83,15 +117,20 @@
 
 def pair_kernel(tile_ref, out_ref):
     low = low_lanes()
+    to = lax.broadcasted_iota(jnp.int32, (SPAN, SPAN), 0)
+    row = lax.broadcasted_iota(jnp.int32, (SPAN, SPAN), 1)
+    order = (row == to % 2 * ROWS_OF_TILE + to // 2).astype(jnp.bfloat16)
     for q in range(out_ref.shape[0] // SPAN):
+        sides = []
         for t in range(0, PER_PART, 2):
             k = q * PER_PART + t
             halves = pair(
                 low, *[tile_ref[pl.ds((k + i) * ROWS_OF_TILE, ROWS_OF_TILE), :] for i in (0, 1)]
             )
-            for h in (0, 1):
-                at = pl.ds(q * SPAN + h * ROWS_OF_TILE, ROWS_OF_TILE)
-                out_ref[at, pl.ds(t * SPAN, LANES)] = halves[h]
+            sides.append(jnp.concatenate(halves, axis=0))
+        both = jnp.concatenate(sides, axis=1)
+        ordered = jnp.dot(order, both, preferred_element_type=jnp.float32)
+        out_ref[pl.ds(q * SPAN, SPAN), :] = ordered.astype(jnp.bfloat16)
 
 
 def partial_kernel(cd_ref, tile_ref, *refs):
@@ -106,7 +145,7 @@
         for t in range(0, PER_PART, 2):
             k = q * PER_PART + t
             amps.append(
-                pair(low, *[amp_ref[tile_rows(cd_ref[k + i] * ROWS_OF_TILE), :] for i in (0, 1)])
+                pair(low, *[amp_ref[tile_rows(cd_ref[k + i, 0]), :] for i in (0, 1)])
             )
         left = jnp.concatenate([jnp.concatenate([a[h] for a in amps], axis=1) for h in (0, 1)], axis=0)
         value = lax.dot_general(
@@ -121,7 +160,7 @@
 
 def add_tiles(slot_ref, ref, sum_ref):
     for q in range(ref.shape[0] // ROWS_OF_TILE):
-        at = tile_rows(slot_ref[q] * ROWS_OF_TILE)
+        at = tile_rows(slot_ref[q, 0])
         sum_ref[at, :] += ref[pl.ds(q * ROWS_OF_TILE, ROWS_OF_TILE), :].astype(jnp.float32)
 
 
@@ -159,14 +198,7 @@
     total = blocks[0].astype(jnp.float32)
     for block in blocks[1:]:
         total += block.astype(jnp.float32)
-    half = SPAN // 2
-    lane = lax.broadcasted_iota(jnp.int32, (LANES, LANES), 0)
-    place = lax.broadcasted_iota(jnp.int32, (LANES, LANES), 1)
-    target = lane // SPAN * SPAN + lane % half * 2 + lane % SPAN // half
-    order = (target == place).astype(jnp.float32)
-    sum_ref[...] = jnp.dot(
-        total, order, precision=lax.Precision.HIGHEST, preferred_element_type=jnp.float32
-    )
+    sum_ref[...] = total
     tiles = size // ROWS_OF_TILE
     for i in range(ROWS_OF_TILE):
         at = pl.ds(i * LANES, LANES)
@@ -204,7 +236,23 @@
     others = exchange([amplitudes] * (inner - 1), ("inner",), (inner,))[::-1]
     shard_rows = own_cd * ROWS_OF_TILE
     row_scratch = [pltpu.VMEM((shard_rows, LANES), f32)]
-    own = call(layout_kernel, shape((shard_rows, LANES), bf16), [VMEM], amplitudes, scratch=row_scratch)
+    sizes = outer, inner, groups, cores
+    rows_of = lambda count: shape((count, LANES), jnp.int32)
+    arguments = [
+        amplitudes,
+        cd_tile.reshape(1, held),
+        part_dest.reshape(1, parts),
+        place.reshape(1, parts),
+    ]
+    own, first_cd, own_slot, other_slot = call(
+        functools.partial(layout_kernel, sizes, per_col, by_permutes),
+        [shape((shard_rows, LANES), bf16), rows_of(held), rows_of(parts), rows_of(parts)],
+        [pl.BlockSpec(memory_space=pltpu.HBM)] * len(arguments),
+        *[pltpu.with_memory_space_constraint(x, pltpu.HBM) for x in arguments],
+        scratch=row_scratch
+        + [pltpu.VMEM(x.shape, x.dtype) for x in arguments]
+        + [pltpu.SemaphoreType.DMA((len(arguments),))],
+    )
     near = call(
         near_kernel,
         shape((inner * shard_rows, LANES), bf16),
@@ -226,41 +274,32 @@
         [VMEM],
         tiles.reshape(held * ROWS_OF_TILE, LANES),
     )
-    dest, col = part_dest[:, 0], place // per_col
-    to_inner = offset(dest % inner, lax.axis_index("inner"), inner)
-    to_group = offset(col // cores, lax.axis_index("groups"), groups)
-    to_outer = dest // inner
-    if by_permutes:
-        to_outer = offset(to_outer, lax.axis_index("outer"), outer)
-    slot = ((to_inner * groups + to_group) * outer + to_outer) * per_col + place % per_col
-    stays = col % cores == lax.axis_index("core")
-    own_slot = jnp.where(stays, slot, slots)
     if cores > 1:
-        other_slot = lax.ppermute(jnp.where(stays, slots, slot), "core", swap)
+        other_slot = lax.ppermute(other_slot, "core", swap)
     else:
-        other_slot = jnp.full_like(slot, slots)
-    gathered, paired, own_slot, other_slot = lax.optimization_barrier(
-        (gathered, paired, own_slot, other_slot)
+        other_slot = jnp.full_like(other_slot, slots * ROWS_OF_TILE)
+    gathered, paired, own_slot, other_slot, first_cd = lax.optimization_barrier(
+        (gathered, paired, own_slot, other_slot, first_cd)
     )
 
     sources = gathered[::-1] + [near] if by_permutes else gathered
     partial = call(
         partial_kernel,
         shape((parts * ROWS_OF_TILE, LANES), bf16),
-        [SMEM] + [VMEM] * (1 + len(sources)),
-        cd_tile,
+        [VMEM] * (2 + len(sources)),
+        first_cd,
         paired,
         *sources,
         scratch=[pltpu.VMEM((rows * shard_rows, LANES), bf16)],
     )
     other = lax.ppermute(partial, "core", swap)
     summed = shape(((slots + 1) * ROWS_OF_TILE, LANES), f32)
-    own_sum = call(own_kernel, summed, [SMEM, VMEM], own_slot, partial)
+    own_sum = call(own_kernel, summed, [VMEM, VMEM], own_slot, partial)
     block = slots // plane * ROWS_OF_TILE
     *leaving, own_sum = call(
         other_kernel,
         [shape((block, LANES), bf16)] * (plane - 1) + [summed],
-        [SMEM, VMEM, VMEM],
+        [VMEM, VMEM, VMEM],
         other_slot,
         other,
         own_sum,

time: 36.2 us -> 34.5 us (0.953)
  local copies, waits for them, and re-layouts: 2.32 us -> 1.56 us
  other arithmetic: 0.71 us -> 0 us
  Pallas kernels: 4.06 us -> 3.38 us
  waiting for transfers between devices: 12.9 us -> 13.4 us
    unnamed x6 -> x2, local copies, waits for them, and re-layouts: 0.77 us -> 0.01 us
    select_n x2 -> x0, other arithmetic: 0.71 us -> none  [the longest x1 0.7 us: per_device(): other_slot = lax.ppermute(jnp.where(stays, slots, slot), 'core', swap)]
    pallas_call x8, Pallas kernels: 4.06 us -> 3.38 us  [call(): pl.pallas_call(kernel, out_shape=out_shape, in_specs=in_specs, out_specs=...]
    ppermute x1, waiting for transfers between devices: 0.77 us -> 1.28 us  [per_device(): other = lax.ppermute(partial, 'core', swap)]
  transfers between devices with their start and end apart: 12 -> 12, of which waited for: 9 -> 7; matrix products, arithmetic and copies ran while one was open for 6% -> 5% of each run, Pallas kernels for 3% -> 5%
where the time goes in v6:
time: 34.5 us; the launch traced here: 34.3 us
  starting transfers between devices  15.9 us (46%)
  waiting for transfers between devices  13.4 us (39%)
  Pallas kernels  3.38 us (10%)
  local copies, waits for them, and re-layouts  1.56 us (5%)
    ppermute x10, starting transfers between devices, exchange(): lax.ppermute(x, axes, pairs)  15.8 us
    ppermute x10, waiting for transfers between devices, exchange(): lax.ppermute(x, axes, pairs)  12.2 us
    pallas_call x8, Pallas kernels, call(): pl.pallas_call(kernel, out_shape=out_shape, in_specs=in_specs, out_specs=...  3.38 us
    reshape x1, local copies, waits for them, and re-layouts, per_device(): tiles.reshape(held * ROWS_OF_TILE, LANES)  1.55 us
    ppermute x1, waiting for transfers between devices, per_device(): other = lax.ppermute(partial, 'core', swap)  1.28 us
  transfers between devices with their start and end apart: 12, of which 7 were waited for; matrix products, arithmetic and copies ran while one was open for 5% of the time, Pallas kernels for 5%

profile of v6, /device:TPU:0, one launch (start us, length us, event | category | flops | bytes accessed | tf_op | source)
XLA Modules:
  0.0 34.3 jit_solution(179272387123300793)
XLA Ops:
  0.0 2.9 %collective-permute-start = (bf16[1,4,4096]{2,1,0:T(4,128)(2,1)}, bf16[1,4,4096]{2,1,0:T(4,128)(2,1)S(1)}, u32[]{:S(2)}, u32[]{:S(2)}) collective-permute-start(bf16[1,4,4096]{2,1,0:T(4,128)(2,1)} %refs_0_.1), channel_id=1, source_target_pairs={{0,4},{4,0},{1,5},{5,1},{2,6},{6,2},{3,7},{7,3},{8,12},{12,8},{9,1... | collective-permute-start | bytes 98312 | tf_op jit(solution)/shard_map/ppermute | solution.py:221
  2.9 1.0 %shard_map.64 = (bf16[128,128]{1,0:T(8,128)(2,1)S(1)}, s32[128,128]{1,0:T(8,128)S(1)}, s32[32,128]{1,0:T(8,128)S(1)}, s32[32,128]{1,0:T(8,128)S(1)}) custom-call(bf16[1,4,4096]{2,1,0:T(4,128)(2,1)} %refs_0_.1, s32[1,128]{1,0:T(1,128)} %bitcast.3, s32[1,32]{1,0:T(1,128)} %bitcast.4, s32[1,32]{1,0:T(1,128)} %bitcast.5), custom_call_target="tpu_custom_call" | custom-call | tf_op jit(solution)/shard_map/pallas_call | solution.py:24
  3.9 1.1 %collective-permute-done.refs_0_ = bf16[1,4,4096]{2,1,0:T(4,128)(2,1)S(1)} collective-permute-done((bf16[1,4,4096]{2,1,0:T(4,128)(2,1)}, bf16[1,4,4096]{2,1,0:T(4,128)(2,1)S(1)}, u32[]{:S(2)}, u32[]{:S(2)}) %collective-permute-start) | collective-permute-done | bytes 32800 | tf_op jit(solution)/shard_map/ppermute | solution.py:221
  5.1 4.2 %collective-permute-start.3 = (bf16[256,128]{1,0:T(8,128)(2,1)S(1)}, bf16[256,128]{1,0:T(8,128)(2,1)S(1)}, u32[]{:S(2)}, u32[]{:S(2)}) collective-permute-start(bf16[256,128]{1,0:T(8,128)(2,1)S(1)} %shard_map.65.refs_3_), channel_id=1, source_target_pairs={{0,24},{8,16},{16,8},{24,0},{1,25},{9,17},{17,9},{25,1},{2,26},{10... | collective-permute-start | bytes 196616 | tf_op jit(solution)/shard_map/ppermute | solution.py:221
  9.3 0.0 collective-permute-start.2
  9.3 0.6 %collective-permute-start.1 = (bf16[256,128]{1,0:T(8,128)(2,1)S(1)}, bf16[256,128]{1,0:T(8,128)(2,1)S(1)}, u32[]{:S(2)}, u32[]{:S(2)}) collective-permute-start(bf16[256,128]{1,0:T(8,128)(2,1)S(1)} %shard_map.65.refs_3_), channel_id=1, source_target_pairs={{0,8},{8,0},{16,24},{24,16},{1,9},{9,1},{17,25},{25,17},{2,10},{10... | collective-permute-start | bytes 196616 | tf_op jit(solution)/shard_map/ppermute | solution.py:221
  9.9 0.0 collective-permute-start.4
  9.9 1.6 %reshape.15.tile_ref = bf16[4096,128]{1,0:T(8,128)(2,1)S(1)} reshape(bf16[128,4096]{1,0:T(8,128)(2,1)} %param.6) | data formatting | bytes 2097152 | tf_op jit(solution)/shard_map/reshape | solution.py:275
  11.5 0.5 %shard_map.66.tile_ref = bf16[2048,256]{1,0:T(8,128)(2,1)S(1)} custom-call(bf16[4096,128]{1,0:T(8,128)(2,1)S(1)} %reshape.15.tile_ref), custom_call_target="tpu_custom_call" | custom-call | tf_op jit(solution)/shard_map/pallas_call | solution.py:24
  12.0 0.0 collective-permute-done.4.slot_ref
  12.0 0.0 collective-permute-done.3.refs_0_
  12.0 2.5 %collective-permute-done.2.refs_1_ = bf16[256,128]{1,0:T(8,128)(2,1)S(1)} collective-permute-done((bf16[256,128]{1,0:T(8,128)(2,1)S(1)}, bf16[256,128]{1,0:T(8,128)(2,1)S(1)}, u32[]{:S(2)}, u32[]{:S(2)}) %collective-permute-start.2) | collective-permute-done | bytes 65568 | tf_op jit(solution)/shard_map/ppermute | solution.py:221
  14.5 0.0 collective-permute-done.1.refs_2_
  14.5 0.6 %shard_map.67.ref = bf16[1024,128]{1,0:T(8,128)(2,1)S(1)} custom-call(s32[128,128]{1,0:T(8,128)S(1)} %get-tuple-element.29.cd_ref, bf16[2048,256]{1,0:T(8,128)(2,1)S(1)} %shard_map.66.tile_ref, bf16[256,128]{1,0:T(8,128)(2,1)S(1)} %collective-permute-done.3.refs_0_, bf16[256,128]{1,0:T(8,128)(2,1)S(1)} %collective-permute-done.2.refs_1_, ...), custom_call_target="tpu_custom_call" | custom-call | tf_op jit(solution)/shard_map/pallas_call | solution.py:24
  15.1 0.1 collective-permute-start.5
  15.2 0.2 shard_map.68.in_ref
  15.4 1.3 %collective-permute-done.5.ref = bf16[1024,128]{1,0:T(8,128)(2,1)S(1)} collective-permute-done((bf16[1024,128]{1,0:T(8,128)(2,1)S(1)}, bf16[1024,128]{1,0:T(8,128)(2,1)S(1)}, u32[]{:S(2)}, u32[]{:S(2)}) %collective-permute-start.5) | collective-permute-done | bytes 262176 | tf_op jit(solution)/shard_map/ppermute | solution.py:295
  16.7 0.2 shard_map.69
  16.9 0.0 copy-start
  17.0 2.5 %collective-permute-start.6 = (bf16[512,128]{1,0:T(8,128)(2,1)S(1)}, bf16[512,128]{1,0:T(8,128)(2,1)S(1)}, u32[]{:S(2)}, u32[]{:S(2)}) collective-permute-start(bf16[512,128]{1,0:T(8,128)(2,1)S(1)} %get-tuple-element.36), channel_id=1, source_target_pairs={{0,6},{2,4},{4,2},{6,0},{1,7},{3,5},{5,3},{7,1},{8,14},{10,12},{12... | collective-permute-start | bytes 393224 | tf_op jit(solution)/shard_map/ppermute | solution.py:221
  19.5 0.5 %collective-permute-start.7 = (bf16[512,128]{1,0:T(8,128)(2,1)S(1)}, bf16[512,128]{1,0:T(8,128)(2,1)S(1)}, u32[]{:S(2)}, u32[]{:S(2)}) collective-permute-start(bf16[512,128]{1,0:T(8,128)(2,1)S(1)} %get-tuple-element.37), channel_id=1, source_target_pairs={{0,4},{2,6},{4,0},{6,2},{1,5},{3,7},{5,1},{7,3},{8,12},{10,14},{12... | collective-permute-start | bytes 393224 | tf_op jit(solution)/shard_map/ppermute | solution.py:221
  20.0 0.5 %collective-permute-start.8 = (bf16[512,128]{1,0:T(8,128)(2,1)S(1)}, bf16[512,128]{1,0:T(8,128)(2,1)S(1)}, u32[]{:S(2)}, u32[]{:S(2)}) collective-permute-start(bf16[512,128]{1,0:T(8,128)(2,1)S(1)} %get-tuple-element.38), channel_id=1, source_target_pairs={{0,2},{2,0},{4,6},{6,4},{1,3},{3,1},{5,7},{7,5},{8,10},{10,8},{12,... | collective-permute-start | bytes 393224 | tf_op jit(solution)/shard_map/ppermute | solution.py:221
  20.5 3.8 %collective-permute-done.6.refs_0_ = bf16[512,128]{1,0:T(8,128)(2,1)S(1)} collective-permute-done((bf16[512,128]{1,0:T(8,128)(2,1)S(1)}, bf16[512,128]{1,0:T(8,128)(2,1)S(1)}, u32[]{:S(2)}, u32[]{:S(2)}) %collective-permute-start.6) | collective-permute-done | bytes 131104 | tf_op jit(solution)/shard_map/ppermute | solution.py:221
  24.3 2.1 %collective-permute-done.7.refs_1_ = bf16[512,128]{1,0:T(8,128)(2,1)S(1)} collective-permute-done((bf16[512,128]{1,0:T(8,128)(2,1)S(1)}, bf16[512,128]{1,0:T(8,128)(2,1)S(1)}, u32[]{:S(2)}, u32[]{:S(2)}) %collective-permute-start.7) | collective-permute-done | bytes 131104 | tf_op jit(solution)/shard_map/ppermute | solution.py:221
  26.3 0.0 collective-permute-done.8.refs_2_
  26.3 0.1 shard_map.70
  26.4 2.2 %collective-permute-start.9 = (bf16[128,128]{1,0:T(8,128)(2,1)S(1)}, bf16[128,128]{1,0:T(8,128)(2,1)S(1)}, u32[]{:S(2)}, u32[]{:S(2)}) collective-permute-start(bf16[128,128]{1,0:T(8,128)(2,1)S(1)} %get-tuple-element.39), channel_id=1, source_target_pairs={{0,24},{8,16},{16,8},{24,0},{1,25},{9,17},{17,9},{25,1},{2,26},{10... | collective-permute-start | bytes 98312 | tf_op jit(solution)/shard_map/ppermute | solution.py:221
  28.6 0.0 collective-permute-start.10
  28.6 2.3 %collective-permute-start.11 = (bf16[128,128]{1,0:T(8,128)(2,1)S(1)}, bf16[128,128]{1,0:T(8,128)(2,1)S(1)}, u32[]{:S(2)}, u32[]{:S(2)}) collective-permute-start(bf16[128,128]{1,0:T(8,128)(2,1)S(1)} %get-tuple-element.41), channel_id=1, source_target_pairs={{0,8},{8,0},{16,24},{24,16},{1,9},{9,1},{17,25},{25,17},{2,10},{10... | collective-permute-start | bytes 98312 | tf_op jit(solution)/shard_map/ppermute | solution.py:221
  30.8 1.3 %collective-permute-done.9.refs_0_ = bf16[128,128]{1,0:T(8,128)(2,1)S(1)} collective-permute-done((bf16[128,128]{1,0:T(8,128)(2,1)S(1)}, bf16[128,128]{1,0:T(8,128)(2,1)S(1)}, u32[]{:S(2)}, u32[]{:S(2)}) %collective-permute-start.9) | collective-permute-done | bytes 32800 | tf_op jit(solution)/shard_map/ppermute | solution.py:221
  32.2 1.4 %collective-permute-done.10.refs_1_ = bf16[128,128]{1,0:T(8,128)(2,1)S(1)} collective-permute-done((bf16[128,128]{1,0:T(8,128)(2,1)S(1)}, bf16[128,128]{1,0:T(8,128)(2,1)S(1)}, u32[]{:S(2)}, u32[]{:S(2)}) %collective-permute-start.10) | collective-permute-done | bytes 32800 | tf_op jit(solution)/shard_map/ppermute | solution.py:221
  33.6 0.0 collective-permute-done.11.refs_2_
  33.6 0.0 copy-done
  33.6 0.7 %shard_map.71 = f32[1,4,4096]{2,1,0:T(4,128)} custom-call(bf16[128,128]{1,0:T(8,128)(2,1)S(1)} %collective-permute-done.9.refs_0_, bf16[128,128]{1,0:T(8,128)(2,1)S(1)} %collective-permute-done.10.refs_1_, bf16[128,128]{1,0:T(8,128)(2,1)S(1)} %collective-permute-done.11.refs_2_, f32[128,128]{1,0:T(8,128)S(1)} %get-tuple-element.42.refs_3_, ...), custom_call_target="tpu_custom_call" | custom-call | tf_op jit(solution)/shard_map/pallas_call | solution.py:24
  (1 shorter events, 0.0 us)
Async XLA Ops:
  0.0 5.0 %collective-permute-start = (bf16[1,4,4096]{2,1,0:T(4,128)(2,1)}, bf16[1,4,4096]{2,1,0:T(4,128)(2,1)S(1)}, u32[]{:S(2)}, u32[]{:S(2)}) collective-permute-start(bf16[1,4,4096]{2,1,0:T(4,128)(2,1)} %refs_0_.1), channel_id=1, source_target_pairs={{0,4},{4,0},{1,5},{5,1},{2,6},{6,2},{3,7},{7,3},{8,12},{12,8},{9,1... | collective-permute-start | bytes 98312 | tf_op jit(solution)/shard_map/ppermute | solution.py:221
  5.1 6.9 %collective-permute-start.3 = (bf16[256,128]{1,0:T(8,128)(2,1)S(1)}, bf16[256,128]{1,0:T(8,128)(2,1)S(1)}, u32[]{:S(2)}, u32[]{:S(2)}) collective-permute-start(bf16[256,128]{1,0:T(8,128)(2,1)S(1)} %shard_map.65.refs_3_), channel_id=1, source_target_pairs={{0,24},{8,16},{16,8},{24,0},{1,25},{9,17},{17,9},{25,1},{2,26},{10... | collective-permute-start | bytes 196616 | tf_op jit(solution)/shard_map/ppermute | solution.py:221
  9.3 5.2 %collective-permute-start.2 = (bf16[256,128]{1,0:T(8,128)(2,1)S(1)}, bf16[256,128]{1,0:T(8,128)(2,1)S(1)}, u32[]{:S(2)}, u32[]{:S(2)}) collective-permute-start(bf16[256,128]{1,0:T(8,128)(2,1)S(1)} %shard_map.65.refs_3_), channel_id=1, source_target_pairs={{0,16},{8,24},{16,0},{24,8},{1,17},{9,25},{17,1},{25,9},{2,18},{10... | collective-permute-start | bytes 196616 | tf_op jit(solution)/shard_map/ppermute | solution.py:221
  9.3 5.2 %collective-permute-start.1 = (bf16[256,128]{1,0:T(8,128)(2,1)S(1)}, bf16[256,128]{1,0:T(8,128)(2,1)S(1)}, u32[]{:S(2)}, u32[]{:S(2)}) collective-permute-start(bf16[256,128]{1,0:T(8,128)(2,1)S(1)} %shard_map.65.refs_3_), channel_id=1, source_target_pairs={{0,8},{8,0},{16,24},{24,16},{1,9},{9,1},{17,25},{25,17},{2,10},{10... | collective-permute-start | bytes 196616 | tf_op jit(solution)/shard_map/ppermute | solution.py:221
  9.9 2.1 %collective-permute-start.4 = (s32[32,128]{1,0:T(8,128)S(1)}, s32[32,128]{1,0:T(8,128)S(1)}, u32[]{:S(2)}, u32[]{:S(2)}) collective-permute-start(s32[32,128]{1,0:T(8,128)S(1)} %get-tuple-element.26), channel_id=1, source_target_pairs={{0,1},{1,0},{2,3},{3,2},{4,5},{5,4},{6,7},{7,6},{8,9},{9,8},{10,11... | collective-permute-start | bytes 49160 | tf_op jit(solution)/shard_map/ppermute | solution.py:278
  15.1 1.6 %collective-permute-start.5 = (bf16[1024,128]{1,0:T(8,128)(2,1)S(1)}, bf16[1024,128]{1,0:T(8,128)(2,1)S(1)}, u32[]{:S(2)}, u32[]{:S(2)}) collective-permute-start(bf16[1024,128]{1,0:T(8,128)(2,1)S(1)} %shard_map.67.ref), channel_id=1, source_target_pairs={{0,1},{1,0},{2,3},{3,2},{4,5},{5,4},{6,7},{7,6},{8,9},{9,8},{10,11... | collective-permute-start | bytes 786440 | tf_op jit(solution)/shard_map/ppermute | solution.py:295
  16.9 16.7 %copy-start = (f32[1,4,4096]{2,1,0:T(4,128)S(1)}, f32[1,4,4096]{2,1,0:T(4,128)}, u32[]{:S(2)}) copy-start(f32[1,4,4096]{2,1,0:T(4,128)} %refs_4_.1) | copy-start | bytes 196612
  17.0 7.3 %collective-permute-start.6 = (bf16[512,128]{1,0:T(8,128)(2,1)S(1)}, bf16[512,128]{1,0:T(8,128)(2,1)S(1)}, u32[]{:S(2)}, u32[]{:S(2)}) collective-permute-start(bf16[512,128]{1,0:T(8,128)(2,1)S(1)} %get-tuple-element.36), channel_id=1, source_target_pairs={{0,6},{2,4},{4,2},{6,0},{1,7},{3,5},{5,3},{7,1},{8,14},{10,12},{12... | collective-permute-start | bytes 393224 | tf_op jit(solution)/shard_map/ppermute | solution.py:221
  19.5 6.8 %collective-permute-start.7 = (bf16[512,128]{1,0:T(8,128)(2,1)S(1)}, bf16[512,128]{1,0:T(8,128)(2,1)S(1)}, u32[]{:S(2)}, u32[]{:S(2)}) collective-permute-start(bf16[512,128]{1,0:T(8,128)(2,1)S(1)} %get-tuple-element.37), channel_id=1, source_target_pairs={{0,4},{2,6},{4,0},{6,2},{1,5},{3,7},{5,1},{7,3},{8,12},{10,14},{12... | collective-permute-start | bytes 393224 | tf_op jit(solution)/shard_map/ppermute | solution.py:221
  20.0 6.3 %collective-permute-start.8 = (bf16[512,128]{1,0:T(8,128)(2,1)S(1)}, bf16[512,128]{1,0:T(8,128)(2,1)S(1)}, u32[]{:S(2)}, u32[]{:S(2)}) collective-permute-start(bf16[512,128]{1,0:T(8,128)(2,1)S(1)} %get-tuple-element.38), channel_id=1, source_target_pairs={{0,2},{2,0},{4,6},{6,4},{1,3},{3,1},{5,7},{7,5},{8,10},{10,8},{12,... | collective-permute-start | bytes 393224 | tf_op jit(solution)/shard_map/ppermute | solution.py:221
  26.4 5.8 %collective-permute-start.9 = (bf16[128,128]{1,0:T(8,128)(2,1)S(1)}, bf16[128,128]{1,0:T(8,128)(2,1)S(1)}, u32[]{:S(2)}, u32[]{:S(2)}) collective-permute-start(bf16[128,128]{1,0:T(8,128)(2,1)S(1)} %get-tuple-element.39), channel_id=1, source_target_pairs={{0,24},{8,16},{16,8},{24,0},{1,25},{9,17},{17,9},{25,1},{2,26},{10... | collective-permute-start | bytes 98312 | tf_op jit(solution)/shard_map/ppermute | solution.py:221
  28.6 5.0 %collective-permute-start.10 = (bf16[128,128]{1,0:T(8,128)(2,1)S(1)}, bf16[128,128]{1,0:T(8,128)(2,1)S(1)}, u32[]{:S(2)}, u32[]{:S(2)}) collective-permute-start(bf16[128,128]{1,0:T(8,128)(2,1)S(1)} %get-tuple-element.40), channel_id=1, source_target_pairs={{0,16},{8,24},{16,0},{24,8},{1,17},{9,25},{17,1},{25,9},{2,18},{10... | collective-permute-start | bytes 98312 | tf_op jit(solution)/shard_map/ppermute | solution.py:221
  28.6 5.0 %collective-permute-start.11 = (bf16[128,128]{1,0:T(8,128)(2,1)S(1)}, bf16[128,128]{1,0:T(8,128)(2,1)S(1)}, u32[]{:S(2)}, u32[]{:S(2)}) collective-permute-start(bf16[128,128]{1,0:T(8,128)(2,1)S(1)} %get-tuple-element.41), channel_id=1, source_target_pairs={{0,8},{8,0},{16,24},{24,16},{1,9},{9,1},{17,25},{25,17},{2,10},{10... | collective-permute-start | bytes 98312 | tf_op jit(solution)/shard_map/ppermute | solution.py:221

commit v7 on v6

--- a/solution.py
+++ b/solution.py
@@ -85,7 +85,8 @@
     if by_permutes:
         to_outer = offset(to_outer, lax.axis_index("outer"), outer)
     slot = ((to_inner * groups + to_group) * outer + to_outer) * per_col + place % per_col
-    stays = col % cores == lax.axis_index("core")
+    flips = (to_outer != 0).astype(jnp.int32) if by_permutes else 0
+    stays = (col + flips) % cores == lax.axis_index("core")
     unused = math.prod(sizes[:3]) * per_col
     own_slot_ref[...] = down(jnp.where(stays, slot, unused) * ROWS_OF_TILE)
     other_slot_ref[...] = down(jnp.where(stays, unused, slot) * ROWS_OF_TILE)
@@ -214,11 +215,14 @@
             a ^ b if n & (n - 1) == 0 else (a + b) % n for a, b, n in zip(place, by, sizes)
         )
 
-    return [[(number[p], number[moved(p, by)]) for p in places] for by in places[1:]]
-
-
-def exchange(blocks, axes, sizes):
-    return [lax.ppermute(x, axes, pairs) for x, pairs in zip(blocks, permutes(sizes))][::-1]
+    return {by: [(number[p], number[moved(p, by)]) for p in places] for by in places[1:]}
+
+
+def exchange(blocks, axes, sizes, flip=0):
+    pairs = permutes(sizes)
+    offsets = itertools.product(*map(range, sizes[:-1]))
+    to = [by + (flip % sizes[-1],) for by in offsets][1:]
+    return [lax.ppermute(x, axes, pairs[by]) for x, by in zip(blocks, to)][::-1]
 
 
 def per_device(outer, inner, groups, cores, tiles, cd_tile, part_dest, place, amplitudes, residual_in):
@@ -233,7 +237,7 @@
     by_permutes = outer <= MOST_PERMUTED
     swap = [(i, (i + 1) % cores) for i in range(cores)]
 
-    others = exchange([amplitudes] * (inner - 1), ("inner",), (inner,))[::-1]
+    others = exchange([amplitudes] * (inner - 1), ("inner", "core"), (inner, cores))[::-1]
     shard_rows = own_cd * ROWS_OF_TILE
     row_scratch = [pltpu.VMEM((shard_rows, LANES), f32)]
     sizes = outer, inner, groups, cores
@@ -262,7 +266,7 @@
         scratch=row_scratch,
     )
     if by_permutes:
-        gathered = exchange([near] * (outer - 1), ("outer",), (outer,))[::-1]
+        gathered = exchange([near] * (outer - 1), ("outer", "core"), (outer, cores))[::-1]
     else:
         repeated = jnp.broadcast_to(near, (outer,) + near.shape)
         gathered = lax.all_to_all(repeated, "outer", split_axis=0, concat_axis=0, tiled=True)
@@ -305,7 +309,7 @@
         own_sum,
         aliases={2: plane - 1},
     )
-    arrived = exchange(leaving, ("inner", "groups"), (inner, groups))
+    arrived = exchange(leaving, ("inner", "groups", "core"), (inner, groups, cores))
     mine = per_col * ROWS_OF_TILE
     if by_permutes:
         split = [shape((mine, LANES), f32)] + [shape((mine, LANES), bf16)] * (outer - 1)
@@ -319,7 +323,7 @@
         *arrived,
     )
     if by_permutes:
-        incoming = exchange(sums[1:], ("outer",), (outer,)) + [sums[0]]
+        incoming = exchange(sums[1:], ("outer", "core"), (outer, cores), flip=1) + [sums[0]]
     else:
         incoming = [
             lax.all_to_all(

time: 34.5 us -> 33.6 us (0.974)
  starting transfers between devices: 15.9 us -> 14.8 us
    ppermute x10, starting transfers between devices: 15.8 us -> 14.7 us  [exchange(): return [lax.ppermute(x, axes, pairs[by]) for x, by in zip(blocks, to)][::-1]]
where the time goes in v7:
time: 33.6 us; the launch traced here: 33.1 us
  starting transfers between devices  14.8 us (44%)
  waiting for transfers between devices  13.4 us (40%)
  Pallas kernels  3.36 us (10%)
  local copies, waits for them, and re-layouts  1.56 us (5%)
    ppermute x10, starting transfers between devices, exchange(): return [lax.ppermute(x, axes, pairs[by]) for x, by in zip(blocks, to)][::-1]  14.7 us
    ppermute x10, waiting for transfers between devices, exchange(): return [lax.ppermute(x, axes, pairs[by]) for x, by in zip(blocks, to)][::-1]  12.1 us
    pallas_call x8, Pallas kernels, call(): pl.pallas_call(kernel, out_shape=out_shape, in_specs=in_specs, out_specs=...  3.36 us
    reshape x1, local copies, waits for them, and re-layouts, per_device(): tiles.reshape(held * ROWS_OF_TILE, LANES)  1.55 us
    ppermute x1, waiting for transfers between devices, per_device(): other = lax.ppermute(partial, 'core', swap)  1.3 us
  transfers between devices with their start and end apart: 12, of which 7 were waited for; matrix products, arithmetic and copies ran while one was open for 5% of the time, Pallas kernels for 5%

profile of v7, /device:TPU:0, one launch (start us, length us, event | category | flops | bytes accessed | tf_op | source)
XLA Modules:
  0.0 33.1 jit_solution(8917515263175967381)
XLA Ops:
  0.0 2.9 %collective-permute-start = (bf16[1,4,4096]{2,1,0:T(4,128)(2,1)}, bf16[1,4,4096]{2,1,0:T(4,128)(2,1)S(1)}, u32[]{:S(2)}, u32[]{:S(2)}) collective-permute-start(bf16[1,4,4096]{2,1,0:T(4,128)(2,1)} %refs_0_.1), channel_id=1, source_target_pairs={{0,4},{1,5},{4,0},{5,1},{2,6},{3,7},{6,2},{7,3},{8,12},{9,13},{12,... | collective-permute-start | bytes 98312 | tf_op jit(solution)/shard_map/ppermute | solution.py:225
  2.9 1.0 %shard_map.64 = (bf16[128,128]{1,0:T(8,128)(2,1)S(1)}, s32[128,128]{1,0:T(8,128)S(1)}, s32[32,128]{1,0:T(8,128)S(1)}, s32[32,128]{1,0:T(8,128)S(1)}) custom-call(bf16[1,4,4096]{2,1,0:T(4,128)(2,1)} %refs_0_.1, s32[1,128]{1,0:T(1,128)} %bitcast.3, s32[1,32]{1,0:T(1,128)} %bitcast.4, s32[1,32]{1,0:T(1,128)} %bitcast.5), custom_call_target="tpu_custom_call" | custom-call | tf_op jit(solution)/shard_map/pallas_call | solution.py:24
  3.9 1.1 %collective-permute-done.refs_0_ = bf16[1,4,4096]{2,1,0:T(4,128)(2,1)S(1)} collective-permute-done((bf16[1,4,4096]{2,1,0:T(4,128)(2,1)}, bf16[1,4,4096]{2,1,0:T(4,128)(2,1)S(1)}, u32[]{:S(2)}, u32[]{:S(2)}) %collective-permute-start) | collective-permute-done | bytes 32800 | tf_op jit(solution)/shard_map/ppermute | solution.py:225
  5.1 4.2 %collective-permute-start.3 = (bf16[256,128]{1,0:T(8,128)(2,1)S(1)}, bf16[256,128]{1,0:T(8,128)(2,1)S(1)}, u32[]{:S(2)}, u32[]{:S(2)}) collective-permute-start(bf16[256,128]{1,0:T(8,128)(2,1)S(1)} %shard_map.65.refs_3_), channel_id=1, source_target_pairs={{0,24},{1,25},{8,16},{9,17},{16,8},{17,9},{24,0},{25,1},{2,26},{3,... | collective-permute-start | bytes 196616 | tf_op jit(solution)/shard_map/ppermute | solution.py:225
  9.3 0.0 collective-permute-start.2
  9.3 0.6 %collective-permute-start.1 = (bf16[256,128]{1,0:T(8,128)(2,1)S(1)}, bf16[256,128]{1,0:T(8,128)(2,1)S(1)}, u32[]{:S(2)}, u32[]{:S(2)}) collective-permute-start(bf16[256,128]{1,0:T(8,128)(2,1)S(1)} %shard_map.65.refs_3_), channel_id=1, source_target_pairs={{0,8},{1,9},{8,0},{9,1},{16,24},{17,25},{24,16},{25,17},{2,10},{3,... | collective-permute-start | bytes 196616 | tf_op jit(solution)/shard_map/ppermute | solution.py:225
  9.9 0.0 collective-permute-start.4
  9.9 1.6 %reshape.15.tile_ref = bf16[4096,128]{1,0:T(8,128)(2,1)S(1)} reshape(bf16[128,4096]{1,0:T(8,128)(2,1)} %param.6) | data formatting | bytes 2097152 | tf_op jit(solution)/shard_map/reshape | solution.py:279
  11.5 0.5 %shard_map.66.tile_ref = bf16[2048,256]{1,0:T(8,128)(2,1)S(1)} custom-call(bf16[4096,128]{1,0:T(8,128)(2,1)S(1)} %reshape.15.tile_ref), custom_call_target="tpu_custom_call" | custom-call | tf_op jit(solution)/shard_map/pallas_call | solution.py:24
  12.0 0.0 collective-permute-done.4.slot_ref
  12.0 0.0 collective-permute-done.3.refs_0_
  12.0 2.5 %collective-permute-done.2.refs_1_ = bf16[256,128]{1,0:T(8,128)(2,1)S(1)} collective-permute-done((bf16[256,128]{1,0:T(8,128)(2,1)S(1)}, bf16[256,128]{1,0:T(8,128)(2,1)S(1)}, u32[]{:S(2)}, u32[]{:S(2)}) %collective-permute-start.2) | collective-permute-done | bytes 65568 | tf_op jit(solution)/shard_map/ppermute | solution.py:225
  14.5 0.0 collective-permute-done.1.refs_2_
  14.5 0.6 %shard_map.67.ref = bf16[1024,128]{1,0:T(8,128)(2,1)S(1)} custom-call(s32[128,128]{1,0:T(8,128)S(1)} %get-tuple-element.29.cd_ref, bf16[2048,256]{1,0:T(8,128)(2,1)S(1)} %shard_map.66.tile_ref, bf16[256,128]{1,0:T(8,128)(2,1)S(1)} %collective-permute-done.3.refs_0_, bf16[256,128]{1,0:T(8,128)(2,1)S(1)} %collective-permute-done.2.refs_1_, ...), custom_call_target="tpu_custom_call" | custom-call | tf_op jit(solution)/shard_map/pallas_call | solution.py:24
  15.1 0.1 collective-permute-start.5
  15.2 0.2 shard_map.68.in_ref
  15.4 1.3 %collective-permute-done.5.ref = bf16[1024,128]{1,0:T(8,128)(2,1)S(1)} collective-permute-done((bf16[1024,128]{1,0:T(8,128)(2,1)S(1)}, bf16[1024,128]{1,0:T(8,128)(2,1)S(1)}, u32[]{:S(2)}, u32[]{:S(2)}) %collective-permute-start.5) | collective-permute-done | bytes 262176 | tf_op jit(solution)/shard_map/ppermute | solution.py:299
  16.7 0.2 shard_map.69
  16.9 0.0 copy-start
  17.0 2.5 %collective-permute-start.6 = (bf16[512,128]{1,0:T(8,128)(2,1)S(1)}, bf16[512,128]{1,0:T(8,128)(2,1)S(1)}, u32[]{:S(2)}, u32[]{:S(2)}) collective-permute-start(bf16[512,128]{1,0:T(8,128)(2,1)S(1)} %get-tuple-element.36), channel_id=1, source_target_pairs={{0,6},{1,7},{2,4},{3,5},{4,2},{5,3},{6,0},{7,1},{8,14},{9,15},{10,... | collective-permute-start | bytes 393224 | tf_op jit(solution)/shard_map/ppermute | solution.py:225
  19.5 0.5 %collective-permute-start.7 = (bf16[512,128]{1,0:T(8,128)(2,1)S(1)}, bf16[512,128]{1,0:T(8,128)(2,1)S(1)}, u32[]{:S(2)}, u32[]{:S(2)}) collective-permute-start(bf16[512,128]{1,0:T(8,128)(2,1)S(1)} %get-tuple-element.37), channel_id=1, source_target_pairs={{0,4},{1,5},{2,6},{3,7},{4,0},{5,1},{6,2},{7,3},{8,12},{9,13},{10,... | collective-permute-start | bytes 393224 | tf_op jit(solution)/shard_map/ppermute | solution.py:225
  20.0 0.5 %collective-permute-start.8 = (bf16[512,128]{1,0:T(8,128)(2,1)S(1)}, bf16[512,128]{1,0:T(8,128)(2,1)S(1)}, u32[]{:S(2)}, u32[]{:S(2)}) collective-permute-start(bf16[512,128]{1,0:T(8,128)(2,1)S(1)} %get-tuple-element.38), channel_id=1, source_target_pairs={{0,2},{1,3},{2,0},{3,1},{4,6},{5,7},{6,4},{7,5},{8,10},{9,11},{10,... | collective-permute-start | bytes 393224 | tf_op jit(solution)/shard_map/ppermute | solution.py:225
  20.5 3.7 %collective-permute-done.6.refs_0_ = bf16[512,128]{1,0:T(8,128)(2,1)S(1)} collective-permute-done((bf16[512,128]{1,0:T(8,128)(2,1)S(1)}, bf16[512,128]{1,0:T(8,128)(2,1)S(1)}, u32[]{:S(2)}, u32[]{:S(2)}) %collective-permute-start.6) | collective-permute-done | bytes 131104 | tf_op jit(solution)/shard_map/ppermute | solution.py:225
  24.3 2.1 %collective-permute-done.7.refs_1_ = bf16[512,128]{1,0:T(8,128)(2,1)S(1)} collective-permute-done((bf16[512,128]{1,0:T(8,128)(2,1)S(1)}, bf16[512,128]{1,0:T(8,128)(2,1)S(1)}, u32[]{:S(2)}, u32[]{:S(2)}) %collective-permute-start.7) | collective-permute-done | bytes 131104 | tf_op jit(solution)/shard_map/ppermute | solution.py:225
  26.3 0.0 collective-permute-done.8.refs_2_
  26.3 0.1 shard_map.70
  26.4 1.4 %collective-permute-start.9 = (bf16[128,128]{1,0:T(8,128)(2,1)S(1)}, bf16[128,128]{1,0:T(8,128)(2,1)S(1)}, u32[]{:S(2)}, u32[]{:S(2)}) collective-permute-start(bf16[128,128]{1,0:T(8,128)(2,1)S(1)} %get-tuple-element.39), channel_id=1, source_target_pairs={{0,25},{1,24},{8,17},{9,16},{16,9},{17,8},{24,1},{25,0},{2,27},{3,... | collective-permute-start | bytes 98312 | tf_op jit(solution)/shard_map/ppermute | solution.py:225
  27.8 0.4 %collective-permute-start.10 = (bf16[128,128]{1,0:T(8,128)(2,1)S(1)}, bf16[128,128]{1,0:T(8,128)(2,1)S(1)}, u32[]{:S(2)}, u32[]{:S(2)}) collective-permute-start(bf16[128,128]{1,0:T(8,128)(2,1)S(1)} %get-tuple-element.40), channel_id=1, source_target_pairs={{0,17},{1,16},{8,25},{9,24},{16,1},{17,0},{24,9},{25,8},{2,19},{3,... | collective-permute-start | bytes 98312 | tf_op jit(solution)/shard_map/ppermute | solution.py:225
  28.2 1.5 %collective-permute-start.11 = (bf16[128,128]{1,0:T(8,128)(2,1)S(1)}, bf16[128,128]{1,0:T(8,128)(2,1)S(1)}, u32[]{:S(2)}, u32[]{:S(2)}) collective-permute-start(bf16[128,128]{1,0:T(8,128)(2,1)S(1)} %get-tuple-element.41), channel_id=1, source_target_pairs={{0,9},{1,8},{8,1},{9,0},{16,25},{17,24},{24,17},{25,16},{2,11},{3,... | collective-permute-start | bytes 98312 | tf_op jit(solution)/shard_map/ppermute | solution.py:225
  29.7 2.0 %collective-permute-done.9.refs_0_ = bf16[128,128]{1,0:T(8,128)(2,1)S(1)} collective-permute-done((bf16[128,128]{1,0:T(8,128)(2,1)S(1)}, bf16[128,128]{1,0:T(8,128)(2,1)S(1)}, u32[]{:S(2)}, u32[]{:S(2)}) %collective-permute-start.9) | collective-permute-done | bytes 32800 | tf_op jit(solution)/shard_map/ppermute | solution.py:225
  31.8 0.7 %collective-permute-done.10.refs_1_ = bf16[128,128]{1,0:T(8,128)(2,1)S(1)} collective-permute-done((bf16[128,128]{1,0:T(8,128)(2,1)S(1)}, bf16[128,128]{1,0:T(8,128)(2,1)S(1)}, u32[]{:S(2)}, u32[]{:S(2)}) %collective-permute-start.10) | collective-permute-done | bytes 32800 | tf_op jit(solution)/shard_map/ppermute | solution.py:225
  32.4 0.0 collective-permute-done.11.refs_2_
  32.4 0.0 copy-done
  32.4 0.7 %shard_map.71 = f32[1,4,4096]{2,1,0:T(4,128)} custom-call(bf16[128,128]{1,0:T(8,128)(2,1)S(1)} %collective-permute-done.9.refs_0_, bf16[128,128]{1,0:T(8,128)(2,1)S(1)} %collective-permute-done.10.refs_1_, bf16[128,128]{1,0:T(8,128)(2,1)S(1)} %collective-permute-done.11.refs_2_, f32[128,128]{1,0:T(8,128)S(1)} %get-tuple-element.42.refs_3_, ...), custom_call_target="tpu_custom_call" | custom-call | tf_op jit(solution)/shard_map/pallas_call | solution.py:24
  (1 shorter events, 0.0 us)
Async XLA Ops:
  0.0 5.0 %collective-permute-start = (bf16[1,4,4096]{2,1,0:T(4,128)(2,1)}, bf16[1,4,4096]{2,1,0:T(4,128)(2,1)S(1)}, u32[]{:S(2)}, u32[]{:S(2)}) collective-permute-start(bf16[1,4,4096]{2,1,0:T(4,128)(2,1)} %refs_0_.1), channel_id=1, source_target_pairs={{0,4},{1,5},{4,0},{5,1},{2,6},{3,7},{6,2},{7,3},{8,12},{9,13},{12,... | collective-permute-start | bytes 98312 | tf_op jit(solution)/shard_map/ppermute | solution.py:225
  5.1 6.9 %collective-permute-start.3 = (bf16[256,128]{1,0:T(8,128)(2,1)S(1)}, bf16[256,128]{1,0:T(8,128)(2,1)S(1)}, u32[]{:S(2)}, u32[]{:S(2)}) collective-permute-start(bf16[256,128]{1,0:T(8,128)(2,1)S(1)} %shard_map.65.refs_3_), channel_id=1, source_target_pairs={{0,24},{1,25},{8,16},{9,17},{16,8},{17,9},{24,0},{25,1},{2,26},{3,... | collective-permute-start | bytes 196616 | tf_op jit(solution)/shard_map/ppermute | solution.py:225
  9.3 5.2 %collective-permute-start.2 = (bf16[256,128]{1,0:T(8,128)(2,1)S(1)}, bf16[256,128]{1,0:T(8,128)(2,1)S(1)}, u32[]{:S(2)}, u32[]{:S(2)}) collective-permute-start(bf16[256,128]{1,0:T(8,128)(2,1)S(1)} %shard_map.65.refs_3_), channel_id=1, source_target_pairs={{0,16},{1,17},{8,24},{9,25},{16,0},{17,1},{24,8},{25,9},{2,18},{3,... | collective-permute-start | bytes 196616 | tf_op jit(solution)/shard_map/ppermute | solution.py:225
  9.3 5.2 %collective-permute-start.1 = (bf16[256,128]{1,0:T(8,128)(2,1)S(1)}, bf16[256,128]{1,0:T(8,128)(2,1)S(1)}, u32[]{:S(2)}, u32[]{:S(2)}) collective-permute-start(bf16[256,128]{1,0:T(8,128)(2,1)S(1)} %shard_map.65.refs_3_), channel_id=1, source_target_pairs={{0,8},{1,9},{8,0},{9,1},{16,24},{17,25},{24,16},{25,17},{2,10},{3,... | collective-permute-start | bytes 196616 | tf_op jit(solution)/shard_map/ppermute | solution.py:225
  9.9 2.1 %collective-permute-start.4 = (s32[32,128]{1,0:T(8,128)S(1)}, s32[32,128]{1,0:T(8,128)S(1)}, u32[]{:S(2)}, u32[]{:S(2)}) collective-permute-start(s32[32,128]{1,0:T(8,128)S(1)} %get-tuple-element.26), channel_id=1, source_target_pairs={{0,1},{1,0},{2,3},{3,2},{4,5},{5,4},{6,7},{7,6},{8,9},{9,8},{10,11... | collective-permute-start | bytes 49160 | tf_op jit(solution)/shard_map/ppermute | solution.py:282
  15.1 1.6 %collective-permute-start.5 = (bf16[1024,128]{1,0:T(8,128)(2,1)S(1)}, bf16[1024,128]{1,0:T(8,128)(2,1)S(1)}, u32[]{:S(2)}, u32[]{:S(2)}) collective-permute-start(bf16[1024,128]{1,0:T(8,128)(2,1)S(1)} %shard_map.67.ref), channel_id=1, source_target_pairs={{0,1},{1,0},{2,3},{3,2},{4,5},{5,4},{6,7},{7,6},{8,9},{9,8},{10,11... | collective-permute-start | bytes 786440 | tf_op jit(solution)/shard_map/ppermute | solution.py:299
  16.9 15.5 %copy-start = (f32[1,4,4096]{2,1,0:T(4,128)S(1)}, f32[1,4,4096]{2,1,0:T(4,128)}, u32[]{:S(2)}) copy-start(f32[1,4,4096]{2,1,0:T(4,128)} %refs_4_.1) | copy-start | bytes 196612
  17.0 7.3 %collective-permute-start.6 = (bf16[512,128]{1,0:T(8,128)(2,1)S(1)}, bf16[512,128]{1,0:T(8,128)(2,1)S(1)}, u32[]{:S(2)}, u32[]{:S(2)}) collective-permute-start(bf16[512,128]{1,0:T(8,128)(2,1)S(1)} %get-tuple-element.36), channel_id=1, source_target_pairs={{0,6},{1,7},{2,4},{3,5},{4,2},{5,3},{6,0},{7,1},{8,14},{9,15},{10,... | collective-permute-start | bytes 393224 | tf_op jit(solution)/shard_map/ppermute | solution.py:225
  19.5 6.9 %collective-permute-start.7 = (bf16[512,128]{1,0:T(8,128)(2,1)S(1)}, bf16[512,128]{1,0:T(8,128)(2,1)S(1)}, u32[]{:S(2)}, u32[]{:S(2)}) collective-permute-start(bf16[512,128]{1,0:T(8,128)(2,1)S(1)} %get-tuple-element.37), channel_id=1, source_target_pairs={{0,4},{1,5},{2,6},{3,7},{4,0},{5,1},{6,2},{7,3},{8,12},{9,13},{10,... | collective-permute-start | bytes 393224 | tf_op jit(solution)/shard_map/ppermute | solution.py:225
  20.0 6.3 %collective-permute-start.8 = (bf16[512,128]{1,0:T(8,128)(2,1)S(1)}, bf16[512,128]{1,0:T(8,128)(2,1)S(1)}, u32[]{:S(2)}, u32[]{:S(2)}) collective-permute-start(bf16[512,128]{1,0:T(8,128)(2,1)S(1)} %get-tuple-element.38), channel_id=1, source_target_pairs={{0,2},{1,3},{2,0},{3,1},{4,6},{5,7},{6,4},{7,5},{8,10},{9,11},{10,... | collective-permute-start | bytes 393224 | tf_op jit(solution)/shard_map/ppermute | solution.py:225
  26.4 5.4 %collective-permute-start.9 = (bf16[128,128]{1,0:T(8,128)(2,1)S(1)}, bf16[128,128]{1,0:T(8,128)(2,1)S(1)}, u32[]{:S(2)}, u32[]{:S(2)}) collective-permute-start(bf16[128,128]{1,0:T(8,128)(2,1)S(1)} %get-tuple-element.39), channel_id=1, source_target_pairs={{0,25},{1,24},{8,17},{9,16},{16,9},{17,8},{24,1},{25,0},{2,27},{3,... | collective-permute-start | bytes 98312 | tf_op jit(solution)/shard_map/ppermute | solution.py:225
  27.8 4.7 %collective-permute-start.10 = (bf16[128,128]{1,0:T(8,128)(2,1)S(1)}, bf16[128,128]{1,0:T(8,128)(2,1)S(1)}, u32[]{:S(2)}, u32[]{:S(2)}) collective-permute-start(bf16[128,128]{1,0:T(8,128)(2,1)S(1)} %get-tuple-element.40), channel_id=1, source_target_pairs={{0,17},{1,16},{8,25},{9,24},{16,1},{17,0},{24,9},{25,8},{2,19},{3,... | collective-permute-start | bytes 98312 | tf_op jit(solution)/shard_map/ppermute | solution.py:225
  28.2 4.2 %collective-permute-start.11 = (bf16[128,128]{1,0:T(8,128)(2,1)S(1)}, bf16[128,128]{1,0:T(8,128)(2,1)S(1)}, u32[]{:S(2)}, u32[]{:S(2)}) collective-permute-start(bf16[128,128]{1,0:T(8,128)(2,1)S(1)} %get-tuple-element.41), channel_id=1, source_target_pairs={{0,9},{1,8},{8,1},{9,0},{16,25},{17,24},{24,17},{25,16},{2,11},{3,... | collective-permute-start | bytes 98312 | tf_op jit(solution)/shard_map/ppermute | solution.py:225

commit v8 on v6

--- a/solution.py
+++ b/solution.py
@@ -62,7 +62,7 @@
     return jnp.broadcast_to(column.astype(jnp.int32), (size, LANES))
 
 
-def layout_kernel(sizes, per_col, by_permutes, *refs):
+def layout_kernel(sizes, per_col, by_permutes, opposite, *refs):
     sources, refs = refs[:4], refs[4:]
     out_ref, first_cd_ref, own_slot_ref, other_slot_ref, row_ref, *local_refs, arrivals = refs
     copies = [
@@ -84,11 +84,20 @@
     to_outer = dest // inner
     if by_permutes:
         to_outer = offset(to_outer, lax.axis_index("outer"), outer)
-    slot = ((to_inner * groups + to_group) * outer + to_outer) * per_col + place % per_col
-    stays = col % cores == lax.axis_index("core")
+    to_plane = to_inner * groups + to_group
+
+    def slot_on(core):
+        plane_first = to_plane * outer + to_outer
+        if not opposite:
+            return plane_first * per_col + place % per_col
+        outer_first = to_outer * (inner * groups) + to_plane
+        return jnp.where(core == 0, plane_first, outer_first) * per_col + place % per_col
+
+    me = lax.axis_index("core")
+    stays = col % cores == me
     unused = math.prod(sizes[:3]) * per_col
-    own_slot_ref[...] = down(jnp.where(stays, slot, unused) * ROWS_OF_TILE)
-    other_slot_ref[...] = down(jnp.where(stays, unused, slot) * ROWS_OF_TILE)
+    own_slot_ref[...] = down(jnp.where(stays, slot_on(me), unused) * ROWS_OF_TILE)
+    other_slot_ref[...] = down(jnp.where(stays, unused, slot_on(1 - me)) * ROWS_OF_TILE)
 
 
 def near_kernel(own_ref, *refs):
@@ -214,11 +223,26 @@
             a ^ b if n & (n - 1) == 0 else (a + b) % n for a, b, n in zip(place, by, sizes)
         )
 
-    return [[(number[p], number[moved(p, by)]) for p in places] for by in places[1:]]
+    return {by: [(number[p], number[moved(p, by)]) for p in places] for by in places[1:]}
 
 
 def exchange(blocks, axes, sizes):
-    return [lax.ppermute(x, axes, pairs) for x, pairs in zip(blocks, permutes(sizes))][::-1]
+    return [lax.ppermute(x, axes, pairs) for x, pairs in zip(blocks, permutes(sizes).values())][::-1]
+
+
+def exchange_crossed(blocks, sizes, outer_core):
+    outer, inner, groups, cores = sizes
+    offsets = (
+        list(itertools.product(range(outer), [0], [0], [0]))[1:],
+        list(itertools.product([0], range(inner), range(groups), [0]))[1:],
+    )
+    pairs = permutes(sizes)
+    arrived = []
+    for i, x in enumerate(blocks):
+        by_core = [pairs[offsets[core != outer_core][i]] for core in range(cores)]
+        both = [by_core[n % cores][n] for n in range(math.prod(sizes))]
+        arrived.append(lax.ppermute(x, ("outer", "inner", "groups", "core"), both))
+    return arrived[::-1]
 
 
 def per_device(outer, inner, groups, cores, tiles, cd_tile, part_dest, place, amplitudes, residual_in):
@@ -231,6 +255,7 @@
     plane = inner * groups
     slots = rows * groups * per_col
     by_permutes = outer <= MOST_PERMUTED
+    opposite = by_permutes and cores == 2 and outer == plane
     swap = [(i, (i + 1) % cores) for i in range(cores)]
 
     others = exchange([amplitudes] * (inner - 1), ("inner",), (inner,))[::-1]
@@ -245,7 +270,7 @@
         place.reshape(1, parts),
     ]
     own, first_cd, own_slot, other_slot = call(
-        functools.partial(layout_kernel, sizes, per_col, by_permutes),
+        functools.partial(layout_kernel, sizes, per_col, by_permutes, opposite),
         [shape((shard_rows, LANES), bf16), rows_of(held), rows_of(parts), rows_of(parts)],
         [pl.BlockSpec(memory_space=pltpu.HBM)] * len(arguments),
         *[pltpu.with_memory_space_constraint(x, pltpu.HBM) for x in arguments],
@@ -305,7 +330,10 @@
         own_sum,
         aliases={2: plane - 1},
     )
-    arrived = exchange(leaving, ("inner", "groups"), (inner, groups))
+    if opposite:
+        arrived = exchange_crossed(leaving, sizes, 1)
+    else:
+        arrived = exchange(leaving, ("inner", "groups"), (inner, groups))
     mine = per_col * ROWS_OF_TILE
     if by_permutes:
         split = [shape((mine, LANES), f32)] + [shape((mine, LANES), bf16)] * (outer - 1)
@@ -318,7 +346,9 @@
         own_sum,
         *arrived,
     )
-    if by_permutes:
+    if opposite:
+        incoming = exchange_crossed(sums[1:], sizes, 0) + [sums[0]]
+    elif by_permutes:
         incoming = exchange(sums[1:], ("outer",), (outer,)) + [sums[0]]
     else:
         incoming = [

time: 34.5 us -> 33.2 us (0.962)
  waiting for transfers between devices: 13.4 us -> 12.1 us
    ppermute x10 -> x4, waiting for transfers between devices: 12.2 us -> 3.57 us  [exchange(): lax.ppermute(x, axes, pairs)]
    ppermute x10 -> x4, starting transfers between devices: 15.8 us -> 7.78 us  [exchange(): lax.ppermute(x, axes, pairs)]
    ppermute x0 -> x6, starting transfers between devices: none -> 8.01 us  [exchange_crossed(): arrived.append(lax.ppermute(x, ('outer', 'inner', 'groups', 'core'), both))]
    ppermute x0 -> x6, waiting for transfers between devices: none -> 7.26 us  [exchange_crossed(): arrived.append(lax.ppermute(x, ('outer', 'inner', 'groups', 'core'), both))]
  transfers between devices with their start and end apart: 12 -> 12, of which waited for: 7 -> 8; matrix products, arithmetic and copies ran while one was open for 5% -> 5% of each run, Pallas kernels for 5% -> 5%
where the time goes in v8:
time: 33.2 us; the launch traced here: 33 us
  starting transfers between devices  15.9 us (48%)
  waiting for transfers between devices  12.1 us (36%)
  Pallas kernels  3.36 us (10%)
  local copies, waits for them, and re-layouts  1.56 us (5%)
    ppermute x6, starting transfers between devices, exchange_crossed(): arrived.append(lax.ppermute(x, ('outer', 'inner', 'groups', 'core'), both))  8.01 us
    ppermute x4, starting transfers between devices, exchange(): lax.ppermute(x, axes, pairs)  7.78 us
    ppermute x6, waiting for transfers between devices, exchange_crossed(): arrived.append(lax.ppermute(x, ('outer', 'inner', 'groups', 'core'), both))  7.26 us
    ppermute x4, waiting for transfers between devices, exchange(): lax.ppermute(x, axes, pairs)  3.57 us
    pallas_call x8, Pallas kernels, call(): pl.pallas_call(kernel, out_shape=out_shape, in_specs=in_specs, out_specs=...  3.36 us
    reshape x1, local copies, waits for them, and re-layouts, per_device(): tiles.reshape(held * ROWS_OF_TILE, LANES)  1.55 us
    ppermute x1, waiting for transfers between devices, per_device(): other = lax.ppermute(partial, 'core', swap)  1.29 us
  transfers between devices with their start and end apart: 12, of which 8 were waited for; matrix products, arithmetic and copies ran while one was open for 5% of the time, Pallas kernels for 5%

profile of v8, /device:TPU:0, one launch (start us, length us, event | category | flops | bytes accessed | tf_op | source)
XLA Modules:
  0.0 33.0 jit_solution(13974345659890860344)
XLA Ops:
  0.0 2.9 %collective-permute-start = (bf16[1,4,4096]{2,1,0:T(4,128)(2,1)}, bf16[1,4,4096]{2,1,0:T(4,128)(2,1)S(1)}, u32[]{:S(2)}, u32[]{:S(2)}) collective-permute-start(bf16[1,4,4096]{2,1,0:T(4,128)(2,1)} %refs_0_.1), channel_id=1, source_target_pairs={{0,4},{4,0},{1,5},{5,1},{2,6},{6,2},{3,7},{7,3},{8,12},{12,8},{9,1... | collective-permute-start | bytes 98312 | tf_op jit(solution)/shard_map/ppermute | solution.py:230
  2.9 1.0 %shard_map.64 = (bf16[128,128]{1,0:T(8,128)(2,1)S(1)}, s32[128,128]{1,0:T(8,128)S(1)}, s32[32,128]{1,0:T(8,128)S(1)}, s32[32,128]{1,0:T(8,128)S(1)}) custom-call(bf16[1,4,4096]{2,1,0:T(4,128)(2,1)} %refs_0_.1, s32[1,128]{1,0:T(1,128)} %bitcast.3, s32[1,32]{1,0:T(1,128)} %bitcast.4, s32[1,32]{1,0:T(1,128)} %bitcast.5), custom_call_target="tpu_custom_call" | custom-call | tf_op jit(solution)/shard_map/pallas_call | solution.py:24
  3.9 1.1 %collective-permute-done.refs_0_ = bf16[1,4,4096]{2,1,0:T(4,128)(2,1)S(1)} collective-permute-done((bf16[1,4,4096]{2,1,0:T(4,128)(2,1)}, bf16[1,4,4096]{2,1,0:T(4,128)(2,1)S(1)}, u32[]{:S(2)}, u32[]{:S(2)}) %collective-permute-start) | collective-permute-done | bytes 32800 | tf_op jit(solution)/shard_map/ppermute | solution.py:230
  5.1 4.2 %collective-permute-start.3 = (bf16[256,128]{1,0:T(8,128)(2,1)S(1)}, bf16[256,128]{1,0:T(8,128)(2,1)S(1)}, u32[]{:S(2)}, u32[]{:S(2)}) collective-permute-start(bf16[256,128]{1,0:T(8,128)(2,1)S(1)} %shard_map.65.refs_3_), channel_id=1, source_target_pairs={{0,24},{8,16},{16,8},{24,0},{1,25},{9,17},{17,9},{25,1},{2,26},{10... | collective-permute-start | bytes 196616 | tf_op jit(solution)/shard_map/ppermute | solution.py:230
  9.3 0.0 collective-permute-start.2
  9.3 0.6 %collective-permute-start.1 = (bf16[256,128]{1,0:T(8,128)(2,1)S(1)}, bf16[256,128]{1,0:T(8,128)(2,1)S(1)}, u32[]{:S(2)}, u32[]{:S(2)}) collective-permute-start(bf16[256,128]{1,0:T(8,128)(2,1)S(1)} %shard_map.65.refs_3_), channel_id=1, source_target_pairs={{0,8},{8,0},{16,24},{24,16},{1,9},{9,1},{17,25},{25,17},{2,10},{10... | collective-permute-start | bytes 196616 | tf_op jit(solution)/shard_map/ppermute | solution.py:230
  9.9 0.0 collective-permute-start.4
  9.9 1.6 %reshape.15.tile_ref = bf16[4096,128]{1,0:T(8,128)(2,1)S(1)} reshape(bf16[128,4096]{1,0:T(8,128)(2,1)} %param.6) | data formatting | bytes 2097152 | tf_op jit(solution)/shard_map/reshape | solution.py:300
  11.5 0.5 %shard_map.66.tile_ref = bf16[2048,256]{1,0:T(8,128)(2,1)S(1)} custom-call(bf16[4096,128]{1,0:T(8,128)(2,1)S(1)} %reshape.15.tile_ref), custom_call_target="tpu_custom_call" | custom-call | tf_op jit(solution)/shard_map/pallas_call | solution.py:24
  12.0 0.0 collective-permute-done.4.slot_ref
  12.0 0.0 collective-permute-done.3.refs_0_
  12.0 2.5 %collective-permute-done.2.refs_1_ = bf16[256,128]{1,0:T(8,128)(2,1)S(1)} collective-permute-done((bf16[256,128]{1,0:T(8,128)(2,1)S(1)}, bf16[256,128]{1,0:T(8,128)(2,1)S(1)}, u32[]{:S(2)}, u32[]{:S(2)}) %collective-permute-start.2) | collective-permute-done | bytes 65568 | tf_op jit(solution)/shard_map/ppermute | solution.py:230
  14.5 0.0 collective-permute-done.1.refs_2_
  14.5 0.6 %shard_map.67.ref = bf16[1024,128]{1,0:T(8,128)(2,1)S(1)} custom-call(s32[128,128]{1,0:T(8,128)S(1)} %get-tuple-element.29.cd_ref, bf16[2048,256]{1,0:T(8,128)(2,1)S(1)} %shard_map.66.tile_ref, bf16[256,128]{1,0:T(8,128)(2,1)S(1)} %collective-permute-done.3.refs_0_, bf16[256,128]{1,0:T(8,128)(2,1)S(1)} %collective-permute-done.2.refs_1_, ...), custom_call_target="tpu_custom_call" | custom-call | tf_op jit(solution)/shard_map/pallas_call | solution.py:24
  15.1 0.1 collective-permute-start.5
  15.2 0.2 shard_map.68.in_ref
  15.4 1.3 %collective-permute-done.5.ref = bf16[1024,128]{1,0:T(8,128)(2,1)S(1)} collective-permute-done((bf16[1024,128]{1,0:T(8,128)(2,1)S(1)}, bf16[1024,128]{1,0:T(8,128)(2,1)S(1)}, u32[]{:S(2)}, u32[]{:S(2)}) %collective-permute-start.5) | collective-permute-done | bytes 262176 | tf_op jit(solution)/shard_map/ppermute | solution.py:320
  16.7 0.2 shard_map.69
  16.9 0.0 copy-start
  16.9 2.5 %collective-permute-start.6 = (bf16[512,128]{1,0:T(8,128)(2,1)S(1)}, bf16[512,128]{1,0:T(8,128)(2,1)S(1)}, u32[]{:S(2)}, u32[]{:S(2)}) collective-permute-start(bf16[512,128]{1,0:T(8,128)(2,1)S(1)} %get-tuple-element.36), channel_id=1, source_target_pairs={{0,6},{1,25},{2,4},{3,27},{4,2},{5,29},{6,0},{7,31},{8,14},{9,17},... | collective-permute-start | bytes 393224 | tf_op jit(solution)/shard_map/ppermute | solution.py:244
  19.5 0.5 %collective-permute-start.7 = (bf16[512,128]{1,0:T(8,128)(2,1)S(1)}, bf16[512,128]{1,0:T(8,128)(2,1)S(1)}, u32[]{:S(2)}, u32[]{:S(2)}) collective-permute-start(bf16[512,128]{1,0:T(8,128)(2,1)S(1)} %get-tuple-element.37), channel_id=1, source_target_pairs={{0,4},{1,17},{2,6},{3,19},{4,0},{5,21},{6,2},{7,23},{8,12},{9,25},... | collective-permute-start | bytes 393224 | tf_op jit(solution)/shard_map/ppermute | solution.py:244
  20.0 0.5 %collective-permute-start.8 = (bf16[512,128]{1,0:T(8,128)(2,1)S(1)}, bf16[512,128]{1,0:T(8,128)(2,1)S(1)}, u32[]{:S(2)}, u32[]{:S(2)}) collective-permute-start(bf16[512,128]{1,0:T(8,128)(2,1)S(1)} %get-tuple-element.38), channel_id=1, source_target_pairs={{0,2},{1,9},{2,0},{3,11},{4,6},{5,13},{6,4},{7,15},{8,10},{9,1},{1... | collective-permute-start | bytes 393224 | tf_op jit(solution)/shard_map/ppermute | solution.py:244
  20.5 2.4 %collective-permute-done.6.refs_0_ = bf16[512,128]{1,0:T(8,128)(2,1)S(1)} collective-permute-done((bf16[512,128]{1,0:T(8,128)(2,1)S(1)}, bf16[512,128]{1,0:T(8,128)(2,1)S(1)}, u32[]{:S(2)}, u32[]{:S(2)}) %collective-permute-start.6) | collective-permute-done | bytes 131104 | tf_op jit(solution)/shard_map/ppermute | solution.py:244
  22.9 1.6 %collective-permute-done.7.refs_1_ = bf16[512,128]{1,0:T(8,128)(2,1)S(1)} collective-permute-done((bf16[512,128]{1,0:T(8,128)(2,1)S(1)}, bf16[512,128]{1,0:T(8,128)(2,1)S(1)}, u32[]{:S(2)}, u32[]{:S(2)}) %collective-permute-start.7) | collective-permute-done | bytes 131104 | tf_op jit(solution)/shard_map/ppermute | solution.py:244
  24.5 0.5 %collective-permute-done.8.refs_2_ = bf16[512,128]{1,0:T(8,128)(2,1)S(1)} collective-permute-done((bf16[512,128]{1,0:T(8,128)(2,1)S(1)}, bf16[512,128]{1,0:T(8,128)(2,1)S(1)}, u32[]{:S(2)}, u32[]{:S(2)}) %collective-permute-start.8) | collective-permute-done | bytes 131104 | tf_op jit(solution)/shard_map/ppermute | solution.py:244
  25.0 0.1 shard_map.70
  25.1 2.2 %collective-permute-start.9 = (bf16[128,128]{1,0:T(8,128)(2,1)S(1)}, bf16[128,128]{1,0:T(8,128)(2,1)S(1)}, u32[]{:S(2)}, u32[]{:S(2)}) collective-permute-start(bf16[128,128]{1,0:T(8,128)(2,1)S(1)} %get-tuple-element.39), channel_id=1, source_target_pairs={{0,24},{1,7},{2,26},{3,5},{4,28},{5,3},{6,30},{7,1},{8,16},{9,15},... | collective-permute-start | bytes 98312 | tf_op jit(solution)/shard_map/ppermute | solution.py:244
  27.2 0.0 collective-permute-start.10
  27.2 2.3 %collective-permute-start.11 = (bf16[128,128]{1,0:T(8,128)(2,1)S(1)}, bf16[128,128]{1,0:T(8,128)(2,1)S(1)}, u32[]{:S(2)}, u32[]{:S(2)}) collective-permute-start(bf16[128,128]{1,0:T(8,128)(2,1)S(1)} %get-tuple-element.41), channel_id=1, source_target_pairs={{0,8},{1,3},{2,10},{3,1},{4,12},{5,7},{6,14},{7,5},{8,0},{9,11},{1... | collective-permute-start | bytes 98312 | tf_op jit(solution)/shard_map/ppermute | solution.py:244
  29.5 1.3 %collective-permute-done.9.refs_0_ = bf16[128,128]{1,0:T(8,128)(2,1)S(1)} collective-permute-done((bf16[128,128]{1,0:T(8,128)(2,1)S(1)}, bf16[128,128]{1,0:T(8,128)(2,1)S(1)}, u32[]{:S(2)}, u32[]{:S(2)}) %collective-permute-start.9) | collective-permute-done | bytes 32800 | tf_op jit(solution)/shard_map/ppermute | solution.py:244
  30.8 1.4 %collective-permute-done.10.refs_1_ = bf16[128,128]{1,0:T(8,128)(2,1)S(1)} collective-permute-done((bf16[128,128]{1,0:T(8,128)(2,1)S(1)}, bf16[128,128]{1,0:T(8,128)(2,1)S(1)}, u32[]{:S(2)}, u32[]{:S(2)}) %collective-permute-start.10) | collective-permute-done | bytes 32800 | tf_op jit(solution)/shard_map/ppermute | solution.py:244
  32.3 0.0 collective-permute-done.11.refs_2_
  32.3 0.0 copy-done
  32.3 0.7 %shard_map.71 = f32[1,4,4096]{2,1,0:T(4,128)} custom-call(bf16[128,128]{1,0:T(8,128)(2,1)S(1)} %collective-permute-done.9.refs_0_, bf16[128,128]{1,0:T(8,128)(2,1)S(1)} %collective-permute-done.10.refs_1_, bf16[128,128]{1,0:T(8,128)(2,1)S(1)} %collective-permute-done.11.refs_2_, f32[128,128]{1,0:T(8,128)S(1)} %get-tuple-element.42.refs_3_, ...), custom_call_target="tpu_custom_call" | custom-call | tf_op jit(solution)/shard_map/pallas_call | solution.py:24
  (1 shorter events, 0.0 us)
Async XLA Ops:
  0.0 5.0 %collective-permute-start = (bf16[1,4,4096]{2,1,0:T(4,128)(2,1)}, bf16[1,4,4096]{2,1,0:T(4,128)(2,1)S(1)}, u32[]{:S(2)}, u32[]{:S(2)}) collective-permute-start(bf16[1,4,4096]{2,1,0:T(4,128)(2,1)} %refs_0_.1), channel_id=1, source_target_pairs={{0,4},{4,0},{1,5},{5,1},{2,6},{6,2},{3,7},{7,3},{8,12},{12,8},{9,1... | collective-permute-start | bytes 98312 | tf_op jit(solution)/shard_map/ppermute | solution.py:230
  5.1 6.9 %collective-permute-start.3 = (bf16[256,128]{1,0:T(8,128)(2,1)S(1)}, bf16[256,128]{1,0:T(8,128)(2,1)S(1)}, u32[]{:S(2)}, u32[]{:S(2)}) collective-permute-start(bf16[256,128]{1,0:T(8,128)(2,1)S(1)} %shard_map.65.refs_3_), channel_id=1, source_target_pairs={{0,24},{8,16},{16,8},{24,0},{1,25},{9,17},{17,9},{25,1},{2,26},{10... | collective-permute-start | bytes 196616 | tf_op jit(solution)/shard_map/ppermute | solution.py:230
  9.3 5.2 %collective-permute-start.2 = (bf16[256,128]{1,0:T(8,128)(2,1)S(1)}, bf16[256,128]{1,0:T(8,128)(2,1)S(1)}, u32[]{:S(2)}, u32[]{:S(2)}) collective-permute-start(bf16[256,128]{1,0:T(8,128)(2,1)S(1)} %shard_map.65.refs_3_), channel_id=1, source_target_pairs={{0,16},{8,24},{16,0},{24,8},{1,17},{9,25},{17,1},{25,9},{2,18},{10... | collective-permute-start | bytes 196616 | tf_op jit(solution)/shard_map/ppermute | solution.py:230
  9.3 5.2 %collective-permute-start.1 = (bf16[256,128]{1,0:T(8,128)(2,1)S(1)}, bf16[256,128]{1,0:T(8,128)(2,1)S(1)}, u32[]{:S(2)}, u32[]{:S(2)}) collective-permute-start(bf16[256,128]{1,0:T(8,128)(2,1)S(1)} %shard_map.65.refs_3_), channel_id=1, source_target_pairs={{0,8},{8,0},{16,24},{24,16},{1,9},{9,1},{17,25},{25,17},{2,10},{10... | collective-permute-start | bytes 196616 | tf_op jit(solution)/shard_map/ppermute | solution.py:230
  9.9 2.1 %collective-permute-start.4 = (s32[32,128]{1,0:T(8,128)S(1)}, s32[32,128]{1,0:T(8,128)S(1)}, u32[]{:S(2)}, u32[]{:S(2)}) collective-permute-start(s32[32,128]{1,0:T(8,128)S(1)} %get-tuple-element.26), channel_id=1, source_target_pairs={{0,1},{1,0},{2,3},{3,2},{4,5},{5,4},{6,7},{7,6},{8,9},{9,8},{10,11... | collective-permute-start | bytes 49160 | tf_op jit(solution)/shard_map/ppermute | solution.py:303
  15.1 1.6 %collective-permute-start.5 = (bf16[1024,128]{1,0:T(8,128)(2,1)S(1)}, bf16[1024,128]{1,0:T(8,128)(2,1)S(1)}, u32[]{:S(2)}, u32[]{:S(2)}) collective-permute-start(bf16[1024,128]{1,0:T(8,128)(2,1)S(1)} %shard_map.67.ref), channel_id=1, source_target_pairs={{0,1},{1,0},{2,3},{3,2},{4,5},{5,4},{6,7},{7,6},{8,9},{9,8},{10,11... | collective-permute-start | bytes 786440 | tf_op jit(solution)/shard_map/ppermute | solution.py:320
  16.9 15.3 %copy-start = (f32[1,4,4096]{2,1,0:T(4,128)S(1)}, f32[1,4,4096]{2,1,0:T(4,128)}, u32[]{:S(2)}) copy-start(f32[1,4,4096]{2,1,0:T(4,128)} %refs_4_.1) | copy-start | bytes 196612
  16.9 5.9 %collective-permute-start.6 = (bf16[512,128]{1,0:T(8,128)(2,1)S(1)}, bf16[512,128]{1,0:T(8,128)(2,1)S(1)}, u32[]{:S(2)}, u32[]{:S(2)}) collective-permute-start(bf16[512,128]{1,0:T(8,128)(2,1)S(1)} %get-tuple-element.36), channel_id=1, source_target_pairs={{0,6},{1,25},{2,4},{3,27},{4,2},{5,29},{6,0},{7,31},{8,14},{9,17},... | collective-permute-start | bytes 393224 | tf_op jit(solution)/shard_map/ppermute | solution.py:244
  19.5 5.0 %collective-permute-start.7 = (bf16[512,128]{1,0:T(8,128)(2,1)S(1)}, bf16[512,128]{1,0:T(8,128)(2,1)S(1)}, u32[]{:S(2)}, u32[]{:S(2)}) collective-permute-start(bf16[512,128]{1,0:T(8,128)(2,1)S(1)} %get-tuple-element.37), channel_id=1, source_target_pairs={{0,4},{1,17},{2,6},{3,19},{4,0},{5,21},{6,2},{7,23},{8,12},{9,25},... | collective-permute-start | bytes 393224 | tf_op jit(solution)/shard_map/ppermute | solution.py:244
  20.0 5.0 %collective-permute-start.8 = (bf16[512,128]{1,0:T(8,128)(2,1)S(1)}, bf16[512,128]{1,0:T(8,128)(2,1)S(1)}, u32[]{:S(2)}, u32[]{:S(2)}) collective-permute-start(bf16[512,128]{1,0:T(8,128)(2,1)S(1)} %get-tuple-element.38), channel_id=1, source_target_pairs={{0,2},{1,9},{2,0},{3,11},{4,6},{5,13},{6,4},{7,15},{8,10},{9,1},{1... | collective-permute-start | bytes 393224 | tf_op jit(solution)/shard_map/ppermute | solution.py:244
  25.1 5.8 %collective-permute-start.9 = (bf16[128,128]{1,0:T(8,128)(2,1)S(1)}, bf16[128,128]{1,0:T(8,128)(2,1)S(1)}, u32[]{:S(2)}, u32[]{:S(2)}) collective-permute-start(bf16[128,128]{1,0:T(8,128)(2,1)S(1)} %get-tuple-element.39), channel_id=1, source_target_pairs={{0,24},{1,7},{2,26},{3,5},{4,28},{5,3},{6,30},{7,1},{8,16},{9,15},... | collective-permute-start | bytes 98312 | tf_op jit(solution)/shard_map/ppermute | solution.py:244
  27.2 5.1 %collective-permute-start.10 = (bf16[128,128]{1,0:T(8,128)(2,1)S(1)}, bf16[128,128]{1,0:T(8,128)(2,1)S(1)}, u32[]{:S(2)}, u32[]{:S(2)}) collective-permute-start(bf16[128,128]{1,0:T(8,128)(2,1)S(1)} %get-tuple-element.40), channel_id=1, source_target_pairs={{0,16},{1,5},{2,18},{3,7},{4,20},{5,1},{6,22},{7,3},{8,24},{9,13},... | collective-permute-start | bytes 98312 | tf_op jit(solution)/shard_map/ppermute | solution.py:244
  27.2 5.1 %collective-permute-start.11 = (bf16[128,128]{1,0:T(8,128)(2,1)S(1)}, bf16[128,128]{1,0:T(8,128)(2,1)S(1)}, u32[]{:S(2)}, u32[]{:S(2)}) collective-permute-start(bf16[128,128]{1,0:T(8,128)(2,1)S(1)} %get-tuple-element.41), channel_id=1, source_target_pairs={{0,8},{1,3},{2,10},{3,1},{4,12},{5,7},{6,14},{7,5},{8,0},{9,11},{1... | collective-permute-start | bytes 98312 | tf_op jit(solution)/shard_map/ppermute | solution.py:244

commit v9 on v8

--- a/solution.py
+++ b/solution.py
@@ -86,11 +86,13 @@
         to_outer = offset(to_outer, lax.axis_index("outer"), outer)
     to_plane = to_inner * groups + to_group
 
+    back = (lax.axis_index("outer") + outer - dest // inner) % outer
+
     def slot_on(core):
-        plane_first = to_plane * outer + to_outer
         if not opposite:
-            return plane_first * per_col + place % per_col
-        outer_first = to_outer * (inner * groups) + to_plane
+            return (to_plane * outer + to_outer) * per_col + place % per_col
+        plane_first = to_plane * outer + back
+        outer_first = back * (inner * groups) + to_plane
         return jnp.where(core == 0, plane_first, outer_first) * per_col + place % per_col
 
     me = lax.axis_index("core")
@@ -232,15 +234,15 @@
 
 def exchange_crossed(blocks, sizes, outer_core):
     outer, inner, groups, cores = sizes
-    offsets = (
-        list(itertools.product(range(outer), [0], [0], [0]))[1:],
-        list(itertools.product([0], range(inner), range(groups), [0]))[1:],
-    )
+    in_plane = [(0, *by, 0) for by in itertools.product(range(inner), range(groups))]
     pairs = permutes(sizes)
+    line, total = inner * groups * cores, math.prod(sizes)
     arrived = []
-    for i, x in enumerate(blocks):
-        by_core = [pairs[offsets[core != outer_core][i]] for core in range(cores)]
-        both = [by_core[n % cores][n] for n in range(math.prod(sizes))]
+    for i, x in enumerate(blocks, 1):
+        across = pairs[in_plane[i]]
+        both = [
+            (n, (n - i * line) % total) if n % cores == outer_core else across[n] for n in range(total)
+        ]
         arrived.append(lax.ppermute(x, ("outer", "inner", "groups", "core"), both))
     return arrived[::-1]
 

time: 33.2 us -> 32.6 us (0.982)
  waiting for transfers between devices: 12.1 us -> 11 us
  starting transfers between devices: 15.9 us -> 16.4 us
    ppermute x6, waiting for transfers between devices: 7.26 us -> 6.14 us  [exchange_crossed(): arrived.append(lax.ppermute(x, ('outer', 'inner', 'groups', 'core'), both))]
    ppermute x6, starting transfers between devices: 8.01 us -> 8.51 us  [exchange_crossed(): arrived.append(lax.ppermute(x, ('outer', 'inner', 'groups', 'core'), both))]
where the time goes in v9:
time: 32.6 us; the launch traced here: 32.4 us
  starting transfers between devices  16.4 us (50%)
  waiting for transfers between devices  11 us (34%)
  Pallas kernels  3.36 us (10%)
  local copies, waits for them, and re-layouts  1.56 us (5%)
    ppermute x6, starting transfers between devices, exchange_crossed(): arrived.append(lax.ppermute(x, ('outer', 'inner', 'groups', 'core'), both))  8.51 us
    ppermute x4, starting transfers between devices, exchange(): lax.ppermute(x, axes, pairs)  7.78 us
    ppermute x6, waiting for transfers between devices, exchange_crossed(): arrived.append(lax.ppermute(x, ('outer', 'inner', 'groups', 'core'), both))  6.14 us
    ppermute x4, waiting for transfers between devices, exchange(): lax.ppermute(x, axes, pairs)  3.57 us
    pallas_call x8, Pallas kernels, call(): pl.pallas_call(kernel, out_shape=out_shape, in_specs=in_specs, out_specs=...  3.36 us
    reshape x1, local copies, waits for them, and re-layouts, per_device(): tiles.reshape(held * ROWS_OF_TILE, LANES)  1.55 us
    ppermute x1, waiting for transfers between devices, per_device(): other = lax.ppermute(partial, 'core', swap)  1.27 us
  transfers between devices with their start and end apart: 12, of which 8 were waited for; matrix products, arithmetic and copies ran while one was open for 5% of the time, Pallas kernels for 5%

profile of v9, /device:TPU:0, one launch (start us, length us, event | category | flops | bytes accessed | tf_op | source)
XLA Modules:
  0.0 32.4 jit_solution(456393969450243313)
XLA Ops:
  0.0 2.9 %collective-permute-start = (bf16[1,4,4096]{2,1,0:T(4,128)(2,1)}, bf16[1,4,4096]{2,1,0:T(4,128)(2,1)S(1)}, u32[]{:S(2)}, u32[]{:S(2)}) collective-permute-start(bf16[1,4,4096]{2,1,0:T(4,128)(2,1)} %refs_0_.1), channel_id=1, source_target_pairs={{0,4},{4,0},{1,5},{5,1},{2,6},{6,2},{3,7},{7,3},{8,12},{12,8},{9,1... | collective-permute-start | bytes 98312 | tf_op jit(solution)/shard_map/ppermute | solution.py:232
  2.9 1.0 %shard_map.64 = (bf16[128,128]{1,0:T(8,128)(2,1)S(1)}, s32[128,128]{1,0:T(8,128)S(1)}, s32[32,128]{1,0:T(8,128)S(1)}, s32[32,128]{1,0:T(8,128)S(1)}) custom-call(bf16[1,4,4096]{2,1,0:T(4,128)(2,1)} %refs_0_.1, s32[1,128]{1,0:T(1,128)} %bitcast.3, s32[1,32]{1,0:T(1,128)} %bitcast.4, s32[1,32]{1,0:T(1,128)} %bitcast.5), custom_call_target="tpu_custom_call" | custom-call | tf_op jit(solution)/shard_map/pallas_call | solution.py:24
  3.9 1.1 %collective-permute-done.refs_0_ = bf16[1,4,4096]{2,1,0:T(4,128)(2,1)S(1)} collective-permute-done((bf16[1,4,4096]{2,1,0:T(4,128)(2,1)}, bf16[1,4,4096]{2,1,0:T(4,128)(2,1)S(1)}, u32[]{:S(2)}, u32[]{:S(2)}) %collective-permute-start) | collective-permute-done | bytes 32800 | tf_op jit(solution)/shard_map/ppermute | solution.py:232
  5.1 4.2 %collective-permute-start.3 = (bf16[256,128]{1,0:T(8,128)(2,1)S(1)}, bf16[256,128]{1,0:T(8,128)(2,1)S(1)}, u32[]{:S(2)}, u32[]{:S(2)}) collective-permute-start(bf16[256,128]{1,0:T(8,128)(2,1)S(1)} %shard_map.65.refs_3_), channel_id=1, source_target_pairs={{0,24},{8,16},{16,8},{24,0},{1,25},{9,17},{17,9},{25,1},{2,26},{10... | collective-permute-start | bytes 196616 | tf_op jit(solution)/shard_map/ppermute | solution.py:232
  9.3 0.0 collective-permute-start.2
  9.3 0.6 %collective-permute-start.1 = (bf16[256,128]{1,0:T(8,128)(2,1)S(1)}, bf16[256,128]{1,0:T(8,128)(2,1)S(1)}, u32[]{:S(2)}, u32[]{:S(2)}) collective-permute-start(bf16[256,128]{1,0:T(8,128)(2,1)S(1)} %shard_map.65.refs_3_), channel_id=1, source_target_pairs={{0,8},{8,0},{16,24},{24,16},{1,9},{9,1},{17,25},{25,17},{2,10},{10... | collective-permute-start | bytes 196616 | tf_op jit(solution)/shard_map/ppermute | solution.py:232
  9.9 0.0 collective-permute-start.4
  9.9 1.6 %reshape.15.tile_ref = bf16[4096,128]{1,0:T(8,128)(2,1)S(1)} reshape(bf16[128,4096]{1,0:T(8,128)(2,1)} %param.6) | data formatting | bytes 2097152 | tf_op jit(solution)/shard_map/reshape | solution.py:302
  11.5 0.5 %shard_map.66.tile_ref = bf16[2048,256]{1,0:T(8,128)(2,1)S(1)} custom-call(bf16[4096,128]{1,0:T(8,128)(2,1)S(1)} %reshape.15.tile_ref), custom_call_target="tpu_custom_call" | custom-call | tf_op jit(solution)/shard_map/pallas_call | solution.py:24
  12.0 0.0 collective-permute-done.4.slot_ref
  12.0 0.0 collective-permute-done.3.refs_0_
  12.0 2.5 %collective-permute-done.2.refs_1_ = bf16[256,128]{1,0:T(8,128)(2,1)S(1)} collective-permute-done((bf16[256,128]{1,0:T(8,128)(2,1)S(1)}, bf16[256,128]{1,0:T(8,128)(2,1)S(1)}, u32[]{:S(2)}, u32[]{:S(2)}) %collective-permute-start.2) | collective-permute-done | bytes 65568 | tf_op jit(solution)/shard_map/ppermute | solution.py:232
  14.5 0.0 collective-permute-done.1.refs_2_
  14.5 0.6 %shard_map.67.ref = bf16[1024,128]{1,0:T(8,128)(2,1)S(1)} custom-call(s32[128,128]{1,0:T(8,128)S(1)} %get-tuple-element.29.cd_ref, bf16[2048,256]{1,0:T(8,128)(2,1)S(1)} %shard_map.66.tile_ref, bf16[256,128]{1,0:T(8,128)(2,1)S(1)} %collective-permute-done.3.refs_0_, bf16[256,128]{1,0:T(8,128)(2,1)S(1)} %collective-permute-done.2.refs_1_, ...), custom_call_target="tpu_custom_call" | custom-call | tf_op jit(solution)/shard_map/pallas_call | solution.py:24
  15.1 0.1 collective-permute-start.5
  15.2 0.2 shard_map.68.in_ref
  15.4 1.3 %collective-permute-done.5.ref = bf16[1024,128]{1,0:T(8,128)(2,1)S(1)} collective-permute-done((bf16[1024,128]{1,0:T(8,128)(2,1)S(1)}, bf16[1024,128]{1,0:T(8,128)(2,1)S(1)}, u32[]{:S(2)}, u32[]{:S(2)}) %collective-permute-start.5) | collective-permute-done | bytes 262176 | tf_op jit(solution)/shard_map/ppermute | solution.py:322
  16.7 0.2 shard_map.69
  16.9 0.0 copy-start
  16.9 2.5 %collective-permute-start.6 = (bf16[512,128]{1,0:T(8,128)(2,1)S(1)}, bf16[512,128]{1,0:T(8,128)(2,1)S(1)}, u32[]{:S(2)}, u32[]{:S(2)}) collective-permute-start(bf16[512,128]{1,0:T(8,128)(2,1)S(1)} %get-tuple-element.36), channel_id=1, source_target_pairs={{0,6},{1,9},{2,4},{3,11},{4,2},{5,13},{6,0},{7,15},{8,14},{9,17},{... | collective-permute-start | bytes 393224 | tf_op jit(solution)/shard_map/ppermute | solution.py:246
  19.5 0.5 %collective-permute-start.7 = (bf16[512,128]{1,0:T(8,128)(2,1)S(1)}, bf16[512,128]{1,0:T(8,128)(2,1)S(1)}, u32[]{:S(2)}, u32[]{:S(2)}) collective-permute-start(bf16[512,128]{1,0:T(8,128)(2,1)S(1)} %get-tuple-element.37), channel_id=1, source_target_pairs={{0,4},{1,17},{2,6},{3,19},{4,0},{5,21},{6,2},{7,23},{8,12},{9,25},... | collective-permute-start | bytes 393224 | tf_op jit(solution)/shard_map/ppermute | solution.py:246
  20.0 0.5 %collective-permute-start.8 = (bf16[512,128]{1,0:T(8,128)(2,1)S(1)}, bf16[512,128]{1,0:T(8,128)(2,1)S(1)}, u32[]{:S(2)}, u32[]{:S(2)}) collective-permute-start(bf16[512,128]{1,0:T(8,128)(2,1)S(1)} %get-tuple-element.38), channel_id=1, source_target_pairs={{0,2},{1,25},{2,0},{3,27},{4,6},{5,29},{6,4},{7,31},{8,10},{9,1},{... | collective-permute-start | bytes 393224 | tf_op jit(solution)/shard_map/ppermute | solution.py:246
  20.5 2.4 %collective-permute-done.6.refs_0_ = bf16[512,128]{1,0:T(8,128)(2,1)S(1)} collective-permute-done((bf16[512,128]{1,0:T(8,128)(2,1)S(1)}, bf16[512,128]{1,0:T(8,128)(2,1)S(1)}, u32[]{:S(2)}, u32[]{:S(2)}) %collective-permute-start.6) | collective-permute-done | bytes 131104 | tf_op jit(solution)/shard_map/ppermute | solution.py:246
  22.8 1.6 %collective-permute-done.7.refs_1_ = bf16[512,128]{1,0:T(8,128)(2,1)S(1)} collective-permute-done((bf16[512,128]{1,0:T(8,128)(2,1)S(1)}, bf16[512,128]{1,0:T(8,128)(2,1)S(1)}, u32[]{:S(2)}, u32[]{:S(2)}) %collective-permute-start.7) | collective-permute-done | bytes 131104 | tf_op jit(solution)/shard_map/ppermute | solution.py:246
  24.4 0.5 %collective-permute-done.8.refs_2_ = bf16[512,128]{1,0:T(8,128)(2,1)S(1)} collective-permute-done((bf16[512,128]{1,0:T(8,128)(2,1)S(1)}, bf16[512,128]{1,0:T(8,128)(2,1)S(1)}, u32[]{:S(2)}, u32[]{:S(2)}) %collective-permute-start.8) | collective-permute-done | bytes 131104 | tf_op jit(solution)/shard_map/ppermute | solution.py:246
  25.0 0.1 shard_map.70
  25.0 0.6 %collective-permute-start.9 = (bf16[128,128]{1,0:T(8,128)(2,1)S(1)}, bf16[128,128]{1,0:T(8,128)(2,1)S(1)}, u32[]{:S(2)}, u32[]{:S(2)}) collective-permute-start(bf16[128,128]{1,0:T(8,128)(2,1)S(1)} %get-tuple-element.39), channel_id=1, source_target_pairs={{0,8},{1,7},{2,10},{3,5},{4,12},{5,3},{6,14},{7,1},{8,16},{9,15},{... | collective-permute-start | bytes 98312 | tf_op jit(solution)/shard_map/ppermute | solution.py:246
  25.6 2.1 %collective-permute-start.10 = (bf16[128,128]{1,0:T(8,128)(2,1)S(1)}, bf16[128,128]{1,0:T(8,128)(2,1)S(1)}, u32[]{:S(2)}, u32[]{:S(2)}) collective-permute-start(bf16[128,128]{1,0:T(8,128)(2,1)S(1)} %get-tuple-element.40), channel_id=1, source_target_pairs={{0,16},{1,5},{2,18},{3,7},{4,20},{5,1},{6,22},{7,3},{8,24},{9,13},... | collective-permute-start | bytes 98312 | tf_op jit(solution)/shard_map/ppermute | solution.py:246
  27.7 2.3 %collective-permute-start.11 = (bf16[128,128]{1,0:T(8,128)(2,1)S(1)}, bf16[128,128]{1,0:T(8,128)(2,1)S(1)}, u32[]{:S(2)}, u32[]{:S(2)}) collective-permute-start(bf16[128,128]{1,0:T(8,128)(2,1)S(1)} %get-tuple-element.41), channel_id=1, source_target_pairs={{0,24},{1,3},{2,26},{3,1},{4,28},{5,7},{6,30},{7,5},{8,0},{9,11},{... | collective-permute-start | bytes 98312 | tf_op jit(solution)/shard_map/ppermute | solution.py:246
  30.0 0.8 %collective-permute-done.9.refs_0_ = bf16[128,128]{1,0:T(8,128)(2,1)S(1)} collective-permute-done((bf16[128,128]{1,0:T(8,128)(2,1)S(1)}, bf16[128,128]{1,0:T(8,128)(2,1)S(1)}, u32[]{:S(2)}, u32[]{:S(2)}) %collective-permute-start.9) | collective-permute-done | bytes 32800 | tf_op jit(solution)/shard_map/ppermute | solution.py:246
  30.8 0.0 collective-permute-done.10.refs_1_
  30.8 0.9 %collective-permute-done.11.refs_2_ = bf16[128,128]{1,0:T(8,128)(2,1)S(1)} collective-permute-done((bf16[128,128]{1,0:T(8,128)(2,1)S(1)}, bf16[128,128]{1,0:T(8,128)(2,1)S(1)}, u32[]{:S(2)}, u32[]{:S(2)}) %collective-permute-start.11) | collective-permute-done | bytes 32800 | tf_op jit(solution)/shard_map/ppermute | solution.py:246
  31.7 0.0 copy-done
  31.7 0.7 %shard_map.71 = f32[1,4,4096]{2,1,0:T(4,128)} custom-call(bf16[128,128]{1,0:T(8,128)(2,1)S(1)} %collective-permute-done.9.refs_0_, bf16[128,128]{1,0:T(8,128)(2,1)S(1)} %collective-permute-done.10.refs_1_, bf16[128,128]{1,0:T(8,128)(2,1)S(1)} %collective-permute-done.11.refs_2_, f32[128,128]{1,0:T(8,128)S(1)} %get-tuple-element.42.refs_3_, ...), custom_call_target="tpu_custom_call" | custom-call | tf_op jit(solution)/shard_map/pallas_call | solution.py:24
  (1 shorter events, 0.0 us)
Async XLA Ops:
  0.0 5.0 %collective-permute-start = (bf16[1,4,4096]{2,1,0:T(4,128)(2,1)}, bf16[1,4,4096]{2,1,0:T(4,128)(2,1)S(1)}, u32[]{:S(2)}, u32[]{:S(2)}) collective-permute-start(bf16[1,4,4096]{2,1,0:T(4,128)(2,1)} %refs_0_.1), channel_id=1, source_target_pairs={{0,4},{4,0},{1,5},{5,1},{2,6},{6,2},{3,7},{7,3},{8,12},{12,8},{9,1... | collective-permute-start | bytes 98312 | tf_op jit(solution)/shard_map/ppermute | solution.py:232
  5.1 6.9 %collective-permute-start.3 = (bf16[256,128]{1,0:T(8,128)(2,1)S(1)}, bf16[256,128]{1,0:T(8,128)(2,1)S(1)}, u32[]{:S(2)}, u32[]{:S(2)}) collective-permute-start(bf16[256,128]{1,0:T(8,128)(2,1)S(1)} %shard_map.65.refs_3_), channel_id=1, source_target_pairs={{0,24},{8,16},{16,8},{24,0},{1,25},{9,17},{17,9},{25,1},{2,26},{10... | collective-permute-start | bytes 196616 | tf_op jit(solution)/shard_map/ppermute | solution.py:232
  9.3 5.2 %collective-permute-start.2 = (bf16[256,128]{1,0:T(8,128)(2,1)S(1)}, bf16[256,128]{1,0:T(8,128)(2,1)S(1)}, u32[]{:S(2)}, u32[]{:S(2)}) collective-permute-start(bf16[256,128]{1,0:T(8,128)(2,1)S(1)} %shard_map.65.refs_3_), channel_id=1, source_target_pairs={{0,16},{8,24},{16,0},{24,8},{1,17},{9,25},{17,1},{25,9},{2,18},{10... | collective-permute-start | bytes 196616 | tf_op jit(solution)/shard_map/ppermute | solution.py:232
  9.3 5.2 %collective-permute-start.1 = (bf16[256,128]{1,0:T(8,128)(2,1)S(1)}, bf16[256,128]{1,0:T(8,128)(2,1)S(1)}, u32[]{:S(2)}, u32[]{:S(2)}) collective-permute-start(bf16[256,128]{1,0:T(8,128)(2,1)S(1)} %shard_map.65.refs_3_), channel_id=1, source_target_pairs={{0,8},{8,0},{16,24},{24,16},{1,9},{9,1},{17,25},{25,17},{2,10},{10... | collective-permute-start | bytes 196616 | tf_op jit(solution)/shard_map/ppermute | solution.py:232
  9.9 2.1 %collective-permute-start.4 = (s32[32,128]{1,0:T(8,128)S(1)}, s32[32,128]{1,0:T(8,128)S(1)}, u32[]{:S(2)}, u32[]{:S(2)}) collective-permute-start(s32[32,128]{1,0:T(8,128)S(1)} %get-tuple-element.26), channel_id=1, source_target_pairs={{0,1},{1,0},{2,3},{3,2},{4,5},{5,4},{6,7},{7,6},{8,9},{9,8},{10,11... | collective-permute-start | bytes 49160 | tf_op jit(solution)/shard_map/ppermute | solution.py:305
  15.1 1.6 %collective-permute-start.5 = (bf16[1024,128]{1,0:T(8,128)(2,1)S(1)}, bf16[1024,128]{1,0:T(8,128)(2,1)S(1)}, u32[]{:S(2)}, u32[]{:S(2)}) collective-permute-start(bf16[1024,128]{1,0:T(8,128)(2,1)S(1)} %shard_map.67.ref), channel_id=1, source_target_pairs={{0,1},{1,0},{2,3},{3,2},{4,5},{5,4},{6,7},{7,6},{8,9},{9,8},{10,11... | collective-permute-start | bytes 786440 | tf_op jit(solution)/shard_map/ppermute | solution.py:322
  16.9 14.7 %copy-start = (f32[1,4,4096]{2,1,0:T(4,128)S(1)}, f32[1,4,4096]{2,1,0:T(4,128)}, u32[]{:S(2)}) copy-start(f32[1,4,4096]{2,1,0:T(4,128)} %refs_4_.1) | copy-start | bytes 196612
  16.9 5.9 %collective-permute-start.6 = (bf16[512,128]{1,0:T(8,128)(2,1)S(1)}, bf16[512,128]{1,0:T(8,128)(2,1)S(1)}, u32[]{:S(2)}, u32[]{:S(2)}) collective-permute-start(bf16[512,128]{1,0:T(8,128)(2,1)S(1)} %get-tuple-element.36), channel_id=1, source_target_pairs={{0,6},{1,9},{2,4},{3,11},{4,2},{5,13},{6,0},{7,15},{8,14},{9,17},{... | collective-permute-start | bytes 393224 | tf_op jit(solution)/shard_map/ppermute | solution.py:246
  19.5 5.0 %collective-permute-start.7 = (bf16[512,128]{1,0:T(8,128)(2,1)S(1)}, bf16[512,128]{1,0:T(8,128)(2,1)S(1)}, u32[]{:S(2)}, u32[]{:S(2)}) collective-permute-start(bf16[512,128]{1,0:T(8,128)(2,1)S(1)} %get-tuple-element.37), channel_id=1, source_target_pairs={{0,4},{1,17},{2,6},{3,19},{4,0},{5,21},{6,2},{7,23},{8,12},{9,25},... | collective-permute-start | bytes 393224 | tf_op jit(solution)/shard_map/ppermute | solution.py:246
  20.0 5.0 %collective-permute-start.8 = (bf16[512,128]{1,0:T(8,128)(2,1)S(1)}, bf16[512,128]{1,0:T(8,128)(2,1)S(1)}, u32[]{:S(2)}, u32[]{:S(2)}) collective-permute-start(bf16[512,128]{1,0:T(8,128)(2,1)S(1)} %get-tuple-element.38), channel_id=1, source_target_pairs={{0,2},{1,25},{2,0},{3,27},{4,6},{5,29},{6,4},{7,31},{8,10},{9,1},{... | collective-permute-start | bytes 393224 | tf_op jit(solution)/shard_map/ppermute | solution.py:246
  25.0 5.8 %collective-permute-start.9 = (bf16[128,128]{1,0:T(8,128)(2,1)S(1)}, bf16[128,128]{1,0:T(8,128)(2,1)S(1)}, u32[]{:S(2)}, u32[]{:S(2)}) collective-permute-start(bf16[128,128]{1,0:T(8,128)(2,1)S(1)} %get-tuple-element.39), channel_id=1, source_target_pairs={{0,8},{1,7},{2,10},{3,5},{4,12},{5,3},{6,14},{7,1},{8,16},{9,15},{... | collective-permute-start | bytes 98312 | tf_op jit(solution)/shard_map/ppermute | solution.py:246
  25.6 5.2 %collective-permute-start.10 = (bf16[128,128]{1,0:T(8,128)(2,1)S(1)}, bf16[128,128]{1,0:T(8,128)(2,1)S(1)}, u32[]{:S(2)}, u32[]{:S(2)}) collective-permute-start(bf16[128,128]{1,0:T(8,128)(2,1)S(1)} %get-tuple-element.40), channel_id=1, source_target_pairs={{0,16},{1,5},{2,18},{3,7},{4,20},{5,1},{6,22},{7,3},{8,24},{9,13},... | collective-permute-start | bytes 98312 | tf_op jit(solution)/shard_map/ppermute | solution.py:246
  27.7 3.9 %collective-permute-start.11 = (bf16[128,128]{1,0:T(8,128)(2,1)S(1)}, bf16[128,128]{1,0:T(8,128)(2,1)S(1)}, u32[]{:S(2)}, u32[]{:S(2)}) collective-permute-start(bf16[128,128]{1,0:T(8,128)(2,1)S(1)} %get-tuple-element.41), channel_id=1, source_target_pairs={{0,24},{1,3},{2,26},{3,1},{4,28},{5,7},{6,30},{7,5},{8,0},{9,11},{... | collective-permute-start | bytes 98312 | tf_op jit(solution)/shard_map/ppermute | solution.py:246

commit v10 on v9

--- a/solution.py
+++ b/solution.py
@@ -145,13 +145,14 @@
 
 
 def partial_kernel(cd_ref, tile_ref, *refs):
-    in_refs, (out_ref, amp_ref) = refs[:-2], refs[-2:]
+    in_refs, (first_ref, second_ref, amp_ref) = refs[:-3], refs[-3:]
     low = low_lanes()
     me = lax.axis_index("outer")
     size = in_refs[0].shape[0]
     for by, in_ref in enumerate(reversed(in_refs)):
         amp_ref[tile_rows(source(by, me, len(in_refs)) * size, size), :] = in_ref[...]
-    for q in range(out_ref.shape[0] // ROWS_OF_TILE):
+    half = first_ref.shape[0] // ROWS_OF_TILE
+    for q in range(2 * half):
         amps = []
         for t in range(0, PER_PART, 2):
             k = q * PER_PART + t
@@ -166,23 +167,29 @@
             preferred_element_type=jnp.float32,
         )
         packed = jnp.concatenate([value[:ROWS_OF_TILE], value[ROWS_OF_TILE:]], axis=1)
-        out_ref[pl.ds(q * ROWS_OF_TILE, ROWS_OF_TILE), :] = packed.astype(jnp.bfloat16)
-
-
-def add_tiles(slot_ref, ref, sum_ref):
+        out_ref = first_ref if q < half else second_ref
+        out_ref[pl.ds(q % half * ROWS_OF_TILE, ROWS_OF_TILE), :] = packed.astype(jnp.bfloat16)
+
+
+def add_tiles(slot_ref, ref, sum_ref, start=0):
     for q in range(ref.shape[0] // ROWS_OF_TILE):
-        at = tile_rows(slot_ref[q, 0])
+        at = tile_rows(slot_ref[start + q, 0])
         sum_ref[at, :] += ref[pl.ds(q * ROWS_OF_TILE, ROWS_OF_TILE), :].astype(jnp.float32)
 
 
-def own_kernel(slot_ref, ref, sum_ref):
+def own_kernel(slot_ref, first_ref, second_ref, sum_ref):
     sum_ref[...] = jnp.zeros_like(sum_ref)
+    add_tiles(slot_ref, first_ref, sum_ref)
+    add_tiles(slot_ref, second_ref, sum_ref, first_ref.shape[0] // ROWS_OF_TILE)
+
+
+def half_kernel(slot_ref, ref, in_ref, sum_ref):
     add_tiles(slot_ref, ref, sum_ref)
 
 
 def other_kernel(slot_ref, ref, in_ref, *refs):
     out_refs, sum_ref = refs[:-1], refs[-1]
-    add_tiles(slot_ref, ref, sum_ref)
+    add_tiles(slot_ref, ref, sum_ref, ref.shape[0] // ROWS_OF_TILE)
     for block, out_ref in enumerate(out_refs):
         size = out_ref.shape[0]
         out_ref[...] = sum_ref[pl.ds((block + 1) * size, size), :].astype(jnp.bfloat16)
@@ -312,23 +319,24 @@
     sources = gathered[::-1] + [near] if by_permutes else gathered
     partial = call(
         partial_kernel,
-        shape((parts * ROWS_OF_TILE, LANES), bf16),
+        [shape((parts // 2 * ROWS_OF_TILE, LANES), bf16)] * 2,
         [VMEM] * (2 + len(sources)),
         first_cd,
         paired,
         *sources,
         scratch=[pltpu.VMEM((rows * shard_rows, LANES), bf16)],
     )
-    other = lax.ppermute(partial, "core", swap)
+    other = [lax.ppermute(x, "core", swap) for x in partial]
     summed = shape(((slots + 1) * ROWS_OF_TILE, LANES), f32)
-    own_sum = call(own_kernel, summed, [VMEM, VMEM], own_slot, partial)
+    own_sum = call(own_kernel, summed, [VMEM] * 3, own_slot, *partial)
+    own_sum = call(half_kernel, summed, [VMEM] * 3, other_slot, other[0], own_sum, aliases={2: 0})
     block = slots // plane * ROWS_OF_TILE
     *leaving, own_sum = call(
         other_kernel,
         [shape((block, LANES), bf16)] * (plane - 1) + [summed],
         [VMEM, VMEM, VMEM],
         other_slot,
-        other,
+        other[1],
         own_sum,
         aliases={2: plane - 1},
     )

time: 32.6 us -> 32.5 us (level)
  waiting for transfers between devices: 11 us -> 10.4 us
  starting transfers between devices: 16.4 us -> 16.9 us
    ppermute x1 -> x2, waiting for transfers between devices: 1.27 us -> 0.69 us  [per_device(): other = [lax.ppermute(x, 'core', swap) for x in partial]]
    ppermute x1 -> x2, starting transfers between devices: 0.07 us -> 0.57 us  [per_device(): other = [lax.ppermute(x, 'core', swap) for x in partial]]
    pallas_call x8 -> x9, Pallas kernels: 3.36 us -> 3.39 us  [call(): pl.pallas_call(kernel, out_shape=out_shape, in_specs=in_specs, out_specs=...]
  transfers between devices with their start and end apart: 12 -> 13, of which waited for: 8 -> 9; matrix products, arithmetic and copies ran while one was open for 5% -> 5% of each run, Pallas kernels for 5% -> 6%
where the time goes in v10:
time: 32.5 us; the launch traced here: 32.3 us
  starting transfers between devices  16.9 us (52%)
  waiting for transfers between devices  10.4 us (32%)
  Pallas kernels  3.39 us (10%)
  local copies, waits for them, and re-layouts  1.56 us (5%)
    ppermute x6, starting transfers between devices, exchange_crossed(): arrived.append(lax.ppermute(x, ('outer', 'inner', 'groups', 'core'), both))  8.51 us
    ppermute x4, starting transfers between devices, exchange(): lax.ppermute(x, axes, pairs)  7.78 us
    ppermute x6, waiting for transfers between devices, exchange_crossed(): arrived.append(lax.ppermute(x, ('outer', 'inner', 'groups', 'core'), both))  6.11 us
    ppermute x4, waiting for transfers between devices, exchange(): lax.ppermute(x, axes, pairs)  3.57 us
    pallas_call x9, Pallas kernels, call(): pl.pallas_call(kernel, out_shape=out_shape, in_specs=in_specs, out_specs=...  3.39 us
    reshape x1, local copies, waits for them, and re-layouts, per_device(): tiles.reshape(held * ROWS_OF_TILE, LANES)  1.55 us
    ppermute x2, waiting for transfers between devices, per_device(): other = [lax.ppermute(x, 'core', swap) for x in partial]  0.69 us
  transfers between devices with their start and end apart: 13, of which 9 were waited for; matrix products, arithmetic and copies ran while one was open for 5% of the time, Pallas kernels for 6%

profile of v10, /device:TPU:0, one launch (start us, length us, event | category | flops | bytes accessed | tf_op | source)
XLA Modules:
  0.0 32.3 jit_solution(15931328758011281051)
XLA Ops:
  0.0 2.9 %collective-permute-start = (bf16[1,4,4096]{2,1,0:T(4,128)(2,1)}, bf16[1,4,4096]{2,1,0:T(4,128)(2,1)S(1)}, u32[]{:S(2)}, u32[]{:S(2)}) collective-permute-start(bf16[1,4,4096]{2,1,0:T(4,128)(2,1)} %refs_0_.1), channel_id=1, source_target_pairs={{0,4},{4,0},{1,5},{5,1},{2,6},{6,2},{3,7},{7,3},{8,12},{12,8},{9,1... | collective-permute-start | bytes 98312 | tf_op jit(solution)/shard_map/ppermute | solution.py:239
  2.9 1.0 %shard_map.64 = (bf16[128,128]{1,0:T(8,128)(2,1)S(1)}, s32[128,128]{1,0:T(8,128)S(1)}, s32[32,128]{1,0:T(8,128)S(1)}, s32[32,128]{1,0:T(8,128)S(1)}) custom-call(bf16[1,4,4096]{2,1,0:T(4,128)(2,1)} %refs_0_.1, s32[1,128]{1,0:T(1,128)} %bitcast.3, s32[1,32]{1,0:T(1,128)} %bitcast.4, s32[1,32]{1,0:T(1,128)} %bitcast.5), custom_call_target="tpu_custom_call" | custom-call | tf_op jit(solution)/shard_map/pallas_call | solution.py:24
  3.9 1.1 %collective-permute-done.refs_0_ = bf16[1,4,4096]{2,1,0:T(4,128)(2,1)S(1)} collective-permute-done((bf16[1,4,4096]{2,1,0:T(4,128)(2,1)}, bf16[1,4,4096]{2,1,0:T(4,128)(2,1)S(1)}, u32[]{:S(2)}, u32[]{:S(2)}) %collective-permute-start) | collective-permute-done | bytes 32800 | tf_op jit(solution)/shard_map/ppermute | solution.py:239
  5.1 4.2 %collective-permute-start.3 = (bf16[256,128]{1,0:T(8,128)(2,1)S(1)}, bf16[256,128]{1,0:T(8,128)(2,1)S(1)}, u32[]{:S(2)}, u32[]{:S(2)}) collective-permute-start(bf16[256,128]{1,0:T(8,128)(2,1)S(1)} %shard_map.65.refs_3_), channel_id=1, source_target_pairs={{0,24},{8,16},{16,8},{24,0},{1,25},{9,17},{17,9},{25,1},{2,26},{10... | collective-permute-start | bytes 196616 | tf_op jit(solution)/shard_map/ppermute | solution.py:239
  9.3 0.0 collective-permute-start.2
  9.3 0.6 %collective-permute-start.1 = (bf16[256,128]{1,0:T(8,128)(2,1)S(1)}, bf16[256,128]{1,0:T(8,128)(2,1)S(1)}, u32[]{:S(2)}, u32[]{:S(2)}) collective-permute-start(bf16[256,128]{1,0:T(8,128)(2,1)S(1)} %shard_map.65.refs_3_), channel_id=1, source_target_pairs={{0,8},{8,0},{16,24},{24,16},{1,9},{9,1},{17,25},{25,17},{2,10},{10... | collective-permute-start | bytes 196616 | tf_op jit(solution)/shard_map/ppermute | solution.py:239
  9.9 0.0 collective-permute-start.4
  9.9 1.6 %reshape.15.tile_ref = bf16[4096,128]{1,0:T(8,128)(2,1)S(1)} reshape(bf16[128,4096]{1,0:T(8,128)(2,1)} %param.6) | data formatting | bytes 2097152 | tf_op jit(solution)/shard_map/reshape | solution.py:309
  11.5 0.5 %shard_map.66.tile_ref = bf16[2048,256]{1,0:T(8,128)(2,1)S(1)} custom-call(bf16[4096,128]{1,0:T(8,128)(2,1)S(1)} %reshape.15.tile_ref), custom_call_target="tpu_custom_call" | custom-call | tf_op jit(solution)/shard_map/pallas_call | solution.py:24
  12.0 0.0 collective-permute-done.4.slot_ref
  12.0 0.0 collective-permute-done.3.refs_0_
  12.0 2.5 %collective-permute-done.2.refs_1_ = bf16[256,128]{1,0:T(8,128)(2,1)S(1)} collective-permute-done((bf16[256,128]{1,0:T(8,128)(2,1)S(1)}, bf16[256,128]{1,0:T(8,128)(2,1)S(1)}, u32[]{:S(2)}, u32[]{:S(2)}) %collective-permute-start.2) | collective-permute-done | bytes 65568 | tf_op jit(solution)/shard_map/ppermute | solution.py:239
  14.5 0.0 collective-permute-done.1.refs_2_
  14.5 0.6 %shard_map.67 = (bf16[512,128]{1,0:T(8,128)(2,1)S(1)}, bf16[512,128]{1,0:T(8,128)(2,1)S(1)}) custom-call(s32[128,128]{1,0:T(8,128)S(1)} %get-tuple-element.31.cd_ref, bf16[2048,256]{1,0:T(8,128)(2,1)S(1)} %shard_map.66.tile_ref, bf16[256,128]{1,0:T(8,128)(2,1)S(1)} %collective-permute-done.3.refs_0_, bf16[256,128]{1,0:T(8,128)(2,1)S(1)} %collective-permute-done.2.refs_1_, ...), custom_call_target="tpu_custom_call" | custom-call | tf_op jit(solution)/shard_map/pallas_call | solution.py:24
  15.1 0.1 collective-permute-start.6
  15.2 0.5 %collective-permute-start.5 = (bf16[512,128]{1,0:T(8,128)(2,1)S(1)}, bf16[512,128]{1,0:T(8,128)(2,1)S(1)}, u32[]{:S(2)}, u32[]{:S(2)}) collective-permute-start(bf16[512,128]{1,0:T(8,128)(2,1)S(1)} %get-tuple-element.36.second_ref), channel_id=1, source_target_pairs={{0,1},{1,0},{2,3},{3,2},{4,5},{5,4},{6,7},{7,6},{8,9},{9,8},{10,11... | collective-permute-start | bytes 393224 | tf_op jit(solution)/shard_map/ppermute | solution.py:329
  15.7 0.2 shard_map.68.in_ref
  15.9 0.6 %collective-permute-done.6.ref = bf16[512,128]{1,0:T(8,128)(2,1)S(1)} collective-permute-done((bf16[512,128]{1,0:T(8,128)(2,1)S(1)}, bf16[512,128]{1,0:T(8,128)(2,1)S(1)}, u32[]{:S(2)}, u32[]{:S(2)}) %collective-permute-start.6) | collective-permute-done | bytes 131104 | tf_op jit(solution)/shard_map/ppermute | solution.py:329
  16.5 0.1 shard_map.69.in_ref
  16.6 0.0 copy-start
  16.6 0.1 collective-permute-done.5.ref
  16.7 0.1 shard_map.70
  16.9 2.5 %collective-permute-start.7 = (bf16[512,128]{1,0:T(8,128)(2,1)S(1)}, bf16[512,128]{1,0:T(8,128)(2,1)S(1)}, u32[]{:S(2)}, u32[]{:S(2)}) collective-permute-start(bf16[512,128]{1,0:T(8,128)(2,1)S(1)} %get-tuple-element.40), channel_id=1, source_target_pairs={{0,6},{1,9},{2,4},{3,11},{4,2},{5,13},{6,0},{7,15},{8,14},{9,17},{... | collective-permute-start | bytes 393224 | tf_op jit(solution)/shard_map/ppermute | solution.py:253
  19.4 0.5 %collective-permute-start.8 = (bf16[512,128]{1,0:T(8,128)(2,1)S(1)}, bf16[512,128]{1,0:T(8,128)(2,1)S(1)}, u32[]{:S(2)}, u32[]{:S(2)}) collective-permute-start(bf16[512,128]{1,0:T(8,128)(2,1)S(1)} %get-tuple-element.41), channel_id=1, source_target_pairs={{0,4},{1,17},{2,6},{3,19},{4,0},{5,21},{6,2},{7,23},{8,12},{9,25},... | collective-permute-start | bytes 393224 | tf_op jit(solution)/shard_map/ppermute | solution.py:253
  19.9 0.5 %collective-permute-start.9 = (bf16[512,128]{1,0:T(8,128)(2,1)S(1)}, bf16[512,128]{1,0:T(8,128)(2,1)S(1)}, u32[]{:S(2)}, u32[]{:S(2)}) collective-permute-start(bf16[512,128]{1,0:T(8,128)(2,1)S(1)} %get-tuple-element.42), channel_id=1, source_target_pairs={{0,2},{1,25},{2,0},{3,27},{4,6},{5,29},{6,4},{7,31},{8,10},{9,1},{... | collective-permute-start | bytes 393224 | tf_op jit(solution)/shard_map/ppermute | solution.py:253
  20.4 2.4 %collective-permute-done.7.refs_0_ = bf16[512,128]{1,0:T(8,128)(2,1)S(1)} collective-permute-done((bf16[512,128]{1,0:T(8,128)(2,1)S(1)}, bf16[512,128]{1,0:T(8,128)(2,1)S(1)}, u32[]{:S(2)}, u32[]{:S(2)}) %collective-permute-start.7) | collective-permute-done | bytes 131104 | tf_op jit(solution)/shard_map/ppermute | solution.py:253
  22.8 1.5 %collective-permute-done.8.refs_1_ = bf16[512,128]{1,0:T(8,128)(2,1)S(1)} collective-permute-done((bf16[512,128]{1,0:T(8,128)(2,1)S(1)}, bf16[512,128]{1,0:T(8,128)(2,1)S(1)}, u32[]{:S(2)}, u32[]{:S(2)}) %collective-permute-start.8) | collective-permute-done | bytes 131104 | tf_op jit(solution)/shard_map/ppermute | solution.py:253
  24.3 0.5 %collective-permute-done.9.refs_2_ = bf16[512,128]{1,0:T(8,128)(2,1)S(1)} collective-permute-done((bf16[512,128]{1,0:T(8,128)(2,1)S(1)}, bf16[512,128]{1,0:T(8,128)(2,1)S(1)}, u32[]{:S(2)}, u32[]{:S(2)}) %collective-permute-start.9) | collective-permute-done | bytes 131104 | tf_op jit(solution)/shard_map/ppermute | solution.py:253
  24.9 0.1 shard_map.71
  24.9 0.6 %collective-permute-start.10 = (bf16[128,128]{1,0:T(8,128)(2,1)S(1)}, bf16[128,128]{1,0:T(8,128)(2,1)S(1)}, u32[]{:S(2)}, u32[]{:S(2)}) collective-permute-start(bf16[128,128]{1,0:T(8,128)(2,1)S(1)} %get-tuple-element.43), channel_id=1, source_target_pairs={{0,8},{1,7},{2,10},{3,5},{4,12},{5,3},{6,14},{7,1},{8,16},{9,15},{... | collective-permute-start | bytes 98312 | tf_op jit(solution)/shard_map/ppermute | solution.py:253
  25.5 2.1 %collective-permute-start.11 = (bf16[128,128]{1,0:T(8,128)(2,1)S(1)}, bf16[128,128]{1,0:T(8,128)(2,1)S(1)}, u32[]{:S(2)}, u32[]{:S(2)}) collective-permute-start(bf16[128,128]{1,0:T(8,128)(2,1)S(1)} %get-tuple-element.44), channel_id=1, source_target_pairs={{0,16},{1,5},{2,18},{3,7},{4,20},{5,1},{6,22},{7,3},{8,24},{9,13},... | collective-permute-start | bytes 98312 | tf_op jit(solution)/shard_map/ppermute | solution.py:253
  27.6 2.3 %collective-permute-start.12 = (bf16[128,128]{1,0:T(8,128)(2,1)S(1)}, bf16[128,128]{1,0:T(8,128)(2,1)S(1)}, u32[]{:S(2)}, u32[]{:S(2)}) collective-permute-start(bf16[128,128]{1,0:T(8,128)(2,1)S(1)} %get-tuple-element.45), channel_id=1, source_target_pairs={{0,24},{1,3},{2,26},{3,1},{4,28},{5,7},{6,30},{7,5},{8,0},{9,11},{... | collective-permute-start | bytes 98312 | tf_op jit(solution)/shard_map/ppermute | solution.py:253
  29.9 0.8 %collective-permute-done.10.refs_0_ = bf16[128,128]{1,0:T(8,128)(2,1)S(1)} collective-permute-done((bf16[128,128]{1,0:T(8,128)(2,1)S(1)}, bf16[128,128]{1,0:T(8,128)(2,1)S(1)}, u32[]{:S(2)}, u32[]{:S(2)}) %collective-permute-start.10) | collective-permute-done | bytes 32800 | tf_op jit(solution)/shard_map/ppermute | solution.py:253
  30.7 0.0 collective-permute-done.11.refs_1_
  30.7 0.9 %collective-permute-done.12.refs_2_ = bf16[128,128]{1,0:T(8,128)(2,1)S(1)} collective-permute-done((bf16[128,128]{1,0:T(8,128)(2,1)S(1)}, bf16[128,128]{1,0:T(8,128)(2,1)S(1)}, u32[]{:S(2)}, u32[]{:S(2)}) %collective-permute-start.12) | collective-permute-done | bytes 32800 | tf_op jit(solution)/shard_map/ppermute | solution.py:253
  31.6 0.0 copy-done
  31.6 0.7 %shard_map.72 = f32[1,4,4096]{2,1,0:T(4,128)} custom-call(bf16[128,128]{1,0:T(8,128)(2,1)S(1)} %collective-permute-done.10.refs_0_, bf16[128,128]{1,0:T(8,128)(2,1)S(1)} %collective-permute-done.11.refs_1_, bf16[128,128]{1,0:T(8,128)(2,1)S(1)} %collective-permute-done.12.refs_2_, f32[128,128]{1,0:T(8,128)S(1)} %get-tuple-element.46.refs_3_, ...), custom_call_target="tpu_custom_call" | custom-call | tf_op jit(solution)/shard_map/pallas_call | solution.py:24
  (1 shorter events, 0.0 us)
Async XLA Ops:
  0.0 5.0 %collective-permute-start = (bf16[1,4,4096]{2,1,0:T(4,128)(2,1)}, bf16[1,4,4096]{2,1,0:T(4,128)(2,1)S(1)}, u32[]{:S(2)}, u32[]{:S(2)}) collective-permute-start(bf16[1,4,4096]{2,1,0:T(4,128)(2,1)} %refs_0_.1), channel_id=1, source_target_pairs={{0,4},{4,0},{1,5},{5,1},{2,6},{6,2},{3,7},{7,3},{8,12},{12,8},{9,1... | collective-permute-start | bytes 98312 | tf_op jit(solution)/shard_map/ppermute | solution.py:239
  5.1 6.9 %collective-permute-start.3 = (bf16[256,128]{1,0:T(8,128)(2,1)S(1)}, bf16[256,128]{1,0:T(8,128)(2,1)S(1)}, u32[]{:S(2)}, u32[]{:S(2)}) collective-permute-start(bf16[256,128]{1,0:T(8,128)(2,1)S(1)} %shard_map.65.refs_3_), channel_id=1, source_target_pairs={{0,24},{8,16},{16,8},{24,0},{1,25},{9,17},{17,9},{25,1},{2,26},{10... | collective-permute-start | bytes 196616 | tf_op jit(solution)/shard_map/ppermute | solution.py:239
  9.3 5.2 %collective-permute-start.2 = (bf16[256,128]{1,0:T(8,128)(2,1)S(1)}, bf16[256,128]{1,0:T(8,128)(2,1)S(1)}, u32[]{:S(2)}, u32[]{:S(2)}) collective-permute-start(bf16[256,128]{1,0:T(8,128)(2,1)S(1)} %shard_map.65.refs_3_), channel_id=1, source_target_pairs={{0,16},{8,24},{16,0},{24,8},{1,17},{9,25},{17,1},{25,9},{2,18},{10... | collective-permute-start | bytes 196616 | tf_op jit(solution)/shard_map/ppermute | solution.py:239
  9.3 5.2 %collective-permute-start.1 = (bf16[256,128]{1,0:T(8,128)(2,1)S(1)}, bf16[256,128]{1,0:T(8,128)(2,1)S(1)}, u32[]{:S(2)}, u32[]{:S(2)}) collective-permute-start(bf16[256,128]{1,0:T(8,128)(2,1)S(1)} %shard_map.65.refs_3_), channel_id=1, source_target_pairs={{0,8},{8,0},{16,24},{24,16},{1,9},{9,1},{17,25},{25,17},{2,10},{10... | collective-permute-start | bytes 196616 | tf_op jit(solution)/shard_map/ppermute | solution.py:239
  9.9 2.1 %collective-permute-start.4 = (s32[32,128]{1,0:T(8,128)S(1)}, s32[32,128]{1,0:T(8,128)S(1)}, u32[]{:S(2)}, u32[]{:S(2)}) collective-permute-start(s32[32,128]{1,0:T(8,128)S(1)} %get-tuple-element.28), channel_id=1, source_target_pairs={{0,1},{1,0},{2,3},{3,2},{4,5},{5,4},{6,7},{7,6},{8,9},{9,8},{10,11... | collective-permute-start | bytes 49160 | tf_op jit(solution)/shard_map/ppermute | solution.py:312
  15.1 1.4 %collective-permute-start.6 = (bf16[512,128]{1,0:T(8,128)(2,1)S(1)}, bf16[512,128]{1,0:T(8,128)(2,1)S(1)}, u32[]{:S(2)}, u32[]{:S(2)}) collective-permute-start(bf16[512,128]{1,0:T(8,128)(2,1)S(1)} %get-tuple-element.37.first_ref), channel_id=1, source_target_pairs={{0,1},{1,0},{2,3},{3,2},{4,5},{5,4},{6,7},{7,6},{8,9},{9,8},{10,11... | collective-permute-start | bytes 393224 | tf_op jit(solution)/shard_map/ppermute | solution.py:329
  15.2 1.5 %collective-permute-start.5 = (bf16[512,128]{1,0:T(8,128)(2,1)S(1)}, bf16[512,128]{1,0:T(8,128)(2,1)S(1)}, u32[]{:S(2)}, u32[]{:S(2)}) collective-permute-start(bf16[512,128]{1,0:T(8,128)(2,1)S(1)} %get-tuple-element.36.second_ref), channel_id=1, source_target_pairs={{0,1},{1,0},{2,3},{3,2},{4,5},{5,4},{6,7},{7,6},{8,9},{9,8},{10,11... | collective-permute-start | bytes 393224 | tf_op jit(solution)/shard_map/ppermute | solution.py:329
  16.6 14.9 %copy-start = (f32[1,4,4096]{2,1,0:T(4,128)S(1)}, f32[1,4,4096]{2,1,0:T(4,128)}, u32[]{:S(2)}) copy-start(f32[1,4,4096]{2,1,0:T(4,128)} %refs_4_.1) | copy-start | bytes 196612
  16.9 5.9 %collective-permute-start.7 = (bf16[512,128]{1,0:T(8,128)(2,1)S(1)}, bf16[512,128]{1,0:T(8,128)(2,1)S(1)}, u32[]{:S(2)}, u32[]{:S(2)}) collective-permute-start(bf16[512,128]{1,0:T(8,128)(2,1)S(1)} %get-tuple-element.40), channel_id=1, source_target_pairs={{0,6},{1,9},{2,4},{3,11},{4,2},{5,13},{6,0},{7,15},{8,14},{9,17},{... | collective-permute-start | bytes 393224 | tf_op jit(solution)/shard_map/ppermute | solution.py:253
  19.4 5.0 %collective-permute-start.8 = (bf16[512,128]{1,0:T(8,128)(2,1)S(1)}, bf16[512,128]{1,0:T(8,128)(2,1)S(1)}, u32[]{:S(2)}, u32[]{:S(2)}) collective-permute-start(bf16[512,128]{1,0:T(8,128)(2,1)S(1)} %get-tuple-element.41), channel_id=1, source_target_pairs={{0,4},{1,17},{2,6},{3,19},{4,0},{5,21},{6,2},{7,23},{8,12},{9,25},... | collective-permute-start | bytes 393224 | tf_op jit(solution)/shard_map/ppermute | solution.py:253
  19.9 5.0 %collective-permute-start.9 = (bf16[512,128]{1,0:T(8,128)(2,1)S(1)}, bf16[512,128]{1,0:T(8,128)(2,1)S(1)}, u32[]{:S(2)}, u32[]{:S(2)}) collective-permute-start(bf16[512,128]{1,0:T(8,128)(2,1)S(1)} %get-tuple-element.42), channel_id=1, source_target_pairs={{0,2},{1,25},{2,0},{3,27},{4,6},{5,29},{6,4},{7,31},{8,10},{9,1},{... | collective-permute-start | bytes 393224 | tf_op jit(solution)/shard_map/ppermute | solution.py:253
  24.9 5.8 %collective-permute-start.10 = (bf16[128,128]{1,0:T(8,128)(2,1)S(1)}, bf16[128,128]{1,0:T(8,128)(2,1)S(1)}, u32[]{:S(2)}, u32[]{:S(2)}) collective-permute-start(bf16[128,128]{1,0:T(8,128)(2,1)S(1)} %get-tuple-element.43), channel_id=1, source_target_pairs={{0,8},{1,7},{2,10},{3,5},{4,12},{5,3},{6,14},{7,1},{8,16},{9,15},{... | collective-permute-start | bytes 98312 | tf_op jit(solution)/shard_map/ppermute | solution.py:253
  25.5 5.2 %collective-permute-start.11 = (bf16[128,128]{1,0:T(8,128)(2,1)S(1)}, bf16[128,128]{1,0:T(8,128)(2,1)S(1)}, u32[]{:S(2)}, u32[]{:S(2)}) collective-permute-start(bf16[128,128]{1,0:T(8,128)(2,1)S(1)} %get-tuple-element.44), channel_id=1, source_target_pairs={{0,16},{1,5},{2,18},{3,7},{4,20},{5,1},{6,22},{7,3},{8,24},{9,13},... | collective-permute-start | bytes 98312 | tf_op jit(solution)/shard_map/ppermute | solution.py:253
  27.6 3.9 %collective-permute-start.12 = (bf16[128,128]{1,0:T(8,128)(2,1)S(1)}, bf16[128,128]{1,0:T(8,128)(2,1)S(1)}, u32[]{:S(2)}, u32[]{:S(2)}) collective-permute-start(bf16[128,128]{1,0:T(8,128)(2,1)S(1)} %get-tuple-element.45), channel_id=1, source_target_pairs={{0,24},{1,3},{2,26},{3,1},{4,28},{5,7},{6,30},{7,5},{8,0},{9,11},{... | collective-permute-start | bytes 98312 | tf_op jit(solution)/shard_map/ppermute | solution.py:253

commit v11 on v10

--- a/solution.py
+++ b/solution.py
@@ -91,7 +91,8 @@
     def slot_on(core):
         if not opposite:
             return (to_plane * outer + to_outer) * per_col + place % per_col
-        plane_first = to_plane * outer + back
+        swapped = to_inner + groups * to_group
+        plane_first = swapped * outer + back
         outer_first = back * (inner * groups) + to_plane
         return jnp.where(core == 0, plane_first, outer_first) * per_col + place % per_col
 
@@ -246,7 +247,7 @@
     line, total = inner * groups * cores, math.prod(sizes)
     arrived = []
     for i, x in enumerate(blocks, 1):
-        across = pairs[in_plane[i]]
+        across = pairs[in_plane[i if outer_core == 0 else (0, 2, 1, 3)[i]]]
         both = [
             (n, (n - i * line) % total) if n % cores == outer_core else across[n] for n in range(total)
         ]

time: 32.5 us -> 32.4 us (level)
  no operation moved by 1% of the time
where the time goes in v11:
time: 32.4 us; the launch traced here: 32.2 us
  starting transfers between devices  16.8 us (52%)
  waiting for transfers between devices  10.4 us (32%)
  Pallas kernels  3.38 us (10%)
  local copies, waits for them, and re-layouts  1.56 us (5%)
    ppermute x6, starting transfers between devices, exchange_crossed(): arrived.append(lax.ppermute(x, ('outer', 'inner', 'groups', 'core'), both))  8.48 us
    ppermute x4, starting transfers between devices, exchange(): lax.ppermute(x, axes, pairs)  7.78 us
    ppermute x6, waiting for transfers between devices, exchange_crossed(): arrived.append(lax.ppermute(x, ('outer', 'inner', 'groups', 'core'), both))  6.13 us
    ppermute x4, waiting for transfers between devices, exchange(): lax.ppermute(x, axes, pairs)  3.57 us
    pallas_call x9, Pallas kernels, call(): pl.pallas_call(kernel, out_shape=out_shape, in_specs=in_specs, out_specs=...  3.38 us
    reshape x1, local copies, waits for them, and re-layouts, per_device(): tiles.reshape(held * ROWS_OF_TILE, LANES)  1.55 us
    ppermute x2, waiting for transfers between devices, per_device(): other = [lax.ppermute(x, 'core', swap) for x in partial]  0.68 us
  transfers between devices with their start and end apart: 13, of which 9 were waited for; matrix products, arithmetic and copies ran while one was open for 5% of the time, Pallas kernels for 6%

profile of v11, /device:TPU:0, one launch (start us, length us, event | category | flops | bytes accessed | tf_op | source)
XLA Modules:
  0.0 32.2 jit_solution(11529709464004255518)
XLA Ops:
  0.0 2.9 %collective-permute-start = (bf16[1,4,4096]{2,1,0:T(4,128)(2,1)}, bf16[1,4,4096]{2,1,0:T(4,128)(2,1)S(1)}, u32[]{:S(2)}, u32[]{:S(2)}) collective-permute-start(bf16[1,4,4096]{2,1,0:T(4,128)(2,1)} %refs_0_.1), channel_id=1, source_target_pairs={{0,4},{4,0},{1,5},{5,1},{2,6},{6,2},{3,7},{7,3},{8,12},{12,8},{9,1... | collective-permute-start | bytes 98312 | tf_op jit(solution)/shard_map/ppermute | solution.py:240
  2.9 1.0 %shard_map.64 = (bf16[128,128]{1,0:T(8,128)(2,1)S(1)}, s32[128,128]{1,0:T(8,128)S(1)}, s32[32,128]{1,0:T(8,128)S(1)}, s32[32,128]{1,0:T(8,128)S(1)}) custom-call(bf16[1,4,4096]{2,1,0:T(4,128)(2,1)} %refs_0_.1, s32[1,128]{1,0:T(1,128)} %bitcast.3, s32[1,32]{1,0:T(1,128)} %bitcast.4, s32[1,32]{1,0:T(1,128)} %bitcast.5), custom_call_target="tpu_custom_call" | custom-call | tf_op jit(solution)/shard_map/pallas_call | solution.py:24
  3.9 1.1 %collective-permute-done.refs_0_ = bf16[1,4,4096]{2,1,0:T(4,128)(2,1)S(1)} collective-permute-done((bf16[1,4,4096]{2,1,0:T(4,128)(2,1)}, bf16[1,4,4096]{2,1,0:T(4,128)(2,1)S(1)}, u32[]{:S(2)}, u32[]{:S(2)}) %collective-permute-start) | collective-permute-done | bytes 32800 | tf_op jit(solution)/shard_map/ppermute | solution.py:240
  5.1 4.2 %collective-permute-start.3 = (bf16[256,128]{1,0:T(8,128)(2,1)S(1)}, bf16[256,128]{1,0:T(8,128)(2,1)S(1)}, u32[]{:S(2)}, u32[]{:S(2)}) collective-permute-start(bf16[256,128]{1,0:T(8,128)(2,1)S(1)} %shard_map.65.refs_3_), channel_id=1, source_target_pairs={{0,24},{8,16},{16,8},{24,0},{1,25},{9,17},{17,9},{25,1},{2,26},{10... | collective-permute-start | bytes 196616 | tf_op jit(solution)/shard_map/ppermute | solution.py:240
  9.3 0.0 collective-permute-start.2
  9.3 0.6 %collective-permute-start.1 = (bf16[256,128]{1,0:T(8,128)(2,1)S(1)}, bf16[256,128]{1,0:T(8,128)(2,1)S(1)}, u32[]{:S(2)}, u32[]{:S(2)}) collective-permute-start(bf16[256,128]{1,0:T(8,128)(2,1)S(1)} %shard_map.65.refs_3_), channel_id=1, source_target_pairs={{0,8},{8,0},{16,24},{24,16},{1,9},{9,1},{17,25},{25,17},{2,10},{10... | collective-permute-start | bytes 196616 | tf_op jit(solution)/shard_map/ppermute | solution.py:240
  9.9 0.0 collective-permute-start.4
  9.9 1.6 %reshape.15.tile_ref = bf16[4096,128]{1,0:T(8,128)(2,1)S(1)} reshape(bf16[128,4096]{1,0:T(8,128)(2,1)} %param.6) | data formatting | bytes 2097152 | tf_op jit(solution)/shard_map/reshape | solution.py:310
  11.5 0.5 %shard_map.66.tile_ref = bf16[2048,256]{1,0:T(8,128)(2,1)S(1)} custom-call(bf16[4096,128]{1,0:T(8,128)(2,1)S(1)} %reshape.15.tile_ref), custom_call_target="tpu_custom_call" | custom-call | tf_op jit(solution)/shard_map/pallas_call | solution.py:24
  12.0 0.0 collective-permute-done.4.slot_ref
  12.0 0.0 collective-permute-done.3.refs_0_
  12.0 2.5 %collective-permute-done.2.refs_1_ = bf16[256,128]{1,0:T(8,128)(2,1)S(1)} collective-permute-done((bf16[256,128]{1,0:T(8,128)(2,1)S(1)}, bf16[256,128]{1,0:T(8,128)(2,1)S(1)}, u32[]{:S(2)}, u32[]{:S(2)}) %collective-permute-start.2) | collective-permute-done | bytes 65568 | tf_op jit(solution)/shard_map/ppermute | solution.py:240
  14.5 0.0 collective-permute-done.1.refs_2_
  14.5 0.6 %shard_map.67 = (bf16[512,128]{1,0:T(8,128)(2,1)S(1)}, bf16[512,128]{1,0:T(8,128)(2,1)S(1)}) custom-call(s32[128,128]{1,0:T(8,128)S(1)} %get-tuple-element.31.cd_ref, bf16[2048,256]{1,0:T(8,128)(2,1)S(1)} %shard_map.66.tile_ref, bf16[256,128]{1,0:T(8,128)(2,1)S(1)} %collective-permute-done.3.refs_0_, bf16[256,128]{1,0:T(8,128)(2,1)S(1)} %collective-permute-done.2.refs_1_, ...), custom_call_target="tpu_custom_call" | custom-call | tf_op jit(solution)/shard_map/pallas_call | solution.py:24
  15.1 0.1 collective-permute-start.6
  15.2 0.5 %collective-permute-start.5 = (bf16[512,128]{1,0:T(8,128)(2,1)S(1)}, bf16[512,128]{1,0:T(8,128)(2,1)S(1)}, u32[]{:S(2)}, u32[]{:S(2)}) collective-permute-start(bf16[512,128]{1,0:T(8,128)(2,1)S(1)} %get-tuple-element.36.second_ref), channel_id=1, source_target_pairs={{0,1},{1,0},{2,3},{3,2},{4,5},{5,4},{6,7},{7,6},{8,9},{9,8},{10,11... | collective-permute-start | bytes 393224 | tf_op jit(solution)/shard_map/ppermute | solution.py:330
  15.7 0.2 shard_map.68.in_ref
  15.9 0.6 %collective-permute-done.6.ref = bf16[512,128]{1,0:T(8,128)(2,1)S(1)} collective-permute-done((bf16[512,128]{1,0:T(8,128)(2,1)S(1)}, bf16[512,128]{1,0:T(8,128)(2,1)S(1)}, u32[]{:S(2)}, u32[]{:S(2)}) %collective-permute-start.6) | collective-permute-done | bytes 131104 | tf_op jit(solution)/shard_map/ppermute | solution.py:330
  16.5 0.1 shard_map.69.in_ref
  16.6 0.0 copy-start
  16.6 0.1 collective-permute-done.5.ref
  16.7 0.1 shard_map.70
  16.9 2.5 %collective-permute-start.7 = (bf16[512,128]{1,0:T(8,128)(2,1)S(1)}, bf16[512,128]{1,0:T(8,128)(2,1)S(1)}, u32[]{:S(2)}, u32[]{:S(2)}) collective-permute-start(bf16[512,128]{1,0:T(8,128)(2,1)S(1)} %get-tuple-element.40), channel_id=1, source_target_pairs={{0,6},{1,9},{2,4},{3,11},{4,2},{5,13},{6,0},{7,15},{8,14},{9,17},{... | collective-permute-start | bytes 393224 | tf_op jit(solution)/shard_map/ppermute | solution.py:254
  19.4 0.5 %collective-permute-start.8 = (bf16[512,128]{1,0:T(8,128)(2,1)S(1)}, bf16[512,128]{1,0:T(8,128)(2,1)S(1)}, u32[]{:S(2)}, u32[]{:S(2)}) collective-permute-start(bf16[512,128]{1,0:T(8,128)(2,1)S(1)} %get-tuple-element.41), channel_id=1, source_target_pairs={{0,2},{1,17},{2,0},{3,19},{4,6},{5,21},{6,4},{7,23},{8,10},{9,25},... | collective-permute-start | bytes 393224 | tf_op jit(solution)/shard_map/ppermute | solution.py:254
  19.9 0.5 %collective-permute-start.9 = (bf16[512,128]{1,0:T(8,128)(2,1)S(1)}, bf16[512,128]{1,0:T(8,128)(2,1)S(1)}, u32[]{:S(2)}, u32[]{:S(2)}) collective-permute-start(bf16[512,128]{1,0:T(8,128)(2,1)S(1)} %get-tuple-element.42), channel_id=1, source_target_pairs={{0,4},{1,25},{2,6},{3,27},{4,0},{5,29},{6,2},{7,31},{8,12},{9,1},{... | collective-permute-start | bytes 393224 | tf_op jit(solution)/shard_map/ppermute | solution.py:254
  20.4 2.4 %collective-permute-done.7.refs_0_ = bf16[512,128]{1,0:T(8,128)(2,1)S(1)} collective-permute-done((bf16[512,128]{1,0:T(8,128)(2,1)S(1)}, bf16[512,128]{1,0:T(8,128)(2,1)S(1)}, u32[]{:S(2)}, u32[]{:S(2)}) %collective-permute-start.7) | collective-permute-done | bytes 131104 | tf_op jit(solution)/shard_map/ppermute | solution.py:254
  22.8 1.6 %collective-permute-done.8.refs_1_ = bf16[512,128]{1,0:T(8,128)(2,1)S(1)} collective-permute-done((bf16[512,128]{1,0:T(8,128)(2,1)S(1)}, bf16[512,128]{1,0:T(8,128)(2,1)S(1)}, u32[]{:S(2)}, u32[]{:S(2)}) %collective-permute-start.8) | collective-permute-done | bytes 131104 | tf_op jit(solution)/shard_map/ppermute | solution.py:254
  24.3 0.5 %collective-permute-done.9.refs_2_ = bf16[512,128]{1,0:T(8,128)(2,1)S(1)} collective-permute-done((bf16[512,128]{1,0:T(8,128)(2,1)S(1)}, bf16[512,128]{1,0:T(8,128)(2,1)S(1)}, u32[]{:S(2)}, u32[]{:S(2)}) %collective-permute-start.9) | collective-permute-done | bytes 131104 | tf_op jit(solution)/shard_map/ppermute | solution.py:254
  24.9 0.1 shard_map.71
  24.9 0.6 %collective-permute-start.10 = (bf16[128,128]{1,0:T(8,128)(2,1)S(1)}, bf16[128,128]{1,0:T(8,128)(2,1)S(1)}, u32[]{:S(2)}, u32[]{:S(2)}) collective-permute-start(bf16[128,128]{1,0:T(8,128)(2,1)S(1)} %get-tuple-element.43), channel_id=1, source_target_pairs={{0,8},{1,7},{2,10},{3,5},{4,12},{5,3},{6,14},{7,1},{8,16},{9,15},{... | collective-permute-start | bytes 98312 | tf_op jit(solution)/shard_map/ppermute | solution.py:254
  25.5 2.1 %collective-permute-start.11 = (bf16[128,128]{1,0:T(8,128)(2,1)S(1)}, bf16[128,128]{1,0:T(8,128)(2,1)S(1)}, u32[]{:S(2)}, u32[]{:S(2)}) collective-permute-start(bf16[128,128]{1,0:T(8,128)(2,1)S(1)} %get-tuple-element.44), channel_id=1, source_target_pairs={{0,16},{1,5},{2,18},{3,7},{4,20},{5,1},{6,22},{7,3},{8,24},{9,13},... | collective-permute-start | bytes 98312 | tf_op jit(solution)/shard_map/ppermute | solution.py:254
  27.6 2.2 %collective-permute-start.12 = (bf16[128,128]{1,0:T(8,128)(2,1)S(1)}, bf16[128,128]{1,0:T(8,128)(2,1)S(1)}, u32[]{:S(2)}, u32[]{:S(2)}) collective-permute-start(bf16[128,128]{1,0:T(8,128)(2,1)S(1)} %get-tuple-element.45), channel_id=1, source_target_pairs={{0,24},{1,3},{2,26},{3,1},{4,28},{5,7},{6,30},{7,5},{8,0},{9,11},{... | collective-permute-start | bytes 98312 | tf_op jit(solution)/shard_map/ppermute | solution.py:254
  29.9 0.8 %collective-permute-done.10.refs_0_ = bf16[128,128]{1,0:T(8,128)(2,1)S(1)} collective-permute-done((bf16[128,128]{1,0:T(8,128)(2,1)S(1)}, bf16[128,128]{1,0:T(8,128)(2,1)S(1)}, u32[]{:S(2)}, u32[]{:S(2)}) %collective-permute-start.10) | collective-permute-done | bytes 32800 | tf_op jit(solution)/shard_map/ppermute | solution.py:254
  30.7 0.0 collective-permute-done.11.refs_1_
  30.7 0.8 %collective-permute-done.12.refs_2_ = bf16[128,128]{1,0:T(8,128)(2,1)S(1)} collective-permute-done((bf16[128,128]{1,0:T(8,128)(2,1)S(1)}, bf16[128,128]{1,0:T(8,128)(2,1)S(1)}, u32[]{:S(2)}, u32[]{:S(2)}) %collective-permute-start.12) | collective-permute-done | bytes 32800 | tf_op jit(solution)/shard_map/ppermute | solution.py:254
  31.5 0.0 copy-done
  31.5 0.7 %shard_map.72 = f32[1,4,4096]{2,1,0:T(4,128)} custom-call(bf16[128,128]{1,0:T(8,128)(2,1)S(1)} %collective-permute-done.10.refs_0_, bf16[128,128]{1,0:T(8,128)(2,1)S(1)} %collective-permute-done.11.refs_1_, bf16[128,128]{1,0:T(8,128)(2,1)S(1)} %collective-permute-done.12.refs_2_, f32[128,128]{1,0:T(8,128)S(1)} %get-tuple-element.46.refs_3_, ...), custom_call_target="tpu_custom_call" | custom-call | tf_op jit(solution)/shard_map/pallas_call | solution.py:24
  (1 shorter events, 0.0 us)
Async XLA Ops:
  0.0 5.0 %collective-permute-start = (bf16[1,4,4096]{2,1,0:T(4,128)(2,1)}, bf16[1,4,4096]{2,1,0:T(4,128)(2,1)S(1)}, u32[]{:S(2)}, u32[]{:S(2)}) collective-permute-start(bf16[1,4,4096]{2,1,0:T(4,128)(2,1)} %refs_0_.1), channel_id=1, source_target_pairs={{0,4},{4,0},{1,5},{5,1},{2,6},{6,2},{3,7},{7,3},{8,12},{12,8},{9,1... | collective-permute-start | bytes 98312 | tf_op jit(solution)/shard_map/ppermute | solution.py:240
  5.1 6.9 %collective-permute-start.3 = (bf16[256,128]{1,0:T(8,128)(2,1)S(1)}, bf16[256,128]{1,0:T(8,128)(2,1)S(1)}, u32[]{:S(2)}, u32[]{:S(2)}) collective-permute-start(bf16[256,128]{1,0:T(8,128)(2,1)S(1)} %shard_map.65.refs_3_), channel_id=1, source_target_pairs={{0,24},{8,16},{16,8},{24,0},{1,25},{9,17},{17,9},{25,1},{2,26},{10... | collective-permute-start | bytes 196616 | tf_op jit(solution)/shard_map/ppermute | solution.py:240
  9.3 5.2 %collective-permute-start.2 = (bf16[256,128]{1,0:T(8,128)(2,1)S(1)}, bf16[256,128]{1,0:T(8,128)(2,1)S(1)}, u32[]{:S(2)}, u32[]{:S(2)}) collective-permute-start(bf16[256,128]{1,0:T(8,128)(2,1)S(1)} %shard_map.65.refs_3_), channel_id=1, source_target_pairs={{0,16},{8,24},{16,0},{24,8},{1,17},{9,25},{17,1},{25,9},{2,18},{10... | collective-permute-start | bytes 196616 | tf_op jit(solution)/shard_map/ppermute | solution.py:240
  9.3 5.2 %collective-permute-start.1 = (bf16[256,128]{1,0:T(8,128)(2,1)S(1)}, bf16[256,128]{1,0:T(8,128)(2,1)S(1)}, u32[]{:S(2)}, u32[]{:S(2)}) collective-permute-start(bf16[256,128]{1,0:T(8,128)(2,1)S(1)} %shard_map.65.refs_3_), channel_id=1, source_target_pairs={{0,8},{8,0},{16,24},{24,16},{1,9},{9,1},{17,25},{25,17},{2,10},{10... | collective-permute-start | bytes 196616 | tf_op jit(solution)/shard_map/ppermute | solution.py:240
  9.9 2.1 %collective-permute-start.4 = (s32[32,128]{1,0:T(8,128)S(1)}, s32[32,128]{1,0:T(8,128)S(1)}, u32[]{:S(2)}, u32[]{:S(2)}) collective-permute-start(s32[32,128]{1,0:T(8,128)S(1)} %get-tuple-element.28), channel_id=1, source_target_pairs={{0,1},{1,0},{2,3},{3,2},{4,5},{5,4},{6,7},{7,6},{8,9},{9,8},{10,11... | collective-permute-start | bytes 49160 | tf_op jit(solution)/shard_map/ppermute | solution.py:313
  15.1 1.4 %collective-permute-start.6 = (bf16[512,128]{1,0:T(8,128)(2,1)S(1)}, bf16[512,128]{1,0:T(8,128)(2,1)S(1)}, u32[]{:S(2)}, u32[]{:S(2)}) collective-permute-start(bf16[512,128]{1,0:T(8,128)(2,1)S(1)} %get-tuple-element.37.first_ref), channel_id=1, source_target_pairs={{0,1},{1,0},{2,3},{3,2},{4,5},{5,4},{6,7},{7,6},{8,9},{9,8},{10,11... | collective-permute-start | bytes 393224 | tf_op jit(solution)/shard_map/ppermute | solution.py:330
  15.2 1.5 %collective-permute-start.5 = (bf16[512,128]{1,0:T(8,128)(2,1)S(1)}, bf16[512,128]{1,0:T(8,128)(2,1)S(1)}, u32[]{:S(2)}, u32[]{:S(2)}) collective-permute-start(bf16[512,128]{1,0:T(8,128)(2,1)S(1)} %get-tuple-element.36.second_ref), channel_id=1, source_target_pairs={{0,1},{1,0},{2,3},{3,2},{4,5},{5,4},{6,7},{7,6},{8,9},{9,8},{10,11... | collective-permute-start | bytes 393224 | tf_op jit(solution)/shard_map/ppermute | solution.py:330
  16.6 14.9 %copy-start = (f32[1,4,4096]{2,1,0:T(4,128)S(1)}, f32[1,4,4096]{2,1,0:T(4,128)}, u32[]{:S(2)}) copy-start(f32[1,4,4096]{2,1,0:T(4,128)} %refs_4_.1) | copy-start | bytes 196612
  16.9 5.9 %collective-permute-start.7 = (bf16[512,128]{1,0:T(8,128)(2,1)S(1)}, bf16[512,128]{1,0:T(8,128)(2,1)S(1)}, u32[]{:S(2)}, u32[]{:S(2)}) collective-permute-start(bf16[512,128]{1,0:T(8,128)(2,1)S(1)} %get-tuple-element.40), channel_id=1, source_target_pairs={{0,6},{1,9},{2,4},{3,11},{4,2},{5,13},{6,0},{7,15},{8,14},{9,17},{... | collective-permute-start | bytes 393224 | tf_op jit(solution)/shard_map/ppermute | solution.py:254
  19.4 5.0 %collective-permute-start.8 = (bf16[512,128]{1,0:T(8,128)(2,1)S(1)}, bf16[512,128]{1,0:T(8,128)(2,1)S(1)}, u32[]{:S(2)}, u32[]{:S(2)}) collective-permute-start(bf16[512,128]{1,0:T(8,128)(2,1)S(1)} %get-tuple-element.41), channel_id=1, source_target_pairs={{0,2},{1,17},{2,0},{3,19},{4,6},{5,21},{6,4},{7,23},{8,10},{9,25},... | collective-permute-start | bytes 393224 | tf_op jit(solution)/shard_map/ppermute | solution.py:254
  19.9 5.0 %collective-permute-start.9 = (bf16[512,128]{1,0:T(8,128)(2,1)S(1)}, bf16[512,128]{1,0:T(8,128)(2,1)S(1)}, u32[]{:S(2)}, u32[]{:S(2)}) collective-permute-start(bf16[512,128]{1,0:T(8,128)(2,1)S(1)} %get-tuple-element.42), channel_id=1, source_target_pairs={{0,4},{1,25},{2,6},{3,27},{4,0},{5,29},{6,2},{7,31},{8,12},{9,1},{... | collective-permute-start | bytes 393224 | tf_op jit(solution)/shard_map/ppermute | solution.py:254
  24.9 5.8 %collective-permute-start.10 = (bf16[128,128]{1,0:T(8,128)(2,1)S(1)}, bf16[128,128]{1,0:T(8,128)(2,1)S(1)}, u32[]{:S(2)}, u32[]{:S(2)}) collective-permute-start(bf16[128,128]{1,0:T(8,128)(2,1)S(1)} %get-tuple-element.43), channel_id=1, source_target_pairs={{0,8},{1,7},{2,10},{3,5},{4,12},{5,3},{6,14},{7,1},{8,16},{9,15},{... | collective-permute-start | bytes 98312 | tf_op jit(solution)/shard_map/ppermute | solution.py:254
  25.5 5.2 %collective-permute-start.11 = (bf16[128,128]{1,0:T(8,128)(2,1)S(1)}, bf16[128,128]{1,0:T(8,128)(2,1)S(1)}, u32[]{:S(2)}, u32[]{:S(2)}) collective-permute-start(bf16[128,128]{1,0:T(8,128)(2,1)S(1)} %get-tuple-element.44), channel_id=1, source_target_pairs={{0,16},{1,5},{2,18},{3,7},{4,20},{5,1},{6,22},{7,3},{8,24},{9,13},... | collective-permute-start | bytes 98312 | tf_op jit(solution)/shard_map/ppermute | solution.py:254
  27.6 3.9 %collective-permute-start.12 = (bf16[128,128]{1,0:T(8,128)(2,1)S(1)}, bf16[128,128]{1,0:T(8,128)(2,1)S(1)}, u32[]{:S(2)}, u32[]{:S(2)}) collective-permute-start(bf16[128,128]{1,0:T(8,128)(2,1)S(1)} %get-tuple-element.45), channel_id=1, source_target_pairs={{0,24},{1,3},{2,26},{3,1},{4,28},{5,7},{6,30},{7,5},{8,0},{9,11},{... | collective-permute-start | bytes 98312 | tf_op jit(solution)/shard_map/ppermute | solution.py:254
